TPU v7x, 512 devices: a whole 4x8x8 slice. The times are simulated.
512 devices in a mesh: tm: 32 (over x, y_hi, core), sku: 16 (over y_lo, z).
Axes of the slice: x: 4, y: 8 (y_hi: 4, y_lo: 2; y = y_hi * 2 + y_lo), z: 8, core: 2. Of those that a mesh axis runs over, the one named last changes fastest.
Arguments:
- primal_x: float32 [256, 131072], P('tm', 'sku'), may hold values from 0 to 2
- stock_v: float32 [256, 131072], P('tm', 'sku'), may hold values from 0 to 2
- balance_dual: float32 [256, 131072], P('tm', 'sku'), may hold values from -6 to 6
- plant_dual: float32 [256, 128], P('tm', 'sku'), may hold values from 0 to 1
- demand: float32 [256, 131072], P('tm', 'sku'), may hold values from 0.2 to 1.5
- unit_cost: float32 [131072], P('sku'), may hold values from 0.1 to 2
- holding_cost: float32 [131072], P('sku'), may hold values from 0.05 to 1
- load_coef: float32 [131072], P('sku'), may hold values from 0.25 to 2
- capacity: float32 [256, 128], P('tm'), may hold values from 307.2 to 1228.8
- lags: int32 [1024], P('sku'), may hold values from 1 to 8
- plants: int32 [131072], P('sku'), may hold values from 0 to 127
- step_codes: int32 [2], replicated, may hold values from 0 to 4
Outputs:
- next_x: float32 [256, 131072], P('tm', 'sku')
- next_v: float32 [256, 131072], P('tm', 'sku')
- next_balance: float32 [256, 131072], P('tm', 'sku')
- next_plant: float32 [256, 128], P('tm', 'sku')
- residuals: float32 [2, 2], replicated
Inputs may be any that keep to these rules, and one draw needn't show every extreme that they name: `lags`: lead time of each block of 128 SKU-sites; 8 occurs.
All inputs are finite; a program needn't handle non-finite values.
Results may differ from a plain program's by a relative error of at most 0.0001.
Values sent between devices are 32-bit elements; how exact they have to be, the bound alone decides.
No kernel may reach another device: no remote copies, remote signals or barrier semaphores. Data moves between devices by JAX's collectives and lax.ppermute only.
A program may use at most 64 MiB of HBM per device.

v0:
```python
import jax
import jax.numpy as jnp
from jax import lax
from jax.sharding import PartitionSpec as P

P_SIZE = 128
LAGMAX = 8
BLOCK = 128
ITERS = 2


def shifted(value, axis, steps):
    count = lax.axis_size(axis)
    pairs = [(source, (source + steps) % count) for source in range(count)]
    return lax.ppermute(value, axis, pairs)


def lagged_past(extended, anchor, length, lag_cells):
    result = jnp.zeros((length, extended.shape[1]), jnp.float32)
    for offset in range(1, LAGMAX + 1):
        result = jnp.where(
            lag_cells == offset, extended[anchor - offset : anchor - offset + length], result
        )
    return result


def lagged_ahead(extended, length, lag_cells):
    result = jnp.zeros((length, extended.shape[1]), jnp.float32)
    for offset in range(1, LAGMAX + 1):
        result = jnp.where(lag_cells == offset, extended[offset : offset + length], result)
    return result


def plant_tables(plants, width):
    window = min(2048, plants.shape[0])
    columns = jnp.arange(width, dtype=jnp.int32)[None, :]
    return [
        (plants[start : start + window, None] == columns).astype(jnp.float32)
        for start in range(0, plants.shape[0], window)
    ]


def plant_load(values, tables):
    window = tables[0].shape[0]
    total = jnp.zeros((values.shape[0], tables[0].shape[1]), jnp.float32)
    for index, matrix in enumerate(tables):
        total = total + jnp.dot(
            values[:, index * window : (index + 1) * window],
            matrix,
            precision=lax.Precision.HIGHEST,
            preferred_element_type=jnp.float32,
        )
    return total


def plant_price(prices, tables):
    pieces = [
        jnp.dot(
            prices, matrix.T, precision=lax.Precision.HIGHEST, preferred_element_type=jnp.float32
        )
        for matrix in tables
    ]
    return jnp.concatenate(pieces, axis=1)


def body(
    primal_x,
    stock_v,
    balance_dual,
    plant_dual,
    demand,
    unit_cost,
    holding_cost,
    load_coef,
    capacity,
    lags,
    plants,
    step_codes,
):
    periods_dev = primal_x.shape[0]
    plants_dev = plant_dual.shape[1]
    total_skus = primal_x.shape[1] * lax.axis_size("sku")
    total_periods = periods_dev * lax.axis_size("tm")
    primal_step = 0.05 * (step_codes[0].astype(jnp.float32) + 2.0)
    dual_step = 0.05 * (step_codes[1].astype(jnp.float32) + 2.0)
    plant_step = dual_step * (P_SIZE / total_skus)
    lag_cells = jnp.repeat(lags, BLOCK)[None, :]
    tables = plant_tables(plants, P_SIZE)
    owner = lax.axis_index("sku") * plants_dev
    prices = lax.all_gather(plant_dual, "sku", axis=1, tiled=True)
    portion = plant_dual
    current_x = primal_x
    current_v = stock_v
    duals = balance_dual
    results = []
    for iteration in range(ITERS):
        upcoming = shifted(duals, "tm", -1)
        extended = jnp.concatenate([duals, upcoming], axis=0)
        ahead = lagged_ahead(extended, periods_dev, lag_cells)
        following = extended[1 : periods_dev + 1]
        present = extended[:periods_dev]
        charged = plant_price(prices, tables) * load_coef[None, :]
        new_x = jnp.maximum(current_x - primal_step * (unit_cost[None, :] + ahead + charged), 0.0)
        new_v = jnp.maximum(
            current_v - primal_step * (holding_cost[None, :] - present + following), 0.0
        )
        bar_x = 2.0 * new_x - current_x
        bar_v = 2.0 * new_v - current_v
        earlier_x, earlier_v = shifted((bar_x, bar_v[periods_dev - 1 :]), "tm", 1)
        past_x = jnp.concatenate([earlier_x, bar_x], axis=0)
        before_v = jnp.concatenate([earlier_v, bar_v[:-1]], axis=0)
        misfit = -demand - (bar_v - before_v - lagged_past(past_x, LAGMAX, periods_dev, lag_cells))
        duals = duals + dual_step * misfit
        loads = plant_load(bar_x * load_coef[None, :], tables)
        totals = lax.psum(loads, "sku")
        excess_all = totals - capacity
        prices = jnp.maximum(prices + plant_step * excess_all, 0.0)
        excess = lax.dynamic_slice_in_dim(excess_all, owner, plants_dev, 1)
        portion = lax.dynamic_slice_in_dim(prices, owner, plants_dev, 1)
        violation = jnp.maximum(excess, 0.0) * (P_SIZE / total_skus)
        local_sums = jnp.stack([jnp.sum(misfit * misfit), jnp.sum(violation * violation)])
        results.append(lax.psum(local_sums, ("tm", "sku")))
        current_x = new_x
        current_v = new_v
    summed = jnp.stack(results)
    divisor = jnp.array([total_periods * total_skus, total_periods * P_SIZE], jnp.float32)
    residuals = summed / divisor[None, :]
    return (current_x, current_v, duals, portion, residuals)


def solution(mesh):
    return jax.shard_map(
        body,
        mesh=mesh,
        in_specs=(
            P("tm", "sku"),
            P("tm", "sku"),
            P("tm", "sku"),
            P("tm", "sku"),
            P("tm", "sku"),
            P("sku"),
            P("sku"),
            P("sku"),
            P("tm", None),
            P("sku"),
            P("sku"),
            P(),
        ),
        out_specs=(P("tm", "sku"), P("tm", "sku"), P("tm", "sku"), P("tm", "sku"), P()),
        check_vma=False,
    )
```

profile of v0, /device:TPU:1, one launch (start us, length us, event | category | flops | bytes accessed | tf_op | source)
XLA Modules:
  0.0 268.6 jit_solution(370310579557020281)
XLA Ops:
  0.6 8.8 %collective-permute-start = (f32[8,8192]{1,0:T(8,128)}, f32[8,8192]{1,0:T(8,128)S(1)}, u32[]{:S(2)}, u32[]{:S(2)}) collective-permute-start(f32[8,8192]{1,0:T(8,128)} %param.15), channel_id=1, source_target_pairs={{0,496},{16,0},{32,16},{48,32},{64,48},{80,64},{96,80},{112,96},{1... | collective-permute-start | bytes 786440 | tf_op jit(solution)/shard_map/ppermute | solution.py:15
  9.4 1.0 constant_dynamic-update-slice_fusion.1
  10.5 0.6 copy-done.11
  11.1 27.6 %all_gather.3 = f32[8,128]{0,1:T(8,128)S(1)} all-gather(f32[8,8]{0,1:T(8,128)S(1)} %copy.18), channel_id=1, replica_groups=mesh['tm'=32,'sku'=16] {'sku'}, dimensions={1}, use_global_device_ids=true | all-gather | bytes 4352 | tf_op jit(solution)/shard_map/all_gather | solution.py:90
  38.7 1.0 convolution_bitcast_fusion
  39.7 1.0 convolution_bitcast_fusion.1
  40.7 1.0 convolution_bitcast_fusion.2
  41.7 0.1 broadcast_bitcast_fusion.6
  42.1 0.6 copy-done.10
  42.6 0.6 fusion.96
  44.6 1.0 convolution_bitcast_fusion.3
  45.7 0.9 copy-done.3
  46.6 0.4 broadcast_multiply_fusion.1
  47.0 0.6 fusion.5
  47.6 0.6 convolution_add_fusion.5
  48.2 0.6 convolution_add_fusion.4
  48.8 0.6 convolution_add_fusion.3
  49.4 23.7 %psum.28 = f32[8,128]{1,0:T(8,128)S(1)} all-reduce(f32[8,128]{1,0:T(8,128)S(1)} %convolution_add_fusion.3), channel_id=1, replica_groups=mesh['tm'=32,'sku'=16] {'sku'}, use_global_device_ids=true, to_apply=%region_0.1 | all-reduce | flops 1024 | bytes 8192 | tf_op jit(solution)/shard_map/psum | solution.py:115
  73.1 0.9 fusion
  74.0 18.1 %collective-permute-start.2 = (f32[8,8192]{1,0:T(8,128)S(1)}, f32[8,8192]{1,0:T(8,128)S(1)}, u32[]{:S(2)}, u32[]{:S(2)}) collective-permute-start(f32[8,8192]{1,0:T(8,128)S(1)} %get-tuple-element.21), channel_id=1, source_target_pairs={{0,16},{16,32},{32,48},{48,64},{64,80},{80,96},{96,112},{112,128},... | collective-permute-start | bytes 786440 | tf_op jit(solution)/shard_map/ppermute | solution.py:15
  92.2 0.9 fusion.1
  93.2 1.9 collective-permute-start.1
  95.1 0.9 fusion.2
  96.0 0.7 multiply_reduce_fusion.3
  96.7 1.8 collective-permute-done.1
  98.6 1.2 multiply_reduce_fusion.1
  99.8 11.1 %collective-permute-start.3 = (f32[8,8192]{1,0:T(8,128)S(1)}, f32[8,8192]{1,0:T(8,128)S(1)}, u32[]{:S(2)}, u32[]{:S(2)}) collective-permute-start(f32[8,8192]{1,0:T(8,128)S(1)} %multiply_add_fusion.1), channel_id=1, source_target_pairs={{0,496},{16,0},{32,16},{48,32},{64,48},{80,64},{96,80},{112,96},{1... | collective-permute-start | bytes 786440 | tf_op jit(solution)/shard_map/ppermute | solution.py:15
  110.9 0.9 fusion.4
  111.8 1.4 maximum_bitcast_fusion
  113.2 1.3 broadcast_multiply_fusion
  114.5 0.6 fusion.3
  115.1 0.6 convolution_add_fusion.2
  115.7 0.6 convolution_add_fusion.1
  116.3 0.6 convolution_add_fusion
  116.9 26.0 %psum.29 = f32[8,128]{1,0:T(8,128)S(1)} all-reduce(f32[8,128]{1,0:T(8,128)S(1)} %convolution_add_fusion), channel_id=1, replica_groups=mesh['tm'=32,'sku'=16] {'sku'}, use_global_device_ids=true, to_apply=%region_1.2 | all-reduce | flops 1024 | bytes 8192 | tf_op jit(solution)/shard_map/psum | solution.py:115
  142.9 0.8 multiply_subtract_fusion.1
  143.7 6.4 %collective-permute-start.4 = (f32[1,8192]{1,0:T(1,128)S(1)}, f32[1,8192]{1,0:T(1,128)S(1)}, u32[]{:S(2)}, u32[]{:S(2)}) collective-permute-start(f32[1,8192]{1,0:T(1,128)S(1)} %slice.223), channel_id=1, source_target_pairs={{0,16},{16,32},{32,48},{48,64},{64,80},{80,96},{96,112},{112,128},... | collective-permute-start | bytes 98312 | tf_op jit(solution)/shard_map/ppermute | solution.py:15
  150.1 1.9 collective-permute-start.5
  152.1 0.7 constant_dynamic-slice_fusion
  152.7 0.7 multiply_reduce_fusion.2
  153.4 3.9 %collective-permute-done.4 = f32[1,8192]{1,0:T(1,128)S(1)} collective-permute-done((f32[1,8192]{1,0:T(1,128)S(1)}, f32[1,8192]{1,0:T(1,128)S(1)}, u32[]{:S(2)}, u32[]{:S(2)}) %collective-permute-start.4) | collective-permute-done | bytes 32800 | tf_op jit(solution)/shard_map/ppermute | solution.py:15
  157.4 2.3 collective-permute-done.5
  159.6 1.2 multiply_reduce_fusion
  160.8 1.4 maximum_bitcast_fusion.1
  162.2 0.7 multiply_add_fusion
  162.9 104.4 %all-reduce = (f32[1,2]{1,0:T(1,128)S(1)}, f32[1,2]{1,0:T(1,128)S(1)}) all-reduce(f32[1,2]{1,0:T(1,128)S(1)} %maximum_bitcast_fusion.1, f32[1,2]{1,0:T(1,128)S(1)} %maximum_bitcast_fusion), channel_id=1, replica_groups=mesh['tm'=32,'sku'=16] {'tm','sku'}, use_global_device_ids=true, to_apply=%region_7.8 | all-reduce | flops 4 | bytes 32 | tf_op jit(solution)/shard_map/psum | solution.py:122
  267.4 0.7 copy-done.12
  268.0 0.6 maximum_multiply_fusion.2
  (39 shorter events, 0.7 us)
Async XLA Ops:
  0.6 9.8 %copy-start.9 = (f32[8,8]{1,0:T(8,128)S(1)}, f32[8,8]{1,0:T(8,128)}, u32[]{:S(2)}) copy-start(f32[8,8]{1,0:T(8,128)} %param.16) | copy-start | bytes 772
  0.6 45.0 %collective-permute-start = (f32[8,8192]{1,0:T(8,128)}, f32[8,8192]{1,0:T(8,128)S(1)}, u32[]{:S(2)}, u32[]{:S(2)}) collective-permute-start(f32[8,8192]{1,0:T(8,128)} %param.15), channel_id=1, source_target_pairs={{0,496},{16,0},{32,16},{48,32},{64,48},{80,64},{96,80},{112,96},{1... | collective-permute-start | bytes 786440 | tf_op jit(solution)/shard_map/ppermute | solution.py:15
  9.4 1.7 copy-start.7
  10.4 0.7 copy-start.11
  42.0 0.7 copy-start.10
  45.6 1.0 copy-start.3
  45.6 0.9 copy-start.5
  45.6 0.9 copy-start.6
  48.2 24.9 %copy-start.8 = (f32[8,128]{1,0:T(8,128)S(1)}, f32[8,128]{1,0:T(8,128)}, u32[]{:S(2)}) copy-start(f32[8,128]{1,0:T(8,128)} %param.21) | copy-start | bytes 12292
  48.8 43.3 %copy-start = (f32[8,8192]{1,0:T(8,128)S(1)}, f32[8,8192]{1,0:T(8,128)}, u32[]{:S(2)}) copy-start(f32[8,8192]{1,0:T(8,128)} %param.15) | copy-start | bytes 786436
  48.8 43.3 %copy-start.2 = (f32[8,8192]{1,0:T(8,128)S(1)}, f32[8,8192]{1,0:T(8,128)}, u32[]{:S(2)}) copy-start(f32[8,8192]{1,0:T(8,128)} %param.14) | copy-start | bytes 786436
  73.1 19.0 %copy-start.4 = (f32[8192]{0:T(1024)S(1)}, f32[8192]{0:T(1024)}, u32[]{:S(2)}) copy-start(f32[8192]{0:T(1024)} %param.19) | copy-start | bytes 98308
  74.0 24.6 %collective-permute-start.2 = (f32[8,8192]{1,0:T(8,128)S(1)}, f32[8,8192]{1,0:T(8,128)S(1)}, u32[]{:S(2)}, u32[]{:S(2)}) collective-permute-start(f32[8,8192]{1,0:T(8,128)S(1)} %get-tuple-element.21), channel_id=1, source_target_pairs={{0,16},{16,32},{32,48},{48,64},{64,80},{80,96},{96,112},{112,128},... | collective-permute-start | bytes 786440 | tf_op jit(solution)/shard_map/ppermute | solution.py:15
  92.2 6.4 %copy-start.1 = (f32[8,8192]{1,0:T(8,128)S(1)}, f32[8,8192]{1,0:T(8,128)}, u32[]{:S(2)}) copy-start(f32[8,8192]{1,0:T(8,128)} %param.17) | copy-start | bytes 786436
  93.2 5.4 %collective-permute-start.1 = (f32[1,8192]{1,0:T(1,128)S(1)}, f32[1,8192]{1,0:T(1,128)S(1)}, u32[]{:S(2)}, u32[]{:S(2)}) collective-permute-start(f32[1,8192]{1,0:T(1,128)S(1)} %slice.193), channel_id=1, source_target_pairs={{0,16},{16,32},{32,48},{48,64},{64,80},{80,96},{96,112},{112,128},... | collective-permute-start | bytes 98312 | tf_op jit(solution)/shard_map/ppermute | solution.py:15
  99.8 13.4 %collective-permute-start.3 = (f32[8,8192]{1,0:T(8,128)S(1)}, f32[8,8192]{1,0:T(8,128)S(1)}, u32[]{:S(2)}, u32[]{:S(2)}) collective-permute-start(f32[8,8192]{1,0:T(8,128)S(1)} %multiply_add_fusion.1), channel_id=1, source_target_pairs={{0,496},{16,0},{32,16},{48,32},{64,48},{80,64},{96,80},{112,96},{1... | collective-permute-start | bytes 786440 | tf_op jit(solution)/shard_map/ppermute | solution.py:15
  143.7 13.6 %collective-permute-start.4 = (f32[1,8192]{1,0:T(1,128)S(1)}, f32[1,8192]{1,0:T(1,128)S(1)}, u32[]{:S(2)}, u32[]{:S(2)}) collective-permute-start(f32[1,8192]{1,0:T(1,128)S(1)} %slice.223), channel_id=1, source_target_pairs={{0,16},{16,32},{32,48},{48,64},{64,80},{80,96},{96,112},{112,128},... | collective-permute-start | bytes 98312 | tf_op jit(solution)/shard_map/ppermute | solution.py:15
  150.1 9.5 %collective-permute-start.5 = (f32[8,8192]{1,0:T(8,128)S(1)}, f32[8,8192]{1,0:T(8,128)S(1)}, u32[]{:S(2)}, u32[]{:S(2)}) collective-permute-start(f32[8,8192]{1,0:T(8,128)S(1)} %get-tuple-element.14), channel_id=1, source_target_pairs={{0,16},{16,32},{32,48},{48,64},{64,80},{80,96},{96,112},{112,128},... | collective-permute-start | bytes 786440 | tf_op jit(solution)/shard_map/ppermute | solution.py:15
  267.4 0.7 copy-start.12
where the time goes:
time: 269 us
  blocking collectives  182 us (68%)
  starting transfers between devices  48.2 us (18%)
  matrix products  12.3 us (5%)
  other arithmetic  10.6 us (4%)
  waiting for transfers between devices  8.02 us (3%)
  local copies, waits for them, and re-layouts  5.52 us (2%)
    psum x1, blocking collectives, body(): results.append(lax.psum(local_sums, ('tm', 'sku')))  104 us
    psum x2, blocking collectives, body(): totals = lax.psum(loads, 'sku')  49.7 us
    ppermute x6, starting transfers between devices, shifted(): return lax.ppermute(value, axis, pairs)  48.2 us
    all_gather x1, blocking collectives, body(): prices = lax.all_gather(plant_dual, 'sku', axis=1, tiled=True)  27.6 us
    ppermute x6, waiting for transfers between devices, shifted(): return lax.ppermute(value, axis, pairs)  8.02 us
    dot_general x8, matrix products, plant_price(): jnp.dot(prices, matrix.T, precision=lax.Precision.HIGHEST, preferred_elem...  7.64 us
  transfers between devices with their start and end apart: 6, of which 3 were waited for; matrix products, arithmetic and copies ran while one was open for 5% of the time, Pallas kernels for 0%

commit v1 on v0

v1 whole, which is shorter than its diff:
```python
import jax
import jax.numpy as jnp
from jax import lax
from jax.experimental import pallas as pl
from jax.experimental.pallas import tpu as pltpu
from jax.sharding import PartitionSpec as P

P_SIZE = 128
LAGMAX = 8
BLOCK = 128
ROWS = 8
F32 = jnp.float32
VMEM = pl.BlockSpec(memory_space=pltpu.VMEM)
SMEM = pl.BlockSpec(memory_space=pltpu.SMEM)


def shifted(value, axis, steps):
    count = lax.axis_size(axis)
    return lax.ppermute(value, axis, [(i, (i + steps) % count) for i in range(count)])


def spread(value, axis):
    return lax.all_to_all(value, axis, 0, 0, tiled=True)


def shape(*dims):
    return jax.ShapeDtypeStruct(dims, F32)


def call(kernel, out_shape, operands, smem=0, out_specs=None, scratch=(), name=None):
    size = sum(o.size * 4 for o in operands)
    outs = out_shape if isinstance(out_shape, tuple) else (out_shape,)
    size += sum(o.size * 4 for o in outs)
    return pl.pallas_call(
        kernel,
        out_shape=out_shape,
        in_specs=[SMEM] * smem + [VMEM] * (len(operands) - smem),
        out_specs=out_specs if out_specs is not None else jax.tree.map(lambda _: VMEM, out_shape),
        scratch_shapes=scratch,
        cost_estimate=pl.CostEstimate(flops=20 * size, bytes_accessed=size, transcendentals=0),
        name=name,
    )(*operands)


def step_size(codes, index):
    return 0.05 * (codes[index].astype(F32) + 2.0)


def row_ids():
    return lax.broadcasted_iota(jnp.int32, (ROWS, BLOCK), 0)


def wide(row):
    return jnp.broadcast_to(row, (ROWS, BLOCK))


def ahead(own, after, lag, rows):
    return pltpu.roll(jnp.where(rows >= lag, own, after), ROWS - lag, 0)


def past(own, before, lag, rows):
    return pltpu.roll(jnp.where(rows < ROWS - lag, own, before), lag & (ROWS - 1), 0)


def row_after(own, last, rows):
    return jnp.where(rows == ROWS - 1, last, pltpu.roll(own, ROWS - 1, 0))


def row_before(own, first, rows):
    return jnp.where(rows == 0, first, pltpu.roll(own, 1, 0))


def stock_step(stock, cost, dual, dual_after, primal):
    return jnp.maximum(stock - primal * (cost - dual + dual_after), 0.0)


def price_of(prices, plant_row):
    return jnp.take_along_axis(prices, wide(plant_row), axis=1, mode="promise_in_bounds")


def load_terms(values, plant_row, plant_ids):
    high = values.astype(jnp.bfloat16).astype(F32)
    rest = values - high
    middle = rest.astype(jnp.bfloat16).astype(F32)
    pieces = jnp.concatenate([high, middle, rest - middle], 0).astype(jnp.bfloat16)
    table = (plant_ids == plant_row).astype(F32).astype(jnp.bfloat16)
    return lax.dot_general(pieces, table, (((1,), (1,)), ((), ())), preferred_element_type=F32)


def folded(total):
    return total[0:8] + total[8:16] + total[16:24]


def blocks(width):
    return [(i, pl.ds(i * BLOCK, BLOCK)) for i in range(width // BLOCK)]


def first_kernel(codes, lags, gathered, x, y, y_next, cost, load, plants, x1, bar, loads, prices):
    primal = step_size(codes, 0)
    rows = row_ids()
    plant_ids = lax.broadcasted_iota(jnp.int32, (P_SIZE, BLOCK), 0)
    each = P_SIZE // gathered.shape[0]
    for j in range(gathered.shape[0]):
        prices[:, j * each : (j + 1) * each] = gathered[j, :, :each]
    w = prices[...]
    total = jnp.zeros((3 * ROWS, P_SIZE), F32)
    for i, at in blocks(x.shape[1]):
        dual = ahead(y[:, at], y_next[:, at], lags[i], rows)
        old = x[:, at]
        charged = price_of(w, plants[:, at]) * load[:, at]
        new = jnp.maximum(old - primal * (cost[:, at] + dual + charged), 0.0)
        over = 2.0 * new - old
        x1[:, at] = new
        bar[:, at] = over
        total += load_terms(over * load[:, at], plants[:, at], plant_ids)
    loads[...] = jnp.broadcast_to(folded(total)[None], loads.shape)


def middle_kernel(
    codes, lags, x, bar, bar_prev, bar_row, v, v_next, y, y_next, d, d_next, prev_rows, far_rows,
    holding, v2, y1, partial, edge, dual_x, field_x, squares,
):
    primal = step_size(codes, 0)
    dual_step = step_size(codes, 1)
    rows = row_ids()
    square = jnp.zeros((ROWS, BLOCK), F32)
    for i, at in blocks(x.shape[1]):
        lag = lags[i]
        cost = holding[:, at]
        ya, yb = y[:, at], y_next[:, at]
        va, vb = v[:, at], v_next[:, at]
        v_before, y_before = prev_rows[0:1, at], prev_rows[1:2, at]
        y16, y17 = far_rows[0:1, at], far_rows[1:2, at]
        v16, d16 = far_rows[2:3, at], far_rows[3:4, at]
        va1 = stock_step(va, cost, ya, row_after(ya, yb[0:1], rows), primal)
        vb1 = stock_step(vb, cost, yb, row_after(yb, y16, rows), primal)
        va_bar = 2.0 * va1 - va
        vb_bar = 2.0 * vb1 - vb
        before_bar = 2.0 * stock_step(v_before, cost, y_before, ya[0:1], primal) - v_before
        far_bar = 2.0 * stock_step(v16, cost, y16, y17, primal) - v16
        ha = -d[:, at] - va_bar + row_before(va_bar, before_bar, rows)
        hb = -d_next[:, at] - vb_bar + row_before(vb_bar, va_bar[7:8], rows)
        h16 = -d16 - far_bar + vb_bar[7:8]
        own = bar[:, at]
        shifted_misfit = ahead(ha, hb, lag, rows) + own
        square += shifted_misfit * shifted_misfit
        yx = ahead(ya, yb, lag, rows) + dual_step * shifted_misfit
        dual_x[:, at] = yx
        late = past(own, bar_prev[:, at], lag, rows)
        ya1 = ya + dual_step * (ha + late)
        y1[:, at] = ya1
        y8 = yb[0:1] + dual_step * (hb[0:1] + pltpu.roll(own, lag & (ROWS - 1), 0)[0:1])
        va2 = stock_step(va1, cost, ya1, row_after(ya1, y8, rows), primal)
        v2[:, at] = va2
        va2_bar = 2.0 * va2 - va1
        edge[:, at] = va2_bar[7:8]
        partial[:, at] = -d[:, at] - va2_bar + row_before(va2_bar, jnp.zeros((1, BLOCK), F32), rows)
        whole = lag == LAGMAX
        y_end = jnp.where(whole, y16, pltpu.roll(yb, ROWS - lag, 0)[0:1])
        h_end = jnp.where(whole, h16, pltpu.roll(hb, ROWS - lag, 0)[0:1])
        yx_end = y_end + dual_step * (h_end + bar_row[:, at])
        vx1 = ahead(va1, vb1, lag, rows)
        vx2 = stock_step(vx1, cost, yx, row_after(yx, yx_end, rows), primal)
        vx_bar = 2.0 * vx2 - vx1
        first = pltpu.roll(va2_bar, ROWS - lag + 1, 0)[0:1]
        dx = ahead(d[:, at], d_next[:, at], lag, rows)
        field_x[:, at] = -dx - vx_bar + row_before(vx_bar, first, rows)
    squares[...] = square


def second_kernel(
    codes, lags, sums, prices, cap, x, dual, field, squares, cost, load, plants,
    x2, bar, loads, prices_new, excess_row,
):
    primal = step_size(codes, 0)
    plant_step = step_size(codes, 1) * (P_SIZE / (x.shape[1] * sums.shape[0]))
    plant_ids = lax.broadcasted_iota(jnp.int32, (P_SIZE, BLOCK), 0)
    excess = jnp.sum(sums[...], axis=0) - cap[...]
    w = jnp.maximum(prices[...] + plant_step * excess, 0.0)
    prices_new[...] = w
    above = jnp.maximum(excess, 0.0)
    excess_row[...] = above * above
    total = jnp.zeros((3 * ROWS, P_SIZE), F32)
    square = jnp.zeros((ROWS, BLOCK), F32)
    for i, at in blocks(x.shape[1]):
        old = x[:, at]
        charged = price_of(w, plants[:, at]) * load[:, at]
        new = jnp.maximum(old - primal * (cost[:, at] + dual[:, at] + charged), 0.0)
        over = 2.0 * new - old
        x2[:, at] = new
        bar[:, at] = over
        misfit = field[:, at] + over
        square += misfit * misfit
        total += load_terms(over * load[:, at], plants[:, at], plant_ids)
    count = loads.shape[0]
    loads[:, 0:8, :] = jnp.broadcast_to(folded(total)[None], (count, ROWS, P_SIZE))
    loads[:, 8:16, :] = jnp.broadcast_to(squares[...][None], (count, ROWS, P_SIZE))
    loads[:, 16:24, :] = jnp.broadcast_to(square[None], (count, ROWS, P_SIZE))


def third_kernel(codes, sums, prices, cap, excess_row, price_out, out, *, total_skus):
    plant_step = step_size(codes, 1) * (P_SIZE / total_skus)
    totals = jnp.sum(sums[...], axis=0)
    excess = totals[0:8] - cap[...]
    price_out[...] = jnp.maximum(prices[...] + plant_step * excess, 0.0)
    above = jnp.maximum(excess, 0.0)
    parts = [totals[8:16], excess_row[...], totals[16:24], above * above]
    packed = jnp.concatenate([jnp.sum(p, axis=0, keepdims=True) for p in parts] * 2, 0)
    out[...] = jnp.broadcast_to(packed[None], out.shape)


def last_kernel(sums, out, *, cells, rows_all):
    scale = P_SIZE / (cells // (rows_all // P_SIZE))
    totals = jnp.sum(jnp.sum(sums[...], axis=0), axis=1, keepdims=True)
    for k in range(2):
        out[k, 0] = jnp.sum(totals[2 * k : 2 * k + 1]) / cells
        out[k, 1] = jnp.sum(totals[2 * k + 1 : 2 * k + 2]) * (scale * scale) / rows_all


def dual_kernel(codes, lags, y1, partial, edge, bar, bar_prev, out):
    dual_step = step_size(codes, 1)
    rows = row_ids()
    for i, at in blocks(y1.shape[1]):
        lag = lags[i]
        field = partial[:, at] + jnp.where(rows == 0, wide(edge[:, at]), 0.0)
        out[:, at] = y1[:, at] + dual_step * (field + past(bar[:, at], bar_prev[:, at], lag, rows))


def body(
    primal_x,
    stock_v,
    balance_dual,
    plant_dual,
    demand,
    unit_cost,
    holding_cost,
    load_coef,
    capacity,
    lags,
    plants,
    step_codes,
):
    width = primal_x.shape[1]
    skus = lax.axis_size("sku")
    times = lax.axis_size("tm")
    each = plant_dual.shape[1]
    total_skus = width * skus
    owner = lax.axis_index("sku") * each
    cost = unit_cost.reshape(1, width)
    holding = holding_cost.reshape(1, width)
    load = load_coef.reshape(1, width)
    plant_row = plants.reshape(1, width)

    y_next = shifted(balance_dual, "tm", -1)
    padded = jnp.pad(plant_dual, ((0, 0), (0, P_SIZE - each)))
    gathered = spread(jnp.broadcast_to(padded[None], (skus, ROWS, P_SIZE)), "sku")
    v_next = shifted(stock_v, "tm", -1)
    d_next = shifted(demand, "tm", -1)
    prev_rows = shifted(jnp.concatenate([stock_v[7:8], balance_dual[7:8]], 0), "tm", 1)
    far_rows = shifted(jnp.concatenate([balance_dual[0:2], stock_v[0:1], demand[0:1]], 0), "tm", -2)

    x1, bar1, loads1, prices0 = call(
        first_kernel,
        (shape(ROWS, width), shape(ROWS, width), shape(skus, ROWS, P_SIZE), shape(ROWS, P_SIZE)),
        (step_codes, lags, gathered, primal_x, balance_dual, y_next, cost, load, plant_row),
        smem=2,
        name="first",
    )
    sums1 = spread(loads1, "sku")
    bar_prev = shifted(bar1, "tm", 1)
    bar_row = shifted(bar1[0:1], "tm", -1)
    v2, y1, partial, edge, dual_x, field_x, squares = call(
        middle_kernel,
        (shape(ROWS, width),) * 3
        + (shape(1, width), shape(ROWS, width), shape(ROWS, width), shape(ROWS, BLOCK)),
        (
            step_codes, lags, x1, bar1, bar_prev, bar_row, stock_v, v_next, balance_dual, y_next,
            demand, d_next, prev_rows, far_rows, holding,
        ),
        smem=2,
        name="middle",
    )
    edge_prev = shifted(edge, "tm", 1)
    x2, bar2, loads2, prices1, above1 = call(
        second_kernel,
        (
            shape(ROWS, width), shape(ROWS, width), shape(skus, 3 * ROWS, P_SIZE),
            shape(ROWS, P_SIZE), shape(ROWS, P_SIZE),
        ),
        (
            step_codes, lags, sums1, prices0, capacity, x1, dual_x, field_x, squares, cost, load,
            plant_row,
        ),
        smem=2,
        name="second",
    )
    sums2 = spread(loads2, "sku")
    bar2_prev = shifted(bar2, "tm", 1)

    def third(*refs):
        third_kernel(*refs, total_skus=total_skus)

    prices2, packed = call(
        third,
        (shape(ROWS, P_SIZE), shape(times, ROWS, P_SIZE)),
        (step_codes, sums2, prices1, capacity, above1),
        smem=1,
        name="third",
    )
    portion = lax.dynamic_slice_in_dim(prices2, owner, each, 1)
    gathered2 = spread(packed, "tm")

    def last(*refs):
        last_kernel(*refs, cells=ROWS * times * total_skus, rows_all=ROWS * times * P_SIZE)

    residuals = call(last, shape(2, 2), (gathered2,), out_specs=SMEM, name="last")
    next_y = call(
        dual_kernel,
        shape(ROWS, width),
        (step_codes, lags, y1, partial, edge_prev, bar2, bar2_prev),
        smem=2,
        name="dual",
    )
    return x2, v2, next_y, portion, residuals


def solution(mesh):
    return jax.shard_map(
        body,
        mesh=mesh,
        in_specs=(
            P("tm", "sku"),
            P("tm", "sku"),
            P("tm", "sku"),
            P("tm", "sku"),
            P("tm", "sku"),
            P("sku"),
            P("sku"),
            P("sku"),
            P("tm", None),
            P("sku"),
            P("sku"),
            P(),
        ),
        out_specs=(P("tm", "sku"), P("tm", "sku"), P("tm", "sku"), P("tm", "sku"), P()),
        check_vma=False,
    )
```

time: 269 us -> 114 us (0.42)
  blocking collectives: 182 us -> 0 us
  starting transfers between devices: 48.2 us -> 70.9 us
  Pallas kernels: 0 us -> 15.3 us
  matrix products: 12.3 us -> 0 us
  other arithmetic: 10.6 us -> 0.15 us
  waiting for transfers between devices: 8.02 us -> 13.9 us
  local copies, waits for them, and re-layouts: 5.52 us -> 11 us
    psum x3 -> x0, blocking collectives: 154 us -> none  [the longest x1 104 us: body(): results.append(lax.psum(local_sums, ('tm', 'sku')))]
    all_to_all x0 -> x4, starting transfers between devices: none -> 35.1 us  [spread(): return lax.all_to_all(value, axis, 0, 0, tiled=True)]
    all_gather x1 -> x0, blocking collectives: 27.6 us -> none  [body(): prices = lax.all_gather(plant_dual, 'sku', axis=1, tiled=True)]
    pallas_call x0 -> x6, Pallas kernels: none -> 15.3 us  [call(): pl.pallas_call(kernel, out_shape=out_shape, in_specs=[SMEM] * smem + [VME...]
    dot_general x16 -> x0, matrix products: 12.3 us -> none  [the longest x8 7.64 us: plant_price(): jnp.dot(prices, matrix.T, precision=lax.Precision.HIGHEST, preferred_elem...]
    ppermute x6 -> x9, starting transfers between devices: 48.2 us -> 35.9 us  [shifted(): lax.ppermute(value, axis, [(i, (i + steps) % count) for i in range(count)])]
    all_to_all x0 -> x4, waiting for transfers between devices: none -> 7.68 us  [spread(): return lax.all_to_all(value, axis, 0, 0, tiled=True)]
    slice x4 -> x5, local copies, waits for them, and re-layouts: 0.66 us -> 4.97 us  [the longest x1 1.08 us: body(): stock_v[0:1]]
  transfers between devices with their start and end apart: 6 -> 13, of which waited for: 3 -> 5; matrix products, arithmetic and copies ran while one was open for 5% -> 5% of each run, Pallas kernels for 0% -> 9%
where the time goes in v1:
time: 114 us; the launch traced here: 112 us
  starting transfers between devices  70.9 us (62%)
  Pallas kernels  15.3 us (13%)
  waiting for transfers between devices  13.9 us (12%)
  local copies, waits for them, and re-layouts  11 us (10%)
    ppermute x9, starting transfers between devices, shifted(): lax.ppermute(value, axis, [(i, (i + steps) % count) for i in range(count)])  35.9 us
    all_to_all x4, starting transfers between devices, spread(): return lax.all_to_all(value, axis, 0, 0, tiled=True)  35.1 us
    pallas_call x6, Pallas kernels, call(): pl.pallas_call(kernel, out_shape=out_shape, in_specs=[SMEM] * smem + [VME...  15.3 us
    all_to_all x4, waiting for transfers between devices, spread(): return lax.all_to_all(value, axis, 0, 0, tiled=True)  7.68 us
    ppermute x9, waiting for transfers between devices, shifted(): lax.ppermute(value, axis, [(i, (i + steps) % count) for i in range(count)])  6.22 us
    unnamed x32, local copies, waits for them, and re-layouts  4.02 us
  transfers between devices with their start and end apart: 13, of which 5 were waited for; matrix products, arithmetic and copies ran while one was open for 5% of the time, Pallas kernels for 9%

profile of v1, /device:TPU:1, one launch (start us, length us, event | category | flops | bytes accessed | tf_op | source)
XLA Modules:
  0.0 112.2 jit_solution(10525217217193685080)
XLA Ops:
  0.6 0.7 pad.4
  1.3 0.6 broadcast_in_dim.2
  2.0 12.0 %all-to-all-start = ((f32[16,8,128]{2,1,0:T(8,128)}), f32[16,8,128]{2,1,0:T(8,128)S(1)}, u32[]{:S(2)}, u32[]{:S(2)}) async-start(f32[16,8,128]{2,1,0:T(8,128)} %broadcast_in_dim.2), calls=%async_computation | async-start | bytes 131072 | tf_op jit(solution)/shard_map/all_to_all | solution.py:23
  14.0 2.9 %collective-permute-start = (f32[8,8192]{1,0:T(8,128)}, f32[8,8192]{1,0:T(8,128)S(1)}, u32[]{:S(2)}, u32[]{:S(2)}) collective-permute-start(f32[8,8192]{1,0:T(8,128)} %y.5), channel_id=1, source_target_pairs={{0,496},{16,0},{32,16},{48,32},{64,48},{80,64},{96,80},{112,96},{1... | collective-permute-start | bytes 786440 | tf_op jit(solution)/shard_map/ppermute | solution.py:19
  16.8 6.6 %collective-permute-start.3 = (f32[8,8192]{1,0:T(8,128)}, f32[8,8192]{1,0:T(8,128)S(1)}, u32[]{:S(2)}, u32[]{:S(2)}) collective-permute-start(f32[8,8192]{1,0:T(8,128)} %v.1), channel_id=1, source_target_pairs={{0,496},{16,0},{32,16},{48,32},{64,48},{80,64},{96,80},{112,96},{1... | collective-permute-start | bytes 786440 | tf_op jit(solution)/shard_map/ppermute | solution.py:19
  23.5 2.9 %collective-permute-start.4 = (f32[8,8192]{1,0:T(8,128)}, f32[8,8192]{1,0:T(8,128)S(1)}, u32[]{:S(2)}, u32[]{:S(2)}) collective-permute-start(f32[8,8192]{1,0:T(8,128)} %d.1), channel_id=1, source_target_pairs={{0,496},{16,0},{32,16},{48,32},{64,48},{80,64},{96,80},{112,96},{1... | collective-permute-start | bytes 786440 | tf_op jit(solution)/shard_map/ppermute | solution.py:19
  26.3 1.1 fusion
  27.4 1.0 slice.23
  28.4 1.0 slice.21
  29.4 0.1 pad_maximum_fusion
  29.5 3.8 %collective-permute-start.6 = (f32[4,8192]{1,0:T(4,128)S(1)}, f32[4,8192]{1,0:T(4,128)S(1)}, u32[]{:S(2)}, u32[]{:S(2)}) collective-permute-start(f32[4,8192]{1,0:T(4,128)S(1)} %pad_maximum_fusion), channel_id=1, source_target_pairs={{0,480},{16,496},{32,0},{48,16},{64,32},{80,48},{96,64},{112,80},{... | collective-permute-start | bytes 393224 | tf_op jit(solution)/shard_map/ppermute | solution.py:19
  33.2 1.0 slice.20
  34.2 0.0 all-to-all-done.gathered
  34.2 0.0 copy-start.7
  34.2 0.0 copy-start
  34.3 0.6 copy-done.7
  34.9 0.1 copy-done
  34.9 3.1 %first.1 = (f32[8,8192]{1,0:T(8,128)}, f32[8,8192]{1,0:T(8,128)}, f32[16,8,128]{2,1,0:T(8,128)}, f32[8,128]{1,0:T(8,128)}) custom-call(s32[2]{0:T(128)} %refs_0_.1, s32[64]{0:T(128)} %lags.7, f32[16,8,128]{2,1,0:T(8,128)} %copy-done.7, f32[8,8192]{1,0:T(8,128)} %x.3, f32[8,8192]{1,0:T(8,128)} %y.5, f32[8,8192]{1,0:T(8,128)} %copy-done, f32[1,8192]{1,0:T(1,128)} %bitcast.4, ...), custom_call_target="tpu_custom_call" | custom-call | flops 30889120 | bytes 1544456 | tf_op jit(solution)/shard_map/first/pallas_call | solution.py:34
  38.1 7.9 %all-to-all-start.1 = ((f32[16,8,128]{2,1,0:T(8,128)}), f32[16,8,128]{2,1,0:T(8,128)S(1)}, u32[]{:S(2)}, u32[]{:S(2)}) async-start(f32[16,8,128]{2,1,0:T(8,128)} %get-tuple-element.23), calls=%async_computation.1 | async-start | bytes 131072 | tf_op jit(solution)/shard_map/all_to_all | solution.py:23
  46.0 3.8 %collective-permute-start.1 = (f32[8,8192]{1,0:T(8,128)}, f32[8,8192]{1,0:T(8,128)S(1)}, u32[]{:S(2)}, u32[]{:S(2)}) collective-permute-start(f32[8,8192]{1,0:T(8,128)} %get-tuple-element.26.bar), channel_id=1, source_target_pairs={{0,16},{16,32},{32,48},{48,64},{64,80},{80,96},{96,112},{112,128},... | collective-permute-start | bytes 786440 | tf_op jit(solution)/shard_map/ppermute | solution.py:19
  49.8 0.1 pad_maximum_fusion.1
  49.9 1.9 %collective-permute-start.5 = (f32[2,8192]{1,0:T(2,128)S(1)}, f32[2,8192]{1,0:T(2,128)S(1)}, u32[]{:S(2)}, u32[]{:S(2)}) collective-permute-start(f32[2,8192]{1,0:T(2,128)S(1)} %pad_maximum_fusion.1), channel_id=1, source_target_pairs={{0,16},{16,32},{32,48},{48,64},{64,80},{80,96},{96,112},{112,128},... | collective-permute-start | bytes 196616 | tf_op jit(solution)/shard_map/ppermute | solution.py:19
  51.8 1.0 slice.18
  52.8 4.4 %collective-permute-done.5.prev_rows = f32[2,8192]{1,0:T(2,128)S(1)} collective-permute-done((f32[2,8192]{1,0:T(2,128)S(1)}, f32[2,8192]{1,0:T(2,128)S(1)}, u32[]{:S(2)}, u32[]{:S(2)}) %collective-permute-start.5) | collective-permute-done | bytes 65568 | tf_op jit(solution)/shard_map/ppermute | solution.py:19
  57.2 7.6 %collective-permute-start.2 = (f32[1,8192]{1,0:T(1,128)S(1)}, f32[1,8192]{1,0:T(1,128)S(1)}, u32[]{:S(2)}, u32[]{:S(2)}) collective-permute-start(f32[1,8192]{1,0:T(1,128)S(1)} %slice.18), channel_id=1, source_target_pairs={{0,496},{16,0},{32,16},{48,32},{64,48},{80,64},{96,80},{112,96},{1... | collective-permute-start | bytes 98312 | tf_op jit(solution)/shard_map/ppermute | solution.py:19
  64.8 0.0 collective-permute-done.6.far_rows
  64.9 0.0 collective-permute-done.3.v_next
  64.9 0.8 collective-permute-done.2.bar_row
  65.7 0.6 copy-done.12
  66.3 0.1 copy-done.5
  66.4 3.7 %middle.1 = (f32[8,8192]{1,0:T(8,128)}, f32[8,8192]{1,0:T(8,128)}, f32[8,8192]{1,0:T(8,128)}, f32[1,8192]{1,0:T(1,128)}, f32[8,8192]{1,0:T(8,128)}, /*index=5*/f32[8,8192]{1,0:T(8,128)}, f32[8,128]{1,0:T(8,128)}) custom-call(s32[2]{0:T(128)} %refs_0_.1, s32[64]{0:T(128)} %lags.7, f32[8,8192]{1,0:T(8,128)} %get-tuple-element.25.x, ...), custom_call_target="tpu_custom_call" | custom-call | flops 79385760 | bytes 3969288 | tf_op jit(solution)/shard_map/middle/pallas_call | solution.py:34
  70.1 0.6 copy-done.6
  70.7 3.2 %second.1 = (f32[8,8192]{1,0:T(8,128)}, f32[8,8192]{1,0:T(8,128)}, f32[16,24,128]{2,1,0:T(8,128)}, f32[8,128]{1,0:T(8,128)}, f32[8,128]{1,0:T(8,128)}) custom-call(s32[2]{0:T(128)} %refs_0_.1, s32[64]{0:T(128)} %lags.7, f32[16,8,128]{2,1,0:T(8,128)} %copy-done.6, f32[8,128]{1,0:T(8,128)} %get-tuple-element.24.prices, f32[8,128]{1,0:T(8,128)} %refs_3_.1, ...), custom_call_target="tpu_custom_call" | custom-call | flops 33838240 | bytes 1691912 | tf_op jit(solution)/shard_map/second/pallas_call | solution.py:34
  73.9 7.1 %all-to-all-start.2 = ((f32[16,24,128]{2,1,0:T(8,128)}), f32[16,24,128]{2,1,0:T(8,128)S(1)}, u32[]{:S(2)}, u32[]{:S(2)}) async-start(f32[16,24,128]{2,1,0:T(8,128)} %get-tuple-element.36), calls=%async_computation.2 | async-start | bytes 393216 | tf_op jit(solution)/shard_map/all_to_all | solution.py:23
  81.0 1.9 %collective-permute-start.8 = (f32[8,8192]{1,0:T(8,128)S(1)}, f32[8,8192]{1,0:T(8,128)S(1)}, u32[]{:S(2)}, u32[]{:S(2)}) collective-permute-start(f32[8,8192]{1,0:T(8,128)S(1)} %copy-done.8), channel_id=1, source_target_pairs={{0,16},{16,32},{32,48},{48,64},{64,80},{80,96},{96,112},{112,128},... | collective-permute-start | bytes 786440 | tf_op jit(solution)/shard_map/ppermute | solution.py:19
  82.9 5.8 %all-to-all-done.2.refs_1_ = f32[16,24,128]{2,1,0:T(8,128)S(1)} async-done(((f32[16,24,128]{2,1,0:T(8,128)}), f32[16,24,128]{2,1,0:T(8,128)S(1)}, u32[]{:S(2)}, u32[]{:S(2)}) %all-to-all-start.2) | async-done | bytes 196640 | tf_op jit(solution)/shard_map/all_to_all | solution.py:23
  88.6 0.7 copy-done.1
  89.3 1.6 %third.1 = (f32[8,128]{1,0:T(8,128)}, f32[32,8,128]{2,1,0:T(8,128)}) custom-call(s32[2]{0:T(128)} %refs_0_.1, f32[16,24,128]{2,1,0:T(8,128)} %copy-done.1, f32[8,128]{1,0:T(8,128)} %get-tuple-element.37.refs_2_, f32[8,128]{1,0:T(8,128)} %refs_3_.1, f32[8,128]{1,0:T(8,128)} %get-tuple-element.38.refs_4_), custom_call_target="tpu_custom_call" | custom-call | flops 6881440 | bytes 344072 | tf_op jit(solution)/shard_map/third/pallas_call | solution.py:34
  91.0 8.2 %all-to-all-start.3 = ((f32[32,8,128]{2,1,0:T(8,128)}), f32[32,8,128]{2,1,0:T(8,128)S(1)}, u32[]{:S(2)}, u32[]{:S(2)}) async-start(f32[32,8,128]{2,1,0:T(8,128)} %get-tuple-element.40), calls=%async_computation.3 | async-start | bytes 262144 | tf_op jit(solution)/shard_map/all_to_all | solution.py:23
  99.1 4.4 %collective-permute-start.7 = (f32[1,8192]{1,0:T(1,128)S(1)}, f32[1,8192]{1,0:T(1,128)S(1)}, u32[]{:S(2)}, u32[]{:S(2)}) collective-permute-start(f32[1,8192]{1,0:T(1,128)S(1)} %copy-done.15), channel_id=1, source_target_pairs={{0,16},{16,32},{32,48},{48,64},{64,80},{80,96},{96,112},{112,128},... | collective-permute-start | bytes 98312 | tf_op jit(solution)/shard_map/ppermute | solution.py:19
  103.6 1.0 collective-permute-done.7.edge
  104.6 0.6 copy-done.13
  105.2 0.1 copy-done.9
  105.3 2.0 %dual.1 = f32[8,8192]{1,0:T(8,128)} custom-call(s32[2]{0:T(128)} %refs_0_.1, s32[64]{0:T(128)} %lags.7, f32[8,8192]{1,0:T(8,128)} %get-tuple-element.32.y1, f32[8,8192]{1,0:T(8,128)} %get-tuple-element.33.partial, f32[1,8192]{1,0:T(1,128)} %copy-done.13, f32[8,8192]{1,0:T(8,128)} %get-tuple-element.35.bar, f32[8,8192]{1,0:T(8,128)} %copy-done.9), custom_call_target="tpu_custom_call" | custom-call | flops 26875040 | bytes 1343752 | tf_op jit(solution)/shard_map/dual/pallas_call | solution.py:34
  107.3 0.7 constant_dynamic-slice_fusion
  108.0 1.9 %all-to-all-done.3.refs_0_ = f32[32,8,128]{2,1,0:T(8,128)S(1)} async-done(((f32[32,8,128]{2,1,0:T(8,128)}), f32[32,8,128]{2,1,0:T(8,128)S(1)}, u32[]{:S(2)}, u32[]{:S(2)}) %all-to-all-start.3) | async-done | bytes 131104 | tf_op jit(solution)/shard_map/all_to_all | solution.py:23
  109.9 0.6 copy-done.2
  110.5 1.6 %last.1 = f32[2,2]{1,0:T(2,128)} custom-call(f32[32,8,128]{2,1,0:T(8,128)} %copy-done.2), custom_call_target="tpu_custom_call" | custom-call | flops 2621760 | bytes 131088 | tf_op jit(solution)/shard_map/last/pallas_call | solution.py:34
  (26 shorter events, 0.1 us)
Async XLA Ops:
  2.0 32.2 %all-to-all-start = ((f32[16,8,128]{2,1,0:T(8,128)}), f32[16,8,128]{2,1,0:T(8,128)S(1)}, u32[]{:S(2)}, u32[]{:S(2)}) async-start(f32[16,8,128]{2,1,0:T(8,128)} %broadcast_in_dim.2), calls=%async_computation | async-start | bytes 131072 | tf_op jit(solution)/shard_map/all_to_all | solution.py:23
  14.0 20.3 %collective-permute-start = (f32[8,8192]{1,0:T(8,128)}, f32[8,8192]{1,0:T(8,128)S(1)}, u32[]{:S(2)}, u32[]{:S(2)}) collective-permute-start(f32[8,8192]{1,0:T(8,128)} %y.5), channel_id=1, source_target_pairs={{0,496},{16,0},{32,16},{48,32},{64,48},{80,64},{96,80},{112,96},{1... | collective-permute-start | bytes 786440 | tf_op jit(solution)/shard_map/ppermute | solution.py:19
  16.8 48.0 %collective-permute-start.3 = (f32[8,8192]{1,0:T(8,128)}, f32[8,8192]{1,0:T(8,128)S(1)}, u32[]{:S(2)}, u32[]{:S(2)}) collective-permute-start(f32[8,8192]{1,0:T(8,128)} %v.1), channel_id=1, source_target_pairs={{0,496},{16,0},{32,16},{48,32},{64,48},{80,64},{96,80},{112,96},{1... | collective-permute-start | bytes 786440 | tf_op jit(solution)/shard_map/ppermute | solution.py:19
  23.5 41.4 %collective-permute-start.4 = (f32[8,8192]{1,0:T(8,128)}, f32[8,8192]{1,0:T(8,128)S(1)}, u32[]{:S(2)}, u32[]{:S(2)}) collective-permute-start(f32[8,8192]{1,0:T(8,128)} %d.1), channel_id=1, source_target_pairs={{0,496},{16,0},{32,16},{48,32},{64,48},{80,64},{96,80},{112,96},{1... | collective-permute-start | bytes 786440 | tf_op jit(solution)/shard_map/ppermute | solution.py:19
  29.5 35.4 %collective-permute-start.6 = (f32[4,8192]{1,0:T(4,128)S(1)}, f32[4,8192]{1,0:T(4,128)S(1)}, u32[]{:S(2)}, u32[]{:S(2)}) collective-permute-start(f32[4,8192]{1,0:T(4,128)S(1)} %pad_maximum_fusion), channel_id=1, source_target_pairs={{0,480},{16,496},{32,0},{48,16},{64,32},{80,48},{96,64},{112,80},{... | collective-permute-start | bytes 393224 | tf_op jit(solution)/shard_map/ppermute | solution.py:19
  34.2 0.6 copy-start.7
  34.2 0.7 copy-start
  38.1 32.0 %all-to-all-start.1 = ((f32[16,8,128]{2,1,0:T(8,128)}), f32[16,8,128]{2,1,0:T(8,128)S(1)}, u32[]{:S(2)}, u32[]{:S(2)}) async-start(f32[16,8,128]{2,1,0:T(8,128)} %get-tuple-element.23), calls=%async_computation.1 | async-start | bytes 131072 | tf_op jit(solution)/shard_map/all_to_all | solution.py:23
  46.0 19.7 %collective-permute-start.1 = (f32[8,8192]{1,0:T(8,128)}, f32[8,8192]{1,0:T(8,128)S(1)}, u32[]{:S(2)}, u32[]{:S(2)}) collective-permute-start(f32[8,8192]{1,0:T(8,128)} %get-tuple-element.26.bar), channel_id=1, source_target_pairs={{0,16},{16,32},{32,48},{48,64},{64,80},{80,96},{96,112},{112,128},... | collective-permute-start | bytes 786440 | tf_op jit(solution)/shard_map/ppermute | solution.py:19
  49.9 7.3 %collective-permute-start.5 = (f32[2,8192]{1,0:T(2,128)S(1)}, f32[2,8192]{1,0:T(2,128)S(1)}, u32[]{:S(2)}, u32[]{:S(2)}) collective-permute-start(f32[2,8192]{1,0:T(2,128)S(1)} %pad_maximum_fusion.1), channel_id=1, source_target_pairs={{0,16},{16,32},{32,48},{48,64},{64,80},{80,96},{96,112},{112,128},... | collective-permute-start | bytes 196616 | tf_op jit(solution)/shard_map/ppermute | solution.py:19
  57.2 8.5 %copy-start.11 = (f32[2,8192]{1,0:T(2,128)}, f32[2,8192]{1,0:T(2,128)S(1)}, u32[]{:S(2)}) copy-start(f32[2,8192]{1,0:T(2,128)S(1)} %collective-permute-done.5.prev_rows) | copy-start | bytes 196612
  57.2 8.5 %collective-permute-start.2 = (f32[1,8192]{1,0:T(1,128)S(1)}, f32[1,8192]{1,0:T(1,128)S(1)}, u32[]{:S(2)}, u32[]{:S(2)}) collective-permute-start(f32[1,8192]{1,0:T(1,128)S(1)} %slice.18), channel_id=1, source_target_pairs={{0,496},{16,0},{32,16},{48,32},{64,48},{80,64},{96,80},{112,96},{1... | collective-permute-start | bytes 98312 | tf_op jit(solution)/shard_map/ppermute | solution.py:19
  64.8 0.8 copy-start.10
  64.9 0.8 copy-start.3
  64.9 0.8 copy-start.4
  65.7 0.6 copy-start.12
  65.7 0.7 copy-start.5
  70.1 0.6 copy-start.6
  73.9 7.1 %copy-start.8 = (f32[8,8192]{1,0:T(8,128)S(1)}, f32[8,8192]{1,0:T(8,128)}, u32[]{:S(2)}) copy-start(f32[8,8192]{1,0:T(8,128)} %get-tuple-element.35.bar) | copy-start | bytes 786436
  73.9 14.8 %all-to-all-start.2 = ((f32[16,24,128]{2,1,0:T(8,128)}), f32[16,24,128]{2,1,0:T(8,128)S(1)}, u32[]{:S(2)}, u32[]{:S(2)}) async-start(f32[16,24,128]{2,1,0:T(8,128)} %get-tuple-element.36), calls=%async_computation.2 | async-start | bytes 393216 | tf_op jit(solution)/shard_map/all_to_all | solution.py:23
  81.0 23.6 %collective-permute-start.8 = (f32[8,8192]{1,0:T(8,128)S(1)}, f32[8,8192]{1,0:T(8,128)S(1)}, u32[]{:S(2)}, u32[]{:S(2)}) collective-permute-start(f32[8,8192]{1,0:T(8,128)S(1)} %copy-done.8), channel_id=1, source_target_pairs={{0,16},{16,32},{32,48},{48,64},{64,80},{80,96},{96,112},{112,128},... | collective-permute-start | bytes 786440 | tf_op jit(solution)/shard_map/ppermute | solution.py:19
  88.6 0.7 copy-start.1
  91.0 8.2 %copy-start.15 = (f32[1,8192]{1,0:T(1,128)S(1)}, f32[1,8192]{1,0:T(1,128)}, u32[]{:S(2)}) copy-start(f32[1,8192]{1,0:T(1,128)} %get-tuple-element.34) | copy-start | bytes 98308
  91.0 18.9 %all-to-all-start.3 = ((f32[32,8,128]{2,1,0:T(8,128)}), f32[32,8,128]{2,1,0:T(8,128)S(1)}, u32[]{:S(2)}, u32[]{:S(2)}) async-start(f32[32,8,128]{2,1,0:T(8,128)} %get-tuple-element.40), calls=%async_computation.3 | async-start | bytes 262144 | tf_op jit(solution)/shard_map/all_to_all | solution.py:23
  99.1 5.4 %collective-permute-start.7 = (f32[1,8192]{1,0:T(1,128)S(1)}, f32[1,8192]{1,0:T(1,128)S(1)}, u32[]{:S(2)}, u32[]{:S(2)}) collective-permute-start(f32[1,8192]{1,0:T(1,128)S(1)} %copy-done.15), channel_id=1, source_target_pairs={{0,16},{16,32},{32,48},{48,64},{64,80},{80,96},{96,112},{112,128},... | collective-permute-start | bytes 98312 | tf_op jit(solution)/shard_map/ppermute | solution.py:19
  104.6 0.6 copy-start.13
  104.6 0.7 copy-start.9
  105.3 2.0 %copy-start.14 = (f32[8,128]{1,0:T(8,128)S(1)}, f32[8,128]{1,0:T(8,128)}, u32[]{:S(2)}) copy-start(f32[8,128]{1,0:T(8,128)} %get-tuple-element.39) | copy-start | bytes 12292
  109.9 0.6 copy-start.2

commit v2 on v1

v2 whole, which is shorter than its diff:
```python
import jax
import jax.numpy as jnp
from jax import lax
from jax.experimental import pallas as pl
from jax.experimental.pallas import tpu as pltpu
from jax.sharding import PartitionSpec as P

P_SIZE = 128
LAGMAX = 8
BLOCK = 128
ROWS = 8
F32 = jnp.float32
VMEM = pl.BlockSpec(memory_space=pltpu.VMEM)
SMEM = pl.BlockSpec(memory_space=pltpu.SMEM)


def shifted(value, axis, steps):
    count = lax.axis_size(axis)
    return lax.ppermute(value, axis, [(i, (i + steps) % count) for i in range(count)])


def spread(value, axis):
    return lax.all_to_all(value, axis, 0, 0, tiled=True)


def shape(*dims):
    return jax.ShapeDtypeStruct(dims, F32)


def call(kernel, out_shape, operands, smem=0, out_specs=None, name=None, grant=16):
    size = sum(o.size * 4 for o in operands)
    outs = out_shape if isinstance(out_shape, tuple) else (out_shape,)
    size += sum(o.size * 4 for o in outs)
    return pl.pallas_call(
        kernel,
        out_shape=out_shape,
        in_specs=[SMEM] * smem + [VMEM] * (len(operands) - smem),
        out_specs=out_specs if out_specs is not None else jax.tree.map(lambda _: VMEM, out_shape),
        cost_estimate=pl.CostEstimate(flops=20 * size, bytes_accessed=size, transcendentals=0),
        name=name,
        compiler_params=pltpu.CompilerParams(vmem_limit_bytes=grant * 2**20),
    )(*operands)


def step_size(codes, index):
    return 0.05 * (codes[index].astype(F32) + 2.0)


def row_ids():
    return lax.broadcasted_iota(jnp.int32, (ROWS, BLOCK), 0)


def wide(row):
    return jnp.broadcast_to(row, (ROWS, BLOCK))


def ahead(own, after, lag, rows):
    return pltpu.roll(jnp.where(rows >= lag, own, after), ROWS - lag, 0)


def past(own, before, lag, rows):
    return pltpu.roll(jnp.where(rows < ROWS - lag, own, before), lag & (ROWS - 1), 0)


def row_after(own, last, rows):
    return jnp.where(rows == ROWS - 1, last, pltpu.roll(own, ROWS - 1, 0))


def row_before(own, first, rows):
    return jnp.where(rows == 0, first, pltpu.roll(own, 1, 0))


def stock_step(stock, cost, dual, dual_after, primal):
    return jnp.maximum(stock - primal * (cost - dual + dual_after), 0.0)


def price_of(prices, plant_row):
    return jnp.take_along_axis(prices, wide(plant_row), axis=1, mode="promise_in_bounds")


def load_terms(values, plant_row, plant_ids):
    high = values.astype(jnp.bfloat16).astype(F32)
    rest = values - high
    middle = rest.astype(jnp.bfloat16).astype(F32)
    pieces = jnp.concatenate([high, middle, rest - middle], 0).astype(jnp.bfloat16)
    table = jnp.where(plant_ids == plant_row, 1.0, 0.0).astype(jnp.bfloat16)
    return lax.dot_general(table, pieces, (((1,), (1,)), ((), ())), preferred_element_type=F32)


def folded(total):
    total = total.T
    return total[0:8] + total[8:16] + total[16:24]


def blocks(width):
    return [(i, pl.ds(i * BLOCK, BLOCK)) for i in range(width // BLOCK)]


def extra_slot(index, width, slot):
    each = width // ROWS // BLOCK
    start = width + slot * (width // ROWS) + (index % each) * BLOCK
    return slice(index // each, index // each + 1), slice(start, start + BLOCK)


def start_kernel(w, y, v, d, payload, sent, stock):
    width = y.shape[1]
    each = w.shape[1]
    payload[:, 0:ROWS, 0:each] = jnp.broadcast_to(w[...][None], (payload.shape[0], ROWS, each))
    sent[:, 0:width] = y[...]
    stock[:, 0:width] = v[...]
    for i, at in blocks(width):
        sent[extra_slot(i, width, 0)] = v[0:1, at]
        sent[extra_slot(i, width, 1)] = d[0:1, at]
        stock[extra_slot(i, width, 0)] = d[0:1, at]
        stock[extra_slot(i, width, 1)] = d[1:2, at]


def first_kernel(
    codes, lags, gathered, x, y, y_next, v, d, cost, holding, load, plants, cap,
    x1, up, down, loads, prices, limits,
):
    primal = step_size(codes, 0)
    rows = row_ids()
    plant_ids = lax.broadcasted_iota(jnp.int32, (P_SIZE, BLOCK), 0)
    width = x.shape[1]
    each = P_SIZE // gathered.shape[0]
    for j in range(gathered.shape[0]):
        prices[:, j * each : (j + 1) * each] = gathered[j, 0:ROWS, 0:each]
    w = prices[...]
    limits[...] = cap[...]
    total = jnp.zeros((P_SIZE, 3 * ROWS), F32)
    for i, at in blocks(width):
        lag = lags[i]
        yb = y_next[:, at]
        dual = ahead(y[:, at], yb, lag, rows)
        old = x[:, at]
        charged = price_of(w, plants[:, at]) * load[:, at]
        new = jnp.maximum(old - primal * (cost[:, at] + dual + charged), 0.0)
        over = 2.0 * new - old
        x1[:, at] = new
        total += load_terms(over * load[:, at], plants[:, at], plant_ids)
        v7, v8 = v[7:8, at], y_next[extra_slot(i, width, 0)]
        d8 = y_next[extra_slot(i, width, 1)]
        bar7 = 2.0 * stock_step(v7, holding[:, at], y[7:8, at], yb[0:1], primal) - v7
        bar8 = 2.0 * stock_step(v8, holding[:, at], yb[0:1], yb[1:2], primal) - v8
        up[:, at] = over
        up[extra_slot(i, width, 0)] = bar7
        first_row = over[0:1] + jnp.where(lag == LAGMAX, -d8 - bar8 + bar7, 0.0)
        down[:, at] = jnp.where(rows == 0, first_row, jnp.where(rows == 1, yb[0:1], d[:, at]))
    loads[...] = jnp.broadcast_to(folded(total)[None], loads.shape)


def middle_kernel(
    codes, lags, bar, bar_prev, after, y, y_next, v, v_next, d, holding,
    v2, dual_x, field_x, squares,
):
    primal = step_size(codes, 0)
    dual_step = step_size(codes, 1)
    rows = row_ids()
    width = v.shape[1]
    square = jnp.zeros((ROWS, BLOCK), F32)
    for i, at in blocks(width):
        lag = lags[i]
        cost = holding[:, at]
        ya, yb = y[:, at], y_next[:, at]
        va, vb = v[:, at], v_next[:, at]
        da, mixed = d[:, at], after[:, at]
        d8, d9 = v_next[extra_slot(i, width, 0)], v_next[extra_slot(i, width, 1)]
        bar8, y16 = mixed[0:1], mixed[1:2]
        db = jnp.where(rows == 0, d8, jnp.where(rows == 1, d9, mixed))
        bar_before = bar_prev[extra_slot(i, width, 0)]
        over = bar[:, at]
        va1 = stock_step(va, cost, ya, row_after(ya, yb[0:1], rows), primal)
        vb1 = stock_step(vb, cost, yb, row_after(yb, y16, rows), primal)
        va_bar = 2.0 * va1 - va
        vb_bar = 2.0 * vb1 - vb
        ha = -da - va_bar + row_before(va_bar, bar_before, rows)
        hb = -db - vb_bar + row_before(vb_bar, va_bar[7:8], rows)
        misfit = ahead(ha, hb, lag, rows) + over
        square += misfit * misfit
        yx = ahead(ya, yb, lag, rows) + dual_step * misfit
        dual_x[:, at] = yx
        ya1 = ya + dual_step * (ha + past(over, bar_prev[:, at], lag, rows))
        y8 = yb[0:1] + dual_step * (hb[0:1] + pltpu.roll(over, lag & (ROWS - 1), 0)[0:1])
        va2 = stock_step(va1, cost, ya1, row_after(ya1, y8, rows), primal)
        v2[:, at] = va2
        start_bar = pltpu.roll(2.0 * va2 - va1, ROWS - lag + 1, 0)[0:1]
        whole = lag == LAGMAX
        y_end = jnp.where(whole, y16, pltpu.roll(yb, ROWS - lag, 0)[0:1])
        h_end = jnp.where(whole, 0.0, pltpu.roll(hb, ROWS - lag, 0)[0:1])
        yx_end = y_end + dual_step * (h_end + bar8)
        vx1 = ahead(va1, vb1, lag, rows)
        vx2 = stock_step(vx1, cost, yx, row_after(yx, yx_end, rows), primal)
        vx_bar = 2.0 * vx2 - vx1
        dx = ahead(da, db, lag, rows)
        field_x[:, at] = -dx - vx_bar + row_before(vx_bar, start_bar, rows)
    squares[...] = jnp.sum(square, axis=0, keepdims=True)


def second_kernel(
    codes, sums, prices, cap, x, dual, field, squares, cost, load, plants,
    x2, dual_x, loads, prices_new, excess_row,
):
    primal = step_size(codes, 0)
    dual_step = step_size(codes, 1)
    plant_step = dual_step * (P_SIZE / (x.shape[1] * sums.shape[0]))
    plant_ids = lax.broadcasted_iota(jnp.int32, (P_SIZE, BLOCK), 0)
    excess = jnp.sum(sums[...], axis=0) - cap[...]
    w = jnp.maximum(prices[...] + plant_step * excess, 0.0)
    prices_new[...] = w
    above = jnp.maximum(excess, 0.0)
    excess_row[...] = jnp.sum(above * above, axis=0, keepdims=True)
    total = jnp.zeros((P_SIZE, 3 * ROWS), F32)
    square = jnp.zeros((ROWS, BLOCK), F32)
    for i, at in blocks(x.shape[1]):
        old = x[:, at]
        charged = price_of(w, plants[:, at]) * load[:, at]
        new = jnp.maximum(old - primal * (cost[:, at] + dual[:, at] + charged), 0.0)
        over = 2.0 * new - old
        x2[:, at] = new
        misfit = field[:, at] + over
        dual_x[:, at] = dual[:, at] + dual_step * misfit
        square += misfit * misfit
        total += load_terms(over * load[:, at], plants[:, at], plant_ids)
    count = loads.shape[0]
    lines = jnp.concatenate([squares[...], jnp.sum(square, axis=0, keepdims=True)] * 4, 0)
    loads[:, 0:8, :] = jnp.broadcast_to(folded(total)[None], (count, ROWS, P_SIZE))
    loads[:, 8:16, :] = jnp.broadcast_to(lines[None], (count, ROWS, P_SIZE))


def third_kernel(codes, sums, prices, cap, excess_row, price_out, out, *, total_skus):
    plant_step = step_size(codes, 1) * (P_SIZE / total_skus)
    totals = jnp.sum(sums[...], axis=0)
    excess = totals[0:8] - cap[...]
    price_out[...] = jnp.maximum(prices[...] + plant_step * excess, 0.0)
    above = jnp.maximum(excess, 0.0)
    above_row = jnp.sum(above * above, axis=0, keepdims=True)
    packed = jnp.concatenate([totals[8:9], excess_row[...], totals[9:10], above_row] * 2, 0)
    out[...] = jnp.broadcast_to(packed[None], out.shape)


def unshift_kernel(lags, dual, dual_prev, y):
    rows = row_ids()
    for i, at in blocks(y.shape[1]):
        y[:, at] = past(dual[:, at], dual_prev[:, at], lags[i], rows)


def body(
    primal_x,
    stock_v,
    balance_dual,
    plant_dual,
    demand,
    unit_cost,
    holding_cost,
    load_coef,
    capacity,
    lags,
    plants,
    step_codes,
):
    width = primal_x.shape[1]
    skus = lax.axis_size("sku")
    times = lax.axis_size("tm")
    each = plant_dual.shape[1]
    total_skus = width * skus
    owner = lax.axis_index("sku") * each
    cost = unit_cost.reshape(1, width)
    holding = holding_cost.reshape(1, width)
    load = load_coef.reshape(1, width)
    plant_row = plants.reshape(1, width)

    longer = width + 2 * (width // ROWS)
    payload, y_sent, v_sent = call(
        start_kernel,
        (shape(skus, 2 * ROWS, P_SIZE), shape(ROWS, longer), shape(ROWS, longer)),
        (plant_dual, balance_dual, stock_v, demand),
        name="start",
        grant=60,
    )
    gathered = spread(payload, "sku")
    y_next = shifted(y_sent, "tm", -1)
    v_next = shifted(v_sent, "tm", -1)

    x1, up, down, loads1, prices0, limits = call(
        first_kernel,
        (
            shape(ROWS, width), shape(ROWS, width + width // ROWS), shape(ROWS, width),
            shape(skus, ROWS, P_SIZE), shape(ROWS, P_SIZE), shape(ROWS, P_SIZE),
        ),
        (
            step_codes, lags, gathered, primal_x, balance_dual, y_next, stock_v, demand, cost,
            holding, load, plant_row, capacity,
        ),
        smem=2,
        name="first",
        grant=60,
    )
    bar_prev = shifted(up, "tm", 1)
    after = shifted(down, "tm", -1)
    sums1 = spread(loads1, "sku")
    v2, dual_x, field_x, squares = call(
        middle_kernel,
        (shape(ROWS, width),) * 3 + (shape(1, BLOCK),),
        (
            step_codes, lags, up, bar_prev, after, balance_dual, y_next, stock_v, v_next, demand,
            holding,
        ),
        smem=2,
        name="middle",
    )
    x2, dual_x2, loads2, prices1, above1 = call(
        second_kernel,
        (
            shape(ROWS, width), shape(ROWS, width), shape(skus, 2 * ROWS, P_SIZE),
            shape(ROWS, P_SIZE), shape(1, P_SIZE),
        ),
        (
            step_codes, sums1, prices0, limits, x1, dual_x, field_x, squares, cost, load,
            plant_row,
        ),
        smem=1,
        name="second",
    )
    sums2 = spread(loads2, "sku")
    dual_prev = shifted(dual_x2, "tm", 1)

    def third(*refs):
        third_kernel(*refs, total_skus=total_skus)

    prices2, packed = call(
        third,
        (shape(ROWS, P_SIZE), shape(times, ROWS, P_SIZE)),
        (step_codes, sums2, prices1, limits, above1),
        smem=1,
        name="third",
    )
    portion = lax.dynamic_slice_in_dim(prices2, owner, each, 1)
    totals = jnp.sum(spread(packed, "tm")[:, 0:4], axis=(0, 2))
    scale = P_SIZE / total_skus
    cells, cap_rows = ROWS * times * total_skus, ROWS * times * P_SIZE
    factors = jnp.array([1.0 / cells, scale * scale / cap_rows] * 2, F32)
    residuals = (totals * factors).reshape(2, 2)
    next_y = call(
        unshift_kernel, shape(ROWS, width), (lags, dual_x2, dual_prev), smem=1, name="unshift"
    )
    return x2, v2, next_y, portion, residuals


def solution(mesh):
    return jax.shard_map(
        body,
        mesh=mesh,
        in_specs=(
            P("tm", "sku"),
            P("tm", "sku"),
            P("tm", "sku"),
            P("tm", "sku"),
            P("tm", "sku"),
            P("sku"),
            P("sku"),
            P("sku"),
            P("tm", None),
            P("sku"),
            P("sku"),
            P(),
        ),
        out_specs=(P("tm", "sku"), P("tm", "sku"), P("tm", "sku"), P("tm", "sku"), P()),
        check_vma=False,
    )
```

time: 114 us -> 92.9 us (0.81)
  starting transfers between devices: 70.9 us -> 55.8 us
  local copies, waits for them, and re-layouts: 11 us -> 4.71 us
  waiting for transfers between devices: 13.9 us -> 18.6 us
  Pallas kernels: 15.3 us -> 12 us
    all_to_all x4, waiting for transfers between devices: 7.68 us -> 16.8 us  [spread(): return lax.all_to_all(value, axis, 0, 0, tiled=True)]
    all_to_all x4, starting transfers between devices: 35.1 us -> 26.5 us  [spread(): return lax.all_to_all(value, axis, 0, 0, tiled=True)]
    ppermute x9 -> x5, starting transfers between devices: 35.9 us -> 29.3 us  [shifted(): lax.ppermute(value, axis, [(i, (i + steps) % count) for i in range(count)])]
    slice x5 -> x0, local copies, waits for them, and re-layouts: 4.97 us -> none  [the longest x1 1.08 us: body(): stock_v[0:1]]
    ppermute x9 -> x5, waiting for transfers between devices: 6.22 us -> 1.84 us  [shifted(): lax.ppermute(value, axis, [(i, (i + steps) % count) for i in range(count)])]
    pallas_call x6, Pallas kernels: 15.3 us -> 12 us  [call(): pl.pallas_call(kernel, out_shape=out_shape, in_specs=[SMEM] * smem + [VME...]
    unnamed x32 -> x34, local copies, waits for them, and re-layouts: 4.02 us -> 3.4 us
  transfers between devices with their start and end apart: 13 -> 9, of which waited for: 5 -> 5; matrix products, arithmetic and copies ran while one was open for 5% -> 1% of each run, Pallas kernels for 9% -> 9%
where the time goes in v2:
time: 92.9 us; the launch traced here: 92.1 us
  starting transfers between devices  55.8 us (60%)
  waiting for transfers between devices  18.6 us (20%)
  Pallas kernels  12 us (13%)
  local copies, waits for them, and re-layouts  4.71 us (5%)
    ppermute x5, starting transfers between devices, shifted(): lax.ppermute(value, axis, [(i, (i + steps) % count) for i in range(count)])  29.3 us
    all_to_all x4, starting transfers between devices, spread(): return lax.all_to_all(value, axis, 0, 0, tiled=True)  26.5 us
    all_to_all x4, waiting for transfers between devices, spread(): return lax.all_to_all(value, axis, 0, 0, tiled=True)  16.8 us
    pallas_call x6, Pallas kernels, call(): pl.pallas_call(kernel, out_shape=out_shape, in_specs=[SMEM] * smem + [VME...  12 us
    unnamed x34, local copies, waits for them, and re-layouts  3.4 us
  transfers between devices with their start and end apart: 9, of which 5 were waited for; matrix products, arithmetic and copies ran while one was open for 1% of the time, Pallas kernels for 9%

profile of v2, /device:TPU:1, one launch (start us, length us, event | category | flops | bytes accessed | tf_op | source)
XLA Modules:
  0.0 92.1 jit_solution(15833036664942679618)
XLA Ops:
  0.6 2.1 %start.1 = (f32[16,16,128]{2,1,0:T(8,128)}, f32[8,10240]{1,0:T(8,128)}, f32[8,10240]{1,0:T(8,128)}) custom-call(f32[8,8]{1,0:T(8,128)} %w.1, f32[8,8192]{1,0:T(8,128)} %y.5, f32[8,8192]{1,0:T(8,128)} %v.5, f32[8,8192]{1,0:T(8,128)} %d.5), custom_call_target="tpu_custom_call" | custom-call | flops 31462400 | bytes 1573120 | tf_op jit(solution)/shard_map/start/pallas_call | solution.py:34
  2.7 8.8 %collective-permute-start = (f32[8,10240]{1,0:T(8,128)}, f32[8,10240]{1,0:T(8,128)S(1)}, u32[]{:S(2)}, u32[]{:S(2)}) collective-permute-start(f32[8,10240]{1,0:T(8,128)} %get-tuple-element.26), channel_id=1, source_target_pairs={{0,496},{16,0},{32,16},{48,32},{64,48},{80,64},{96,80},{112,96},{1... | collective-permute-start | bytes 983048 | tf_op jit(solution)/shard_map/ppermute | solution.py:19
  11.5 5.8 %all-to-all-start = ((f32[16,16,128]{2,1,0:T(8,128)}), f32[16,16,128]{2,1,0:T(8,128)S(1)}, u32[]{:S(2)}, u32[]{:S(2)}) async-start(f32[16,16,128]{2,1,0:T(8,128)} %get-tuple-element.25), calls=%async_computation | async-start | bytes 262144 | tf_op jit(solution)/shard_map/all_to_all | solution.py:23
  17.3 7.2 %collective-permute-start.3 = (f32[8,10240]{1,0:T(8,128)}, f32[8,10240]{1,0:T(8,128)S(1)}, u32[]{:S(2)}, u32[]{:S(2)}) collective-permute-start(f32[8,10240]{1,0:T(8,128)} %get-tuple-element.33), channel_id=1, source_target_pairs={{0,496},{16,0},{32,16},{48,32},{64,48},{80,64},{96,80},{112,96},{1... | collective-permute-start | bytes 983048 | tf_op jit(solution)/shard_map/ppermute | solution.py:19
  24.5 1.7 %all-to-all-done.gathered = f32[16,16,128]{2,1,0:T(8,128)S(1)} async-done(((f32[16,16,128]{2,1,0:T(8,128)}), f32[16,16,128]{2,1,0:T(8,128)S(1)}, u32[]{:S(2)}, u32[]{:S(2)}) %all-to-all-start) | async-done | bytes 131104 | tf_op jit(solution)/shard_map/all_to_all | solution.py:23
  26.1 0.0 collective-permute-done.y_next
  26.1 0.6 copy-done.15
  26.8 0.1 copy-done.3
  26.9 3.2 %first.1 = (f32[8,8192]{1,0:T(8,128)}, f32[8,9216]{1,0:T(8,128)}, f32[8,8192]{1,0:T(8,128)}, f32[16,8,128]{2,1,0:T(8,128)}, f32[8,128]{1,0:T(8,128)}, /*index=5*/f32[8,128]{1,0:T(8,128)}) custom-call(s32[2]{0:T(128)} %refs_0_.1, s32[64]{0:T(128)} %lags.5, f32[16,16,128]{2,1,0:T(8,128)} %copy-done.15, f32[8,8192]{1,0:T(8,128)} %x.1, f32[8,8192]{1,0:T(8,128)} %y.5, ...), custom_call_target="tpu_custom_call" | custom-call | flops 50713760 | bytes 2535688 | tf_op jit(solution)/shard_map/first/pallas_call | solution.py:34
  30.1 6.0 %collective-permute-start.1 = (f32[8,9216]{1,0:T(8,128)}, f32[8,9216]{1,0:T(8,128)S(1)}, u32[]{:S(2)}, u32[]{:S(2)}) collective-permute-start(f32[8,9216]{1,0:T(8,128)} %get-tuple-element.31.bar), channel_id=1, source_target_pairs={{0,16},{16,32},{32,48},{48,64},{64,80},{80,96},{96,112},{112,128},... | collective-permute-start | bytes 884744 | tf_op jit(solution)/shard_map/ppermute | solution.py:19
  36.2 4.8 %collective-permute-start.2 = (f32[8,8192]{1,0:T(8,128)}, f32[8,8192]{1,0:T(8,128)S(1)}, u32[]{:S(2)}, u32[]{:S(2)}) collective-permute-start(f32[8,8192]{1,0:T(8,128)} %get-tuple-element.32), channel_id=1, source_target_pairs={{0,496},{16,0},{32,16},{48,32},{64,48},{80,64},{96,80},{112,96},{1... | collective-permute-start | bytes 786440 | tf_op jit(solution)/shard_map/ppermute | solution.py:19
  41.0 0.0 copy-start.7
  41.0 0.0 copy-start.12
  41.0 0.0 copy-start.13
  41.0 4.3 %all-to-all-start.1 = ((f32[16,8,128]{2,1,0:T(8,128)}), f32[16,8,128]{2,1,0:T(8,128)S(1)}, u32[]{:S(2)}, u32[]{:S(2)}) async-start(f32[16,8,128]{2,1,0:T(8,128)} %get-tuple-element.27), calls=%async_computation.1 | async-start | bytes 131072 | tf_op jit(solution)/shard_map/all_to_all | solution.py:23
  45.3 0.0 collective-permute-done.3.v_next
  45.3 1.8 %collective-permute-done.2.after = f32[8,8192]{1,0:T(8,128)S(1)} collective-permute-done((f32[8,8192]{1,0:T(8,128)}, f32[8,8192]{1,0:T(8,128)S(1)}, u32[]{:S(2)}, u32[]{:S(2)}) %collective-permute-start.2) | collective-permute-done | bytes 262176 | tf_op jit(solution)/shard_map/ppermute | solution.py:19
  47.2 0.0 collective-permute-done.1.bar_prev
  47.2 0.0 copy-done
  47.2 0.0 copy-done.1
  47.2 0.0 copy-done.2
  47.2 0.0 copy-done.7
  47.2 0.0 copy-done.12
  47.2 0.0 copy-done.13
  47.2 0.0 copy-start.4
  47.2 1.0 %copy-done.4 = f32[8,10240]{1,0:T(8,128)S(1)} copy-done((f32[8,10240]{1,0:T(8,128)S(1)}, f32[8,10240]{1,0:T(8,128)}, u32[]{:S(2)}) %copy-start.4) | copy-done | bytes 327704
  48.2 1.0 %copy-done.5 = f32[8,9216]{1,0:T(8,128)S(1)} copy-done((f32[8,9216]{1,0:T(8,128)S(1)}, f32[8,9216]{1,0:T(8,128)}, u32[]{:S(2)}) %copy-start.5) | copy-done | bytes 294936
  49.2 2.1 %middle.1 = (f32[8,8192]{1,0:T(8,128)}, f32[8,8192]{1,0:T(8,128)S(1)}, f32[8,8192]{1,0:T(8,128)S(1)}, f32[1,128]{1,0:T(1,128)S(1)}) custom-call(s32[2]{0:T(128)S(1)} %copy-done.12, s32[64]{0:T(128)S(1)} %copy-done.13, f32[8,9216]{1,0:T(8,128)S(1)} %copy-done.5, f32[8,9216]{1,0:T(8,128)S(1)} %collective-permute-done.1.bar_prev, ...), custom_call_target="tpu_custom_call" | custom-call | flops 62274720 | bytes 3113736 | tf_op jit(solution)/shard_map/middle/pallas_call | solution.py:34
  51.2 1.5 %all-to-all-done.1.sums = f32[16,8,128]{2,1,0:T(8,128)S(1)} async-done(((f32[16,8,128]{2,1,0:T(8,128)}), f32[16,8,128]{2,1,0:T(8,128)S(1)}, u32[]{:S(2)}, u32[]{:S(2)}) %all-to-all-start.1) | async-done | bytes 65568 | tf_op jit(solution)/shard_map/all_to_all | solution.py:23
  52.7 0.0 copy-done.6
  52.7 0.0 copy-done.8
  52.7 0.0 copy-done.9
  52.7 0.0 copy-done.10
  52.7 0.7 copy-done.14
  53.4 0.0 copy-done.11
  53.4 2.1 %second.1 = (f32[8,8192]{1,0:T(8,128)}, f32[8,8192]{1,0:T(8,128)S(1)}, f32[16,16,128]{2,1,0:T(8,128)}, f32[8,128]{1,0:T(8,128)S(1)}, f32[1,128]{1,0:T(1,128)S(1)}) custom-call(s32[2]{0:T(128)S(1)} %copy-done.12, f32[16,8,128]{2,1,0:T(8,128)S(1)} %all-to-all-done.1.sums, f32[8,128]{1,0:T(8,128)S(1)} %copy-done.14, f32[8,128]{1,0:T(8,128)S(1)} %copy-done.11, ...), custom_call_target="tpu_custom_call" | custom-call | flops 32379040 | bytes 1618952 | tf_op jit(solution)/shard_map/second/pallas_call | solution.py:34
  55.5 4.3 %all-to-all-start.2 = ((f32[16,16,128]{2,1,0:T(8,128)}), f32[16,16,128]{2,1,0:T(8,128)S(1)}, u32[]{:S(2)}, u32[]{:S(2)}) async-start(f32[16,16,128]{2,1,0:T(8,128)} %get-tuple-element.40), calls=%async_computation.2 | async-start | bytes 262144 | tf_op jit(solution)/shard_map/all_to_all | solution.py:23
  59.8 2.5 %collective-permute-start.4 = (f32[8,8192]{1,0:T(8,128)S(1)}, f32[8,8192]{1,0:T(8,128)S(1)}, u32[]{:S(2)}, u32[]{:S(2)}) collective-permute-start(f32[8,8192]{1,0:T(8,128)S(1)} %get-tuple-element.39.dual), channel_id=1, source_target_pairs={{0,16},{16,32},{32,48},{48,64},{64,80},{80,96},{96,112},{112,128},... | collective-permute-start | bytes 786440 | tf_op jit(solution)/shard_map/ppermute | solution.py:19
  62.3 4.9 %all-to-all-done.2.refs_1_ = f32[16,16,128]{2,1,0:T(8,128)S(1)} async-done(((f32[16,16,128]{2,1,0:T(8,128)}), f32[16,16,128]{2,1,0:T(8,128)S(1)}, u32[]{:S(2)}, u32[]{:S(2)}) %all-to-all-start.2) | async-done | bytes 131104 | tf_op jit(solution)/shard_map/all_to_all | solution.py:23
  67.2 1.2 %third.1 = (f32[8,128]{1,0:T(8,128)S(1)}, f32[32,8,128]{2,1,0:T(8,128)}) custom-call(s32[2]{0:T(128)S(1)} %copy-done.12, f32[16,16,128]{2,1,0:T(8,128)S(1)} %all-to-all-done.2.refs_1_, f32[8,128]{1,0:T(8,128)S(1)} %get-tuple-element.41.refs_2_, f32[8,128]{1,0:T(8,128)S(1)} %copy-done.11, f32[1,128]{1,0:T(1,128)S(1)} %get-tuple-element.42.refs_4_), custom_call_target="tpu_custom_call" | custom-call | flops 5499040 | bytes 274952 | tf_op jit(solution)/shard_map/third/pallas_call | solution.py:34
  68.4 12.2 %all-to-all-start.3 = ((f32[32,8,128]{2,1,0:T(8,128)}), f32[32,8,128]{2,1,0:T(8,128)S(1)}, u32[]{:S(2)}, u32[]{:S(2)}) async-start(f32[32,8,128]{2,1,0:T(8,128)} %get-tuple-element.44), calls=%async_computation.3 | async-start | bytes 262144 | tf_op jit(solution)/shard_map/all_to_all | solution.py:23
  80.6 0.7 constant_dynamic-slice_fusion
  81.3 0.0 collective-permute-done.4.dual_prev
  81.3 1.3 %unshift.1 = f32[8,8192]{1,0:T(8,128)} custom-call(s32[64]{0:T(128)S(1)} %copy-done.13, f32[8,8192]{1,0:T(8,128)S(1)} %get-tuple-element.39.dual, f32[8,8192]{1,0:T(8,128)S(1)} %collective-permute-done.4.dual_prev), custom_call_target="tpu_custom_call" | custom-call | flops 15733760 | bytes 786688 | tf_op jit(solution)/shard_map/unshift/pallas_call | solution.py:34
  82.6 8.7 %all-to-all-done.3 = f32[32,8,128]{2,1,0:T(8,128)S(1)} async-done(((f32[32,8,128]{2,1,0:T(8,128)}), f32[32,8,128]{2,1,0:T(8,128)S(1)}, u32[]{:S(2)}, u32[]{:S(2)}) %all-to-all-start.3) | async-done | bytes 131104 | tf_op jit(solution)/shard_map/all_to_all | solution.py:23
  91.3 0.1 slice_reduce_fusion
  91.5 0.0 copy-done.16
  91.5 0.6 reshape.29
  (14 shorter events, 0.0 us)
Async XLA Ops:
  2.7 23.4 %collective-permute-start = (f32[8,10240]{1,0:T(8,128)}, f32[8,10240]{1,0:T(8,128)S(1)}, u32[]{:S(2)}, u32[]{:S(2)}) collective-permute-start(f32[8,10240]{1,0:T(8,128)} %get-tuple-element.26), channel_id=1, source_target_pairs={{0,496},{16,0},{32,16},{48,32},{64,48},{80,64},{96,80},{112,96},{1... | collective-permute-start | bytes 983048 | tf_op jit(solution)/shard_map/ppermute | solution.py:19
  11.5 14.6 %all-to-all-start = ((f32[16,16,128]{2,1,0:T(8,128)}), f32[16,16,128]{2,1,0:T(8,128)S(1)}, u32[]{:S(2)}, u32[]{:S(2)}) async-start(f32[16,16,128]{2,1,0:T(8,128)} %get-tuple-element.25), calls=%async_computation | async-start | bytes 262144 | tf_op jit(solution)/shard_map/all_to_all | solution.py:23
  17.3 28.0 %collective-permute-start.3 = (f32[8,10240]{1,0:T(8,128)}, f32[8,10240]{1,0:T(8,128)S(1)}, u32[]{:S(2)}, u32[]{:S(2)}) collective-permute-start(f32[8,10240]{1,0:T(8,128)} %get-tuple-element.33), channel_id=1, source_target_pairs={{0,496},{16,0},{32,16},{48,32},{64,48},{80,64},{96,80},{112,96},{1... | collective-permute-start | bytes 983048 | tf_op jit(solution)/shard_map/ppermute | solution.py:19
  26.1 0.7 copy-start.15
  26.1 0.8 copy-start.3
  26.9 20.3 %copy-start = (f32[8,8192]{1,0:T(8,128)S(1)}, f32[8,8192]{1,0:T(8,128)}, u32[]{:S(2)}) copy-start(f32[8,8192]{1,0:T(8,128)} %y.5) | copy-start | bytes 786436
  26.9 20.3 %copy-start.1 = (f32[8,8192]{1,0:T(8,128)S(1)}, f32[8,8192]{1,0:T(8,128)}, u32[]{:S(2)}) copy-start(f32[8,8192]{1,0:T(8,128)} %v.5) | copy-start | bytes 786436
  26.9 20.3 %copy-start.2 = (f32[8,8192]{1,0:T(8,128)S(1)}, f32[8,8192]{1,0:T(8,128)}, u32[]{:S(2)}) copy-start(f32[8,8192]{1,0:T(8,128)} %d.5) | copy-start | bytes 786436
  30.1 17.0 %collective-permute-start.1 = (f32[8,9216]{1,0:T(8,128)}, f32[8,9216]{1,0:T(8,128)S(1)}, u32[]{:S(2)}, u32[]{:S(2)}) collective-permute-start(f32[8,9216]{1,0:T(8,128)} %get-tuple-element.31.bar), channel_id=1, source_target_pairs={{0,16},{16,32},{32,48},{48,64},{64,80},{80,96},{96,112},{112,128},... | collective-permute-start | bytes 884744 | tf_op jit(solution)/shard_map/ppermute | solution.py:19
  36.2 11.0 %collective-permute-start.2 = (f32[8,8192]{1,0:T(8,128)}, f32[8,8192]{1,0:T(8,128)S(1)}, u32[]{:S(2)}, u32[]{:S(2)}) collective-permute-start(f32[8,8192]{1,0:T(8,128)} %get-tuple-element.32), channel_id=1, source_target_pairs={{0,496},{16,0},{32,16},{48,32},{64,48},{80,64},{96,80},{112,96},{1... | collective-permute-start | bytes 786440 | tf_op jit(solution)/shard_map/ppermute | solution.py:19
  41.0 6.2 %copy-start.7 = (f32[8192]{0:T(1024)S(1)}, f32[8192]{0:T(1024)}, u32[]{:S(2)}) copy-start(f32[8192]{0:T(1024)} %param.19) | copy-start | bytes 98308
  41.0 6.2 %copy-start.12 = (s32[2]{0:T(128)S(1)}, s32[2]{0:T(128)}, u32[]{:S(2)}) copy-start(s32[2]{0:T(128)} %refs_0_.1) | copy-start | bytes 28
  41.0 6.2 %copy-start.13 = (s32[64]{0:T(128)S(1)}, s32[64]{0:T(128)}, u32[]{:S(2)}) copy-start(s32[64]{0:T(128)} %lags.5) | copy-start | bytes 772
  41.0 11.6 %all-to-all-start.1 = ((f32[16,8,128]{2,1,0:T(8,128)}), f32[16,8,128]{2,1,0:T(8,128)S(1)}, u32[]{:S(2)}, u32[]{:S(2)}) async-start(f32[16,8,128]{2,1,0:T(8,128)} %get-tuple-element.27), calls=%async_computation.1 | async-start | bytes 131072 | tf_op jit(solution)/shard_map/all_to_all | solution.py:23
  47.2 1.0 %copy-start.4 = (f32[8,10240]{1,0:T(8,128)S(1)}, f32[8,10240]{1,0:T(8,128)}, u32[]{:S(2)}) copy-start(f32[8,10240]{1,0:T(8,128)} %copy-done.3) | copy-start | bytes 983044
  48.2 1.0 %copy-start.5 = (f32[8,9216]{1,0:T(8,128)S(1)}, f32[8,9216]{1,0:T(8,128)}, u32[]{:S(2)}) copy-start(f32[8,9216]{1,0:T(8,128)} %get-tuple-element.31.bar) | copy-start | bytes 884740
  49.1 3.5 %copy-start.6 = (f32[8,8192]{1,0:T(8,128)S(1)}, f32[8,8192]{1,0:T(8,128)}, u32[]{:S(2)}) copy-start(f32[8,8192]{1,0:T(8,128)} %get-tuple-element.30.x) | copy-start | bytes 786436
  49.1 3.5 %copy-start.8 = (f32[8192]{0:T(1024)S(1)}, f32[8192]{0:T(1024)}, u32[]{:S(2)}) copy-start(f32[8192]{0:T(1024)} %param.18) | copy-start | bytes 98308
  49.2 3.6 %copy-start.9 = (f32[8192]{0:T(1024)S(1)}, f32[8192]{0:T(1024)}, u32[]{:S(2)}) copy-start(f32[8192]{0:T(1024)} %param.20) | copy-start | bytes 98308
  49.2 3.6 %copy-start.10 = (s32[8192]{0:T(1024)S(1)}, s32[8192]{0:T(1024)}, u32[]{:S(2)}) copy-start(s32[8192]{0:T(1024)} %param.23) | copy-start | bytes 98308
  52.7 0.7 copy-start.14
  52.7 0.7 copy-start.11
  55.5 11.7 %all-to-all-start.2 = ((f32[16,16,128]{2,1,0:T(8,128)}), f32[16,16,128]{2,1,0:T(8,128)S(1)}, u32[]{:S(2)}, u32[]{:S(2)}) async-start(f32[16,16,128]{2,1,0:T(8,128)} %get-tuple-element.40), calls=%async_computation.2 | async-start | bytes 262144 | tf_op jit(solution)/shard_map/all_to_all | solution.py:23
  59.8 21.5 %collective-permute-start.4 = (f32[8,8192]{1,0:T(8,128)S(1)}, f32[8,8192]{1,0:T(8,128)S(1)}, u32[]{:S(2)}, u32[]{:S(2)}) collective-permute-start(f32[8,8192]{1,0:T(8,128)S(1)} %get-tuple-element.39.dual), channel_id=1, source_target_pairs={{0,16},{16,32},{32,48},{48,64},{64,80},{80,96},{96,112},{112,128},... | collective-permute-start | bytes 786440 | tf_op jit(solution)/shard_map/ppermute | solution.py:19
  68.4 22.9 %all-to-all-start.3 = ((f32[32,8,128]{2,1,0:T(8,128)}), f32[32,8,128]{2,1,0:T(8,128)S(1)}, u32[]{:S(2)}, u32[]{:S(2)}) async-start(f32[32,8,128]{2,1,0:T(8,128)} %get-tuple-element.44), calls=%async_computation.3 | async-start | bytes 262144 | tf_op jit(solution)/shard_map/all_to_all | solution.py:23
  82.6 8.9 %copy-start.16 = (f32[4]{0:T(128)S(1)}, f32[4]{0:T(128)}, u32[]{:S(2)}) copy-start(f32[4]{0:T(128)} %constant.14.clone) | copy-start | bytes 52

commit v3 on v2

--- a/solution.py
+++ b/solution.py
@@ -1,3 +1,5 @@
+import math
+
 import jax
 import jax.numpy as jnp
 from jax import lax
@@ -19,6 +21,12 @@
     return lax.ppermute(value, axis, [(i, (i + steps) % count) for i in range(count)])
 
 
+def swapped(value, axis, first):
+    count = lax.axis_size(axis)
+    pairs = [(i, (i + 1 if (i - first) % 2 == 0 else i - 1) % count) for i in range(count)]
+    return lax.ppermute(value, axis, pairs)
+
+
 def spread(value, axis):
     return lax.all_to_all(value, axis, 0, 0, tiled=True)
 
@@ -27,15 +35,18 @@
     return jax.ShapeDtypeStruct(dims, F32)
 
 
-def call(kernel, out_shape, operands, smem=0, out_specs=None, name=None, grant=16):
-    size = sum(o.size * 4 for o in operands)
+def near(*dims, dtype=F32):
+    return pltpu.VMEM(dims, dtype)
+
+
+def call(kernel, out_shape, operands, smem=0, name=None, grant=16):
     outs = out_shape if isinstance(out_shape, tuple) else (out_shape,)
-    size += sum(o.size * 4 for o in outs)
+    size = sum(4 * math.prod(o.shape) for o in (*operands, *outs))
     return pl.pallas_call(
         kernel,
         out_shape=out_shape,
         in_specs=[SMEM] * smem + [VMEM] * (len(operands) - smem),
-        out_specs=out_specs if out_specs is not None else jax.tree.map(lambda _: VMEM, out_shape),
+        out_specs=(VMEM,) * len(out_shape) if isinstance(out_shape, tuple) else VMEM,
         cost_estimate=pl.CostEstimate(flops=20 * size, bytes_accessed=size, transcendentals=0),
         name=name,
         compiler_params=pltpu.CompilerParams(vmem_limit_bytes=grant * 2**20),
@@ -102,32 +113,61 @@
     return slice(index // each, index // each + 1), slice(start, start + BLOCK)
 
 
-def start_kernel(w, y, v, d, payload, sent, stock):
+def start_kernel(w, y, v, d, payload, sent):
     width = y.shape[1]
     each = w.shape[1]
     payload[:, 0:ROWS, 0:each] = jnp.broadcast_to(w[...][None], (payload.shape[0], ROWS, each))
     sent[:, 0:width] = y[...]
-    stock[:, 0:width] = v[...]
     for i, at in blocks(width):
         sent[extra_slot(i, width, 0)] = v[0:1, at]
         sent[extra_slot(i, width, 1)] = d[0:1, at]
-        stock[extra_slot(i, width, 0)] = d[0:1, at]
-        stock[extra_slot(i, width, 1)] = d[1:2, at]
+
+
+def stage(scalars, v, d, others):
+    operands = (*scalars, v, d, *others)
+    count, at_v = len(operands), len(scalars)
+
+    def kernel(*refs):
+        outs, sent, sems = refs[count : 2 * count], refs[2 * count], refs[2 * count + 1]
+        copies = [pltpu.make_async_copy(refs[i], outs[i], sems.at[i]) for i in range(count)]
+        for copy in copies:
+            copy.start()
+        for copy in copies:
+            copy.wait()
+        v, d = outs[at_v], outs[at_v + 1]
+        width = v.shape[1]
+        sent[:, 0:width] = v[...]
+        for i, at in blocks(width):
+            sent[extra_slot(i, width, 0)] = d[0:1, at]
+            sent[extra_slot(i, width, 1)] = d[1:2, at]
+
+    width = v.shape[1]
+    return pl.pallas_call(
+        kernel,
+        out_shape=tuple(pltpu.SMEM(o.shape, o.dtype) for o in scalars)
+        + tuple(near(*o.shape, dtype=o.dtype) for o in operands[at_v:])
+        + (near(ROWS, width + 2 * (width // ROWS)),),
+        in_specs=[pl.BlockSpec(memory_space=pltpu.HBM)] * count,
+        out_specs=(SMEM,) * at_v + (VMEM,) * (count - at_v + 1),
+        scratch_shapes=[pltpu.SemaphoreType.DMA((count,))],
+        name="stage",
+        compiler_params=pltpu.CompilerParams(vmem_limit_bytes=16 * 2**20),
+    )(*(pltpu.with_memory_space_constraint(o, pltpu.HBM) for o in operands))
 
 
 def first_kernel(
-    codes, lags, gathered, x, y, y_next, v, d, cost, holding, load, plants, cap,
-    x1, up, down, loads, prices, limits,
+    codes, lags, gathered, x, y, y_next, v, d, cost, holding, load, plants,
+    x1, inner, outer, loads, prices,
 ):
     primal = step_size(codes, 0)
     rows = row_ids()
     plant_ids = lax.broadcasted_iota(jnp.int32, (P_SIZE, BLOCK), 0)
+    odd = codes[2] == 1
     width = x.shape[1]
     each = P_SIZE // gathered.shape[0]
     for j in range(gathered.shape[0]):
         prices[:, j * each : (j + 1) * each] = gathered[j, 0:ROWS, 0:each]
     w = prices[...]
-    limits[...] = cap[...]
     total = jnp.zeros((P_SIZE, 3 * ROWS), F32)
     for i, at in blocks(width):
         lag = lags[i]
@@ -143,20 +183,23 @@
         d8 = y_next[extra_slot(i, width, 1)]
         bar7 = 2.0 * stock_step(v7, holding[:, at], y[7:8, at], yb[0:1], primal) - v7
         bar8 = 2.0 * stock_step(v8, holding[:, at], yb[0:1], yb[1:2], primal) - v8
-        up[:, at] = over
-        up[extra_slot(i, width, 0)] = bar7
         first_row = over[0:1] + jnp.where(lag == LAGMAX, -d8 - bar8 + bar7, 0.0)
-        down[:, at] = jnp.where(rows == 0, first_row, jnp.where(rows == 1, yb[0:1], d[:, at]))
+        down = jnp.where(rows == 0, first_row, jnp.where(rows == 1, yb[0:1], d[:, at]))
+        inner[:, at] = jnp.where(odd, down, over)
+        outer[:, at] = jnp.where(odd, over, down)
+        inner[extra_slot(i, width, 0)] = bar7
+        outer[extra_slot(i, width, 0)] = bar7
     loads[...] = jnp.broadcast_to(folded(total)[None], loads.shape)
 
 
 def middle_kernel(
-    codes, lags, bar, bar_prev, after, y, y_next, v, v_next, d, holding,
-    v2, dual_x, field_x, squares,
+    codes, lags, x, x1, inner, outer, y, y_next, v, v_next, d, holding,
+    v2, dual_x, field_x,
 ):
     primal = step_size(codes, 0)
     dual_step = step_size(codes, 1)
     rows = row_ids()
+    odd = codes[2] == 1
     width = v.shape[1]
     square = jnp.zeros((ROWS, BLOCK), F32)
     for i, at in blocks(width):
@@ -164,12 +207,15 @@
         cost = holding[:, at]
         ya, yb = y[:, at], y_next[:, at]
         va, vb = v[:, at], v_next[:, at]
-        da, mixed = d[:, at], after[:, at]
+        pair = inner[:, at], outer[:, at]
+        bar_prev, mixed = jnp.where(odd, *pair), jnp.where(odd, *pair[::-1])
+        da = d[:, at]
         d8, d9 = v_next[extra_slot(i, width, 0)], v_next[extra_slot(i, width, 1)]
         bar8, y16 = mixed[0:1], mixed[1:2]
         db = jnp.where(rows == 0, d8, jnp.where(rows == 1, d9, mixed))
-        bar_before = bar_prev[extra_slot(i, width, 0)]
-        over = bar[:, at]
+        slot = extra_slot(i, width, 0)
+        bar_before = jnp.where(odd, inner[slot], outer[slot])
+        over = 2.0 * x1[:, at] - x[:, at]
         va1 = stock_step(va, cost, ya, row_after(ya, yb[0:1], rows), primal)
         vb1 = stock_step(vb, cost, yb, row_after(yb, y16, rows), primal)
         va_bar = 2.0 * va1 - va
@@ -180,7 +226,7 @@
         square += misfit * misfit
         yx = ahead(ya, yb, lag, rows) + dual_step * misfit
         dual_x[:, at] = yx
-        ya1 = ya + dual_step * (ha + past(over, bar_prev[:, at], lag, rows))
+        ya1 = ya + dual_step * (ha + past(over, bar_prev, lag, rows))
         y8 = yb[0:1] + dual_step * (hb[0:1] + pltpu.roll(over, lag & (ROWS - 1), 0)[0:1])
         va2 = stock_step(va1, cost, ya1, row_after(ya1, y8, rows), primal)
         v2[:, at] = va2
@@ -194,11 +240,11 @@
         vx_bar = 2.0 * vx2 - vx1
         dx = ahead(da, db, lag, rows)
         field_x[:, at] = -dx - vx_bar + row_before(vx_bar, start_bar, rows)
-    squares[...] = jnp.sum(square, axis=0, keepdims=True)
+    field_x[:, width : width + BLOCK] = square
 
 
 def second_kernel(
-    codes, sums, prices, cap, x, dual, field, squares, cost, load, plants,
+    codes, sums, prices, cap, x, dual, field, cost, load, plants,
     x2, dual_x, loads, prices_new, excess_row,
 ):
     primal = step_size(codes, 0)
@@ -223,7 +269,8 @@
         square += misfit * misfit
         total += load_terms(over * load[:, at], plants[:, at], plant_ids)
     count = loads.shape[0]
-    lines = jnp.concatenate([squares[...], jnp.sum(square, axis=0, keepdims=True)] * 4, 0)
+    pair = (field[:, x.shape[1] :], square)
+    lines = jnp.concatenate([jnp.sum(p, axis=0, keepdims=True) for p in pair] * 4, 0)
     loads[:, 0:8, :] = jnp.broadcast_to(folded(total)[None], (count, ROWS, P_SIZE))
     loads[:, 8:16, :] = jnp.broadcast_to(lines[None], (count, ROWS, P_SIZE))
 
@@ -235,8 +282,9 @@
     price_out[...] = jnp.maximum(prices[...] + plant_step * excess, 0.0)
     above = jnp.maximum(excess, 0.0)
     above_row = jnp.sum(above * above, axis=0, keepdims=True)
-    packed = jnp.concatenate([totals[8:9], excess_row[...], totals[9:10], above_row] * 2, 0)
-    out[...] = jnp.broadcast_to(packed[None], out.shape)
+    for k, rows in enumerate(((totals[8:9], excess_row[...]), (totals[9:10], above_row))):
+        pair = jnp.concatenate(rows, 0)
+        out[:, k] = jnp.broadcast_to(pair[None], (out.shape[0],) + pair.shape)
 
 
 def unshift_kernel(lags, dual, dual_prev, y):
@@ -271,52 +319,55 @@
     plant_row = plants.reshape(1, width)
 
     longer = width + 2 * (width // ROWS)
-    payload, y_sent, v_sent = call(
+    payload, y_sent = call(
         start_kernel,
-        (shape(skus, 2 * ROWS, P_SIZE), shape(ROWS, longer), shape(ROWS, longer)),
+        (shape(skus, 2 * ROWS, P_SIZE), shape(ROWS, longer)),
         (plant_dual, balance_dual, stock_v, demand),
         name="start",
         grant=60,
     )
+    y_next = shifted(y_sent, "tm", -1)
+    payload, codes, lags, v, d, *held = lax.optimization_barrier(
+        (
+            payload, step_codes, lags, stock_v, demand, primal_x, balance_dual, cost, holding,
+            load, plant_row, capacity,
+        )
+    )
+    parity = lax.axis_index("tm") % 2
+    codes = jnp.concatenate([codes, parity.astype(jnp.int32)[None]])
+    codes, lags, v, d, x, y, cost, holding, load, plant_row, limits, v_sent = stage(
+        (codes, lags), v, d, held
+    )
+    v_next = shifted(v_sent, "tm", -1)
     gathered = spread(payload, "sku")
-    y_next = shifted(y_sent, "tm", -1)
-    v_next = shifted(v_sent, "tm", -1)
-
-    x1, up, down, loads1, prices0, limits = call(
+    x1, inner, outer, loads1, prices0 = call(
         first_kernel,
         (
-            shape(ROWS, width), shape(ROWS, width + width // ROWS), shape(ROWS, width),
-            shape(skus, ROWS, P_SIZE), shape(ROWS, P_SIZE), shape(ROWS, P_SIZE),
+            near(ROWS, width), near(ROWS, width + width // ROWS),
+            near(ROWS, width + width // ROWS), shape(skus, ROWS, P_SIZE), near(ROWS, P_SIZE),
         ),
-        (
-            step_codes, lags, gathered, primal_x, balance_dual, y_next, stock_v, demand, cost,
-            holding, load, plant_row, capacity,
-        ),
+        (codes, lags, gathered, x, y, y_next, v, d, cost, holding, load, plant_row),
         smem=2,
         name="first",
-        grant=60,
-    )
-    bar_prev = shifted(up, "tm", 1)
-    after = shifted(down, "tm", -1)
+    )
+    inner = swapped(inner, "tm", 0)
+    outer = swapped(outer, "tm", 1)
     sums1 = spread(loads1, "sku")
-    v2, dual_x, field_x, squares = call(
+    v2, dual_x, field_x = call(
         middle_kernel,
-        (shape(ROWS, width),) * 3 + (shape(1, BLOCK),),
-        (
-            step_codes, lags, up, bar_prev, after, balance_dual, y_next, stock_v, v_next, demand,
-            holding,
-        ),
+        (near(ROWS, width), near(ROWS, width), near(ROWS, width + BLOCK)),
+        (codes, lags, x, x1, inner, outer, y, y_next, v, v_next, d, holding),
         smem=2,
         name="middle",
     )
     x2, dual_x2, loads2, prices1, above1 = call(
         second_kernel,
         (
-            shape(ROWS, width), shape(ROWS, width), shape(skus, 2 * ROWS, P_SIZE),
-            shape(ROWS, P_SIZE), shape(1, P_SIZE),
+            near(ROWS, width), near(ROWS, width), shape(skus, 2 * ROWS, P_SIZE),
+            near(ROWS, P_SIZE), near(1, P_SIZE),
         ),
         (
-            step_codes, sums1, prices0, limits, x1, dual_x, field_x, squares, cost, load,
+            codes, sums1, prices0, limits, x1, dual_x, field_x, cost, load,
             plant_row,
         ),
         smem=1,
@@ -330,17 +381,17 @@
 
     prices2, packed = call(
         third,
-        (shape(ROWS, P_SIZE), shape(times, ROWS, P_SIZE)),
-        (step_codes, sums2, prices1, limits, above1),
+        (near(ROWS, P_SIZE), shape(times, 2, 2, P_SIZE)),
+        (codes, sums2, prices1, limits, above1),
         smem=1,
         name="third",
     )
     portion = lax.dynamic_slice_in_dim(prices2, owner, each, 1)
-    totals = jnp.sum(spread(packed, "tm")[:, 0:4], axis=(0, 2))
+    totals = jnp.sum(spread(packed, "tm"), axis=(0, 3))
     scale = P_SIZE / total_skus
     cells, cap_rows = ROWS * times * total_skus, ROWS * times * P_SIZE
-    factors = jnp.array([1.0 / cells, scale * scale / cap_rows] * 2, F32)
-    residuals = (totals * factors).reshape(2, 2)
+    column = lax.broadcasted_iota(jnp.int32, totals.shape, 1)
+    residuals = totals * jnp.where(column == 0, 1.0 / cells, scale * scale / cap_rows)
     next_y = call(
         unshift_kernel, shape(ROWS, width), (lags, dual_x2, dual_prev), smem=1, name="unshift"
     )

time: 92.9 us -> 82.4 us (0.89)
  starting transfers between devices: 55.8 us -> 51 us
  Pallas kernels: 12 us -> 8.96 us
  local copies, waits for them, and re-layouts: 4.71 us -> 2.72 us
  waiting for transfers between devices: 18.6 us -> 17.1 us
  other arithmetic: 0.15 us -> 1.28 us
    ppermute x5 -> x3, starting transfers between devices: 29.3 us -> 20.5 us  [shifted(): lax.ppermute(value, axis, [(i, (i + steps) % count) for i in range(count)])]
    ppermute x0 -> x2, starting transfers between devices: none -> 7.82 us  [swapped(): return lax.ppermute(value, axis, pairs)]
    ppermute x0 -> x2, waiting for transfers between devices: none -> 5.99 us  [swapped(): return lax.ppermute(value, axis, pairs)]
    all_to_all x4, waiting for transfers between devices: 16.8 us -> 11.1 us  [spread(): return lax.all_to_all(value, axis, 0, 0, tiled=True)]
    pallas_call x6, Pallas kernels: 12 us -> 7.61 us  [call(): pl.pallas_call(kernel, out_shape=out_shape, in_specs=[SMEM] * smem + [VME...]
    all_to_all x4, starting transfers between devices: 26.5 us -> 22.6 us  [spread(): return lax.all_to_all(value, axis, 0, 0, tiled=True)]
    ppermute x5 -> x3, waiting for transfers between devices: 1.84 us -> 0.01 us  [shifted(): lax.ppermute(value, axis, [(i, (i + steps) % count) for i in range(count)])]
    pallas_call x0 -> x1, Pallas kernels: none -> 1.35 us  [stage(): pl.pallas_call(kernel, out_shape=tuple((pltpu.SMEM(o.shape, o.dtype) for...]
  transfers between devices with their start and end apart: 9 -> 9, of which waited for: 5 -> 4; matrix products, arithmetic and copies ran while one was open for 1% -> 3% of each run, Pallas kernels for 9% -> 7%
where the time goes in v3:
time: 82.4 us; the launch traced here: 81.8 us
  starting transfers between devices  51 us (62%)
  waiting for transfers between devices  17.1 us (21%)
  Pallas kernels  8.96 us (11%)
  local copies, waits for them, and re-layouts  2.72 us (3%)
  other arithmetic  1.28 us (2%)
    all_to_all x4, starting transfers between devices, spread(): return lax.all_to_all(value, axis, 0, 0, tiled=True)  22.6 us
    ppermute x3, starting transfers between devices, shifted(): lax.ppermute(value, axis, [(i, (i + steps) % count) for i in range(count)])  20.5 us
    all_to_all x4, waiting for transfers between devices, spread(): return lax.all_to_all(value, axis, 0, 0, tiled=True)  11.1 us
    ppermute x2, starting transfers between devices, swapped(): return lax.ppermute(value, axis, pairs)  7.82 us
    pallas_call x6, Pallas kernels, call(): pl.pallas_call(kernel, out_shape=out_shape, in_specs=[SMEM] * smem + [VME...  7.61 us
    ppermute x2, waiting for transfers between devices, swapped(): return lax.ppermute(value, axis, pairs)  5.99 us
    unnamed x4, local copies, waits for them, and re-layouts  2.06 us
  transfers between devices with their start and end apart: 9, of which 4 were waited for; matrix products, arithmetic and copies ran while one was open for 3% of the time, Pallas kernels for 7%

profile of v3, /device:TPU:1, one launch (start us, length us, event | category | flops | bytes accessed | tf_op | source)
XLA Modules:
  0.0 81.8 jit_solution(14846930626236513781)
XLA Ops:
  0.6 1.9 %start.1 = (f32[16,16,128]{2,1,0:T(8,128)}, f32[8,10240]{1,0:T(8,128)}) custom-call(f32[8,8]{1,0:T(8,128)} %w.1, f32[8,8192]{1,0:T(8,128)} %refs_5_, f32[8,8192]{1,0:T(8,128)} %refs_2_, f32[8,8192]{1,0:T(8,128)} %refs_3_), custom_call_target="tpu_custom_call" | custom-call | flops 24908800 | bytes 1245440 | tf_op jit(solution)/shard_map/start/pallas_call | solution.py:45
  2.5 8.8 %collective-permute-start = (f32[8,10240]{1,0:T(8,128)}, f32[8,10240]{1,0:T(8,128)S(1)}, u32[]{:S(2)}, u32[]{:S(2)}) collective-permute-start(f32[8,10240]{1,0:T(8,128)} %get-tuple-element.63), channel_id=1, source_target_pairs={{0,496},{16,0},{32,16},{48,32},{64,48},{80,64},{96,80},{112,96},{1... | collective-permute-start | bytes 983048 | tf_op jit(solution)/shard_map/ppermute | solution.py:21
  11.3 5.8 %all-to-all-start = ((f32[16,16,128]{2,1,0:T(8,128)}), f32[16,16,128]{2,1,0:T(8,128)S(1)}, u32[]{:S(2)}, u32[]{:S(2)}) async-start(f32[16,16,128]{2,1,0:T(8,128)} %get-tuple-element.60), calls=%async_computation | async-start | bytes 262144 | tf_op jit(solution)/shard_map/all_to_all | solution.py:31
  17.1 0.0 copy-start
  17.1 0.6 copy-done
  17.8 0.6 pad_add_fusion.refs_0_
  18.4 1.4 %stage.1 = (s32[3]{0:T(128)S(4)}, s32[64]{0:T(128)S(4)}, f32[8,8192]{1,0:T(8,128)S(1)}, f32[8,8192]{1,0:T(8,128)S(1)}, f32[8,8192]{1,0:T(8,128)S(1)}, /*index=5*...) custom-call(s32[3]{0:T(128)} %pad_add_fusion.refs_0_, ...), custom_call_target="tpu_custom_call" | custom-call | tf_op jit(solution)/shard_map/stage/pallas_call | solution.py:145
  19.7 7.2 %collective-permute-start.3 = (f32[8,10240]{1,0:T(8,128)S(1)}, f32[8,10240]{1,0:T(8,128)S(1)}, u32[]{:S(2)}, u32[]{:S(2)}) collective-permute-start(f32[8,10240]{1,0:T(8,128)S(1)} %get-tuple-element.76), channel_id=1, source_target_pairs={{0,496},{16,0},{32,16},{48,32},{64,48},{80,64},{96,80},{112,96},{1... | collective-permute-start | bytes 983048 | tf_op jit(solution)/shard_map/ppermute | solution.py:21
  26.9 0.0 all-to-all-done.gathered
  26.9 0.0 collective-permute-done.y_next
  26.9 1.8 %first.1 = (f32[8,8192]{1,0:T(8,128)S(1)}, f32[8,9216]{1,0:T(8,128)}, f32[8,9216]{1,0:T(8,128)}, f32[16,8,128]{2,1,0:T(8,128)}, f32[8,128]{1,0:T(8,128)S(1)}) custom-call(s32[3]{0:T(128)S(4)} %get-tuple-element.58.codes.refs_0_, s32[64]{0:T(128)S(4)} %get-tuple-element.59.lags, f32[16,16,128]{2,1,0:T(8,128)S(1)} %all-to-all-done.gathered, ...), custom_call_target="tpu_custom_call" | custom-call | flops 51205360 | bytes 2560268 | tf_op jit(solution)/shard_map/first/pallas_call | solution.py:45
  28.7 5.9 %collective-permute-start.1 = (f32[8,9216]{1,0:T(8,128)}, f32[8,9216]{1,0:T(8,128)S(1)}, u32[]{:S(2)}, u32[]{:S(2)}) collective-permute-start(f32[8,9216]{1,0:T(8,128)} %get-tuple-element.74), channel_id=1, source_target_pairs={{0,16},{16,0},{32,48},{48,32},{64,80},{80,64},{96,112},{112,96},{1... | collective-permute-start | bytes 884744 | tf_op jit(solution)/shard_map/ppermute | solution.py:27
  34.7 1.9 %collective-permute-start.2 = (f32[8,9216]{1,0:T(8,128)}, f32[8,9216]{1,0:T(8,128)S(1)}, u32[]{:S(2)}, u32[]{:S(2)}) collective-permute-start(f32[8,9216]{1,0:T(8,128)} %get-tuple-element.75), channel_id=1, source_target_pairs={{0,496},{16,32},{32,16},{48,64},{64,48},{80,96},{96,80},{112,128},... | collective-permute-start | bytes 884744 | tf_op jit(solution)/shard_map/ppermute | solution.py:27
  36.6 3.9 %all-to-all-start.1 = ((f32[16,8,128]{2,1,0:T(8,128)}), f32[16,8,128]{2,1,0:T(8,128)S(1)}, u32[]{:S(2)}, u32[]{:S(2)}) async-start(f32[16,8,128]{2,1,0:T(8,128)} %get-tuple-element.70), calls=%async_computation.1 | async-start | bytes 131072 | tf_op jit(solution)/shard_map/all_to_all | solution.py:31
  40.5 0.0 collective-permute-done.3.v_next
  40.5 0.0 collective-permute-done.1.inner
  40.6 6.0 %collective-permute-done.2.outer = f32[8,9216]{1,0:T(8,128)S(1)} collective-permute-done((f32[8,9216]{1,0:T(8,128)}, f32[8,9216]{1,0:T(8,128)S(1)}, u32[]{:S(2)}, u32[]{:S(2)}) %collective-permute-start.2) | collective-permute-done | bytes 294944 | tf_op jit(solution)/shard_map/ppermute | solution.py:27
  46.5 0.9 %middle.1 = (f32[8,8192]{1,0:T(8,128)S(1)}, f32[8,8192]{1,0:T(8,128)S(1)}, f32[8,8320]{1,0:T(8,128)S(1)}) custom-call(s32[3]{0:T(128)S(4)} %get-tuple-element.58.codes.refs_0_, s32[64]{0:T(128)S(4)} %get-tuple-element.59.lags, f32[8,8192]{1,0:T(8,128)S(1)} %get-tuple-element.61.x, f32[8,8192]{1,0:T(8,128)S(1)} %get-tuple-element.73.x1.x, ...), custom_call_target="tpu_custom_call" | custom-call | flops 67589360 | bytes 3379468 | tf_op jit(solution)/shard_map/middle/pallas_call | solution.py:45
  47.4 1.1 %all-to-all-done.1.sums = f32[16,8,128]{2,1,0:T(8,128)S(1)} async-done(((f32[16,8,128]{2,1,0:T(8,128)}), f32[16,8,128]{2,1,0:T(8,128)S(1)}, u32[]{:S(2)}, u32[]{:S(2)}) %all-to-all-start.1) | async-done | bytes 65568 | tf_op jit(solution)/shard_map/all_to_all | solution.py:31
  48.6 1.6 %second.1 = (f32[8,8192]{1,0:T(8,128)S(1)}, f32[8,8192]{1,0:T(8,128)S(1)}, f32[16,16,128]{2,1,0:T(8,128)}, f32[8,128]{1,0:T(8,128)S(1)}, f32[1,128]{1,0:T(1,128)S(1)}) custom-call(s32[3]{0:T(128)S(4)} %get-tuple-element.58.codes.refs_0_, f32[16,8,128]{2,1,0:T(8,128)S(1)} %all-to-all-done.1.sums, f32[8,128]{1,0:T(8,128)S(1)} %get-tuple-element.71.prices, ...), custom_call_target="tpu_custom_call" | custom-call | flops 32450800 | bytes 1622540 | tf_op jit(solution)/shard_map/second/pallas_call | solution.py:45
  50.1 4.2 %all-to-all-start.2 = ((f32[16,16,128]{2,1,0:T(8,128)}), f32[16,16,128]{2,1,0:T(8,128)S(1)}, u32[]{:S(2)}, u32[]{:S(2)}) async-start(f32[16,16,128]{2,1,0:T(8,128)} %get-tuple-element.82), calls=%async_computation.2 | async-start | bytes 262144 | tf_op jit(solution)/shard_map/all_to_all | solution.py:31
  54.4 4.6 %collective-permute-start.4 = (f32[8,8192]{1,0:T(8,128)S(1)}, f32[8,8192]{1,0:T(8,128)S(1)}, u32[]{:S(2)}, u32[]{:S(2)}) collective-permute-start(f32[8,8192]{1,0:T(8,128)S(1)} %get-tuple-element.81.dual), channel_id=1, source_target_pairs={{0,16},{16,32},{32,48},{48,64},{64,80},{80,96},{96,112},{112,128},... | collective-permute-start | bytes 786440 | tf_op jit(solution)/shard_map/ppermute | solution.py:21
  59.0 2.9 %all-to-all-done.2.refs_1_ = f32[16,16,128]{2,1,0:T(8,128)S(1)} async-done(((f32[16,16,128]{2,1,0:T(8,128)}), f32[16,16,128]{2,1,0:T(8,128)S(1)}, u32[]{:S(2)}, u32[]{:S(2)}) %all-to-all-start.2) | async-done | bytes 131104 | tf_op jit(solution)/shard_map/all_to_all | solution.py:31
  61.9 0.7 third.1
  62.5 8.6 %all-to-all-start.3 = ((f32[32,2,2,128]{3,2,1,0:T(2,128)}), f32[32,2,2,128]{3,2,1,0:T(2,128)S(1)}, u32[]{:S(2)}, u32[]{:S(2)}) async-start(f32[32,2,2,128]{3,2,1,0:T(2,128)} %get-tuple-element.86), calls=%async_computation.3 | async-start | bytes 131072 | tf_op jit(solution)/shard_map/all_to_all | solution.py:31
  71.2 0.7 copy.17
  71.9 0.7 copy.18
  72.6 0.7 constant_dynamic-slice_fusion
  73.3 0.0 collective-permute-done.4.dual_prev
  73.3 0.8 unshift.1
  74.1 7.0 %all-to-all-done.3 = f32[32,2,2,128]{3,2,1,0:T(2,128)S(1)} async-done(((f32[32,2,2,128]{3,2,1,0:T(2,128)}), f32[32,2,2,128]{3,2,1,0:T(2,128)S(1)}, u32[]{:S(2)}, u32[]{:S(2)}) %all-to-all-start.3) | async-done | bytes 65568 | tf_op jit(solution)/shard_map/all_to_all | solution.py:31
  81.1 0.1 reduce_sum.9
  81.2 0.6 broadcast_multiply_fusion
  (1 shorter events, 0.0 us)
Async XLA Ops:
  2.5 24.4 %collective-permute-start = (f32[8,10240]{1,0:T(8,128)}, f32[8,10240]{1,0:T(8,128)S(1)}, u32[]{:S(2)}, u32[]{:S(2)}) collective-permute-start(f32[8,10240]{1,0:T(8,128)} %get-tuple-element.63), channel_id=1, source_target_pairs={{0,496},{16,0},{32,16},{48,32},{64,48},{80,64},{96,80},{112,96},{1... | collective-permute-start | bytes 983048 | tf_op jit(solution)/shard_map/ppermute | solution.py:21
  11.3 15.6 %all-to-all-start = ((f32[16,16,128]{2,1,0:T(8,128)}), f32[16,16,128]{2,1,0:T(8,128)S(1)}, u32[]{:S(2)}, u32[]{:S(2)}) async-start(f32[16,16,128]{2,1,0:T(8,128)} %get-tuple-element.60), calls=%async_computation | async-start | bytes 262144 | tf_op jit(solution)/shard_map/all_to_all | solution.py:31
  17.1 0.7 copy-start
  19.7 20.8 %collective-permute-start.3 = (f32[8,10240]{1,0:T(8,128)S(1)}, f32[8,10240]{1,0:T(8,128)S(1)}, u32[]{:S(2)}, u32[]{:S(2)}) collective-permute-start(f32[8,10240]{1,0:T(8,128)S(1)} %get-tuple-element.76), channel_id=1, source_target_pairs={{0,496},{16,0},{32,16},{48,32},{64,48},{80,64},{96,80},{112,96},{1... | collective-permute-start | bytes 983048 | tf_op jit(solution)/shard_map/ppermute | solution.py:21
  28.7 11.8 %collective-permute-start.1 = (f32[8,9216]{1,0:T(8,128)}, f32[8,9216]{1,0:T(8,128)S(1)}, u32[]{:S(2)}, u32[]{:S(2)}) collective-permute-start(f32[8,9216]{1,0:T(8,128)} %get-tuple-element.74), channel_id=1, source_target_pairs={{0,16},{16,0},{32,48},{48,32},{64,80},{80,64},{96,112},{112,96},{1... | collective-permute-start | bytes 884744 | tf_op jit(solution)/shard_map/ppermute | solution.py:27
  34.7 11.9 %collective-permute-start.2 = (f32[8,9216]{1,0:T(8,128)}, f32[8,9216]{1,0:T(8,128)S(1)}, u32[]{:S(2)}, u32[]{:S(2)}) collective-permute-start(f32[8,9216]{1,0:T(8,128)} %get-tuple-element.75), channel_id=1, source_target_pairs={{0,496},{16,32},{32,16},{48,64},{64,48},{80,96},{96,80},{112,128},... | collective-permute-start | bytes 884744 | tf_op jit(solution)/shard_map/ppermute | solution.py:27
  36.6 12.0 %all-to-all-start.1 = ((f32[16,8,128]{2,1,0:T(8,128)}), f32[16,8,128]{2,1,0:T(8,128)S(1)}, u32[]{:S(2)}, u32[]{:S(2)}) async-start(f32[16,8,128]{2,1,0:T(8,128)} %get-tuple-element.70), calls=%async_computation.1 | async-start | bytes 131072 | tf_op jit(solution)/shard_map/all_to_all | solution.py:31
  50.1 11.8 %all-to-all-start.2 = ((f32[16,16,128]{2,1,0:T(8,128)}), f32[16,16,128]{2,1,0:T(8,128)S(1)}, u32[]{:S(2)}, u32[]{:S(2)}) async-start(f32[16,16,128]{2,1,0:T(8,128)} %get-tuple-element.82), calls=%async_computation.2 | async-start | bytes 262144 | tf_op jit(solution)/shard_map/all_to_all | solution.py:31
  54.4 18.9 %collective-permute-start.4 = (f32[8,8192]{1,0:T(8,128)S(1)}, f32[8,8192]{1,0:T(8,128)S(1)}, u32[]{:S(2)}, u32[]{:S(2)}) collective-permute-start(f32[8,8192]{1,0:T(8,128)S(1)} %get-tuple-element.81.dual), channel_id=1, source_target_pairs={{0,16},{16,32},{32,48},{48,64},{64,80},{80,96},{96,112},{112,128},... | collective-permute-start | bytes 786440 | tf_op jit(solution)/shard_map/ppermute | solution.py:21
  62.5 18.6 %all-to-all-start.3 = ((f32[32,2,2,128]{3,2,1,0:T(2,128)}), f32[32,2,2,128]{3,2,1,0:T(2,128)S(1)}, u32[]{:S(2)}, u32[]{:S(2)}) async-start(f32[32,2,2,128]{3,2,1,0:T(2,128)} %get-tuple-element.86), calls=%async_computation.3 | async-start | bytes 131072 | tf_op jit(solution)/shard_map/all_to_all | solution.py:31

commit v4 on v3

--- a/solution.py
+++ b/solution.py
@@ -29,6 +29,17 @@
 
 def spread(value, axis):
     return lax.all_to_all(value, axis, 0, 0, tiled=True)
+
+
+def spread_rows(value):
+    times, skus = lax.axis_size("tm"), lax.axis_size("sku")
+    half = skus // 2
+    groups = [
+        [t * skus + (side ^ (t // 2 % 4 < 2)) * half + rest for t in range(times)]
+        for side in range(2)
+        for rest in range(half)
+    ]
+    return lax.all_to_all(value, ("tm", "sku"), 0, 0, axis_index_groups=groups, tiled=True)
 
 
 def shape(*dims):
@@ -113,14 +124,51 @@
     return slice(index // each, index // each + 1), slice(start, start + BLOCK)
 
 
-def start_kernel(w, y, v, d, payload, sent):
-    width = y.shape[1]
-    each = w.shape[1]
-    payload[:, 0:ROWS, 0:each] = jnp.broadcast_to(w[...][None], (payload.shape[0], ROWS, each))
-    sent[:, 0:width] = y[...]
-    for i, at in blocks(width):
-        sent[extra_slot(i, width, 0)] = v[0:1, at]
-        sent[extra_slot(i, width, 1)] = d[0:1, at]
+def start(plant_dual, y, v, d, copies):
+    rows, width = y.shape
+    each = plant_dual.shape[1]
+    parts = 4
+
+    def kernel(w, y, v, d, payload, sent, mine, firsts, filled, sems):
+        piece = width // parts
+        fetches = [
+            pltpu.make_async_copy(w, mine, sems.at[0]),
+            pltpu.make_async_copy(v.at[0:1], firsts.at[0], sems.at[1]),
+            pltpu.make_async_copy(d.at[0:1], firsts.at[1], sems.at[2]),
+        ]
+        for k in range(parts):
+            at = pl.ds(k * piece, piece)
+            fetches.append(pltpu.make_async_copy(y.at[:, at], sent.at[:, at], sems.at[3 + k]))
+        for fetch in fetches:
+            fetch.start()
+        filled[...] = jnp.zeros(filled.shape, F32)
+        fetches[0].wait()
+        filled[:, 0:rows, 0:each] = jnp.broadcast_to(mine[...][None], (copies, rows, each))
+        out = pltpu.make_async_copy(filled, payload, sems.at[3 + parts])
+        out.start()
+        fetches[1].wait()
+        fetches[2].wait()
+        for i, at in blocks(width):
+            sent[extra_slot(i, width, 0)] = firsts[0, :, at]
+            sent[extra_slot(i, width, 1)] = firsts[1, :, at]
+        for fetch in fetches[3:]:
+            fetch.wait()
+        out.wait()
+
+    return pl.pallas_call(
+        kernel,
+        out_shape=(shape(copies, 2 * rows, P_SIZE), near(rows, width + 2 * (width // rows))),
+        in_specs=[pl.BlockSpec(memory_space=pltpu.HBM)] * 4,
+        out_specs=(pl.BlockSpec(memory_space=pltpu.HBM), VMEM),
+        scratch_shapes=[
+            pltpu.VMEM((rows, each), F32),
+            pltpu.VMEM((2, 1, width), F32),
+            pltpu.VMEM((copies, 2 * rows, P_SIZE), F32),
+            pltpu.SemaphoreType.DMA((4 + parts,)),
+        ],
+        name="start",
+        compiler_params=pltpu.CompilerParams(vmem_limit_bytes=16 * 2**20),
+    )(*(pltpu.with_memory_space_constraint(o, pltpu.HBM) for o in (plant_dual, y, v, d)))
 
 
 def stage(scalars, v, d, others):
@@ -318,14 +366,7 @@
     load = load_coef.reshape(1, width)
     plant_row = plants.reshape(1, width)
 
-    longer = width + 2 * (width // ROWS)
-    payload, y_sent = call(
-        start_kernel,
-        (shape(skus, 2 * ROWS, P_SIZE), shape(ROWS, longer)),
-        (plant_dual, balance_dual, stock_v, demand),
-        name="start",
-        grant=60,
-    )
+    payload, y_sent = start(plant_dual, balance_dual, stock_v, demand, skus)
     y_next = shifted(y_sent, "tm", -1)
     payload, codes, lags, v, d, *held = lax.optimization_barrier(
         (
@@ -387,7 +428,7 @@
         name="third",
     )
     portion = lax.dynamic_slice_in_dim(prices2, owner, each, 1)
-    totals = jnp.sum(spread(packed, "tm"), axis=(0, 3))
+    totals = jnp.sum(spread_rows(packed), axis=(0, 3))
     scale = P_SIZE / total_skus
     cells, cap_rows = ROWS * times * total_skus, ROWS * times * P_SIZE
     column = lax.broadcasted_iota(jnp.int32, totals.shape, 1)

time: 82.4 us -> 80.5 us (0.977)
  waiting for transfers between devices: 17.1 us -> 16 us
    all_to_all x4 -> x3, starting transfers between devices: 22.6 us -> 14 us  [spread(): return lax.all_to_all(value, axis, 0, 0, tiled=True)]
    all_to_all x0 -> x1, starting transfers between devices: none -> 8.23 us  [spread_rows(): lax.all_to_all(value, ('tm', 'sku'), 0, 0, axis_index_groups=groups, tile...]
    all_to_all x4 -> x3, waiting for transfers between devices: 11.1 us -> 4.01 us  [spread(): return lax.all_to_all(value, axis, 0, 0, tiled=True)]
    all_to_all x0 -> x1, waiting for transfers between devices: none -> 5.95 us  [spread_rows(): lax.all_to_all(value, ('tm', 'sku'), 0, 0, axis_index_groups=groups, tile...]
    pallas_call x6 -> x5, Pallas kernels: 7.61 us -> 5.7 us  [call(): pl.pallas_call(kernel, out_shape=out_shape, in_specs=[SMEM] * smem + [VME...]
    pallas_call x0 -> x1, Pallas kernels: none -> 1.42 us  [start(): pl.pallas_call(kernel, out_shape=(shape(copies, 2 * rows, P_SIZE), near(r...]
where the time goes in v4:
time: 80.5 us; the launch traced here: 79.8 us
  starting transfers between devices  50.6 us (63%)
  waiting for transfers between devices  16 us (20%)
  Pallas kernels  8.47 us (11%)
  local copies, waits for them, and re-layouts  2.72 us (3%)
  other arithmetic  1.28 us (2%)
    ppermute x3, starting transfers between devices, shifted(): lax.ppermute(value, axis, [(i, (i + steps) % count) for i in range(count)])  20.5 us
    all_to_all x3, starting transfers between devices, spread(): return lax.all_to_all(value, axis, 0, 0, tiled=True)  14 us
    all_to_all x1, starting transfers between devices, spread_rows(): lax.all_to_all(value, ('tm', 'sku'), 0, 0, axis_index_groups=groups, tile...  8.23 us
    ppermute x2, starting transfers between devices, swapped(): return lax.ppermute(value, axis, pairs)  7.82 us
    ppermute x2, waiting for transfers between devices, swapped(): return lax.ppermute(value, axis, pairs)  6.04 us
    all_to_all x1, waiting for transfers between devices, spread_rows(): lax.all_to_all(value, ('tm', 'sku'), 0, 0, axis_index_groups=groups, tile...  5.95 us
    pallas_call x5, Pallas kernels, call(): pl.pallas_call(kernel, out_shape=out_shape, in_specs=[SMEM] * smem + [VME...  5.7 us
    all_to_all x3, waiting for transfers between devices, spread(): return lax.all_to_all(value, axis, 0, 0, tiled=True)  4.01 us
  transfers between devices with their start and end apart: 9, of which 4 were waited for; matrix products, arithmetic and copies ran while one was open for 3% of the time, Pallas kernels for 7%

profile of v4, /device:TPU:1, one launch (start us, length us, event | category | flops | bytes accessed | tf_op | source)
XLA Modules:
  0.0 79.8 jit_solution(6110712948939832149)
XLA Ops:
  0.6 1.4 %start.1 = (f32[16,16,128]{2,1,0:T(8,128)}, f32[8,10240]{1,0:T(8,128)S(1)}) custom-call(f32[8,8]{1,0:T(8,128)} %w.1, f32[8,8192]{1,0:T(8,128)} %refs_5_, f32[8,8192]{1,0:T(8,128)} %refs_2_, f32[8,8192]{1,0:T(8,128)} %refs_3_), custom_call_target="tpu_custom_call" | custom-call | tf_op jit(solution)/shard_map/start/pallas_call | solution.py:158
  2.1 8.8 %collective-permute-start = (f32[8,10240]{1,0:T(8,128)S(1)}, f32[8,10240]{1,0:T(8,128)S(1)}, u32[]{:S(2)}, u32[]{:S(2)}) collective-permute-start(f32[8,10240]{1,0:T(8,128)S(1)} %get-tuple-element.63), channel_id=1, source_target_pairs={{0,496},{16,0},{32,16},{48,32},{64,48},{80,64},{96,80},{112,96},{1... | collective-permute-start | bytes 983048 | tf_op jit(solution)/shard_map/ppermute | solution.py:21
  10.9 5.8 %all-to-all-start = ((f32[16,16,128]{2,1,0:T(8,128)}), f32[16,16,128]{2,1,0:T(8,128)S(1)}, u32[]{:S(2)}, u32[]{:S(2)}) async-start(f32[16,16,128]{2,1,0:T(8,128)} %get-tuple-element.60), calls=%async_computation | async-start | bytes 262144 | tf_op jit(solution)/shard_map/all_to_all | solution.py:31
  16.7 0.0 copy-start
  16.7 0.6 copy-done
  17.3 0.6 pad_add_fusion.refs_0_
  17.9 1.4 %stage.1 = (s32[3]{0:T(128)S(4)}, s32[64]{0:T(128)S(4)}, f32[8,8192]{1,0:T(8,128)S(1)}, f32[8,8192]{1,0:T(8,128)S(1)}, f32[8,8192]{1,0:T(8,128)S(1)}, /*index=5*...) custom-call(s32[3]{0:T(128)} %pad_add_fusion.refs_0_, ...), custom_call_target="tpu_custom_call" | custom-call | tf_op jit(solution)/shard_map/stage/pallas_call | solution.py:193
  19.3 7.2 %collective-permute-start.3 = (f32[8,10240]{1,0:T(8,128)S(1)}, f32[8,10240]{1,0:T(8,128)S(1)}, u32[]{:S(2)}, u32[]{:S(2)}) collective-permute-start(f32[8,10240]{1,0:T(8,128)S(1)} %get-tuple-element.76), channel_id=1, source_target_pairs={{0,496},{16,0},{32,16},{48,32},{64,48},{80,64},{96,80},{112,96},{1... | collective-permute-start | bytes 983048 | tf_op jit(solution)/shard_map/ppermute | solution.py:21
  26.5 0.0 all-to-all-done.gathered
  26.5 0.0 collective-permute-done.y_next
  26.5 1.8 %first.1 = (f32[8,8192]{1,0:T(8,128)S(1)}, f32[8,9216]{1,0:T(8,128)}, f32[8,9216]{1,0:T(8,128)}, f32[16,8,128]{2,1,0:T(8,128)}, f32[8,128]{1,0:T(8,128)S(1)}) custom-call(s32[3]{0:T(128)S(4)} %get-tuple-element.58.codes.refs_0_, s32[64]{0:T(128)S(4)} %get-tuple-element.59.lags, f32[16,16,128]{2,1,0:T(8,128)S(1)} %all-to-all-done.gathered, ...), custom_call_target="tpu_custom_call" | custom-call | flops 51205360 | bytes 2560268 | tf_op jit(solution)/shard_map/first/pallas_call | solution.py:56
  28.3 5.9 %collective-permute-start.1 = (f32[8,9216]{1,0:T(8,128)}, f32[8,9216]{1,0:T(8,128)S(1)}, u32[]{:S(2)}, u32[]{:S(2)}) collective-permute-start(f32[8,9216]{1,0:T(8,128)} %get-tuple-element.74), channel_id=1, source_target_pairs={{0,16},{16,0},{32,48},{48,32},{64,80},{80,64},{96,112},{112,96},{1... | collective-permute-start | bytes 884744 | tf_op jit(solution)/shard_map/ppermute | solution.py:27
  34.2 1.9 %collective-permute-start.2 = (f32[8,9216]{1,0:T(8,128)}, f32[8,9216]{1,0:T(8,128)S(1)}, u32[]{:S(2)}, u32[]{:S(2)}) collective-permute-start(f32[8,9216]{1,0:T(8,128)} %get-tuple-element.75), channel_id=1, source_target_pairs={{0,496},{16,32},{32,16},{48,64},{64,48},{80,96},{96,80},{112,128},... | collective-permute-start | bytes 884744 | tf_op jit(solution)/shard_map/ppermute | solution.py:27
  36.1 3.9 %all-to-all-start.1 = ((f32[16,8,128]{2,1,0:T(8,128)}), f32[16,8,128]{2,1,0:T(8,128)S(1)}, u32[]{:S(2)}, u32[]{:S(2)}) async-start(f32[16,8,128]{2,1,0:T(8,128)} %get-tuple-element.70), calls=%async_computation.1 | async-start | bytes 131072 | tf_op jit(solution)/shard_map/all_to_all | solution.py:31
  40.1 0.0 collective-permute-done.3.v_next
  40.1 0.0 collective-permute-done.1.inner
  40.1 6.0 %collective-permute-done.2.outer = f32[8,9216]{1,0:T(8,128)S(1)} collective-permute-done((f32[8,9216]{1,0:T(8,128)}, f32[8,9216]{1,0:T(8,128)S(1)}, u32[]{:S(2)}, u32[]{:S(2)}) %collective-permute-start.2) | collective-permute-done | bytes 294944 | tf_op jit(solution)/shard_map/ppermute | solution.py:27
  46.1 0.9 %middle.1 = (f32[8,8192]{1,0:T(8,128)S(1)}, f32[8,8192]{1,0:T(8,128)S(1)}, f32[8,8320]{1,0:T(8,128)S(1)}) custom-call(s32[3]{0:T(128)S(4)} %get-tuple-element.58.codes.refs_0_, s32[64]{0:T(128)S(4)} %get-tuple-element.59.lags, f32[8,8192]{1,0:T(8,128)S(1)} %get-tuple-element.61.x, f32[8,8192]{1,0:T(8,128)S(1)} %get-tuple-element.73.x1.x, ...), custom_call_target="tpu_custom_call" | custom-call | flops 67589360 | bytes 3379468 | tf_op jit(solution)/shard_map/middle/pallas_call | solution.py:56
  47.0 1.1 %all-to-all-done.1.sums = f32[16,8,128]{2,1,0:T(8,128)S(1)} async-done(((f32[16,8,128]{2,1,0:T(8,128)}), f32[16,8,128]{2,1,0:T(8,128)S(1)}, u32[]{:S(2)}, u32[]{:S(2)}) %all-to-all-start.1) | async-done | bytes 65568 | tf_op jit(solution)/shard_map/all_to_all | solution.py:31
  48.1 1.6 %second.1 = (f32[8,8192]{1,0:T(8,128)S(1)}, f32[8,8192]{1,0:T(8,128)S(1)}, f32[16,16,128]{2,1,0:T(8,128)}, f32[8,128]{1,0:T(8,128)S(1)}, f32[1,128]{1,0:T(1,128)S(1)}) custom-call(s32[3]{0:T(128)S(4)} %get-tuple-element.58.codes.refs_0_, f32[16,8,128]{2,1,0:T(8,128)S(1)} %all-to-all-done.1.sums, f32[8,128]{1,0:T(8,128)S(1)} %get-tuple-element.71.prices, ...), custom_call_target="tpu_custom_call" | custom-call | flops 32450800 | bytes 1622540 | tf_op jit(solution)/shard_map/second/pallas_call | solution.py:56
  49.6 4.3 %all-to-all-start.2 = ((f32[16,16,128]{2,1,0:T(8,128)}), f32[16,16,128]{2,1,0:T(8,128)S(1)}, u32[]{:S(2)}, u32[]{:S(2)}) async-start(f32[16,16,128]{2,1,0:T(8,128)} %get-tuple-element.82), calls=%async_computation.2 | async-start | bytes 262144 | tf_op jit(solution)/shard_map/all_to_all | solution.py:31
  53.9 4.6 %collective-permute-start.4 = (f32[8,8192]{1,0:T(8,128)S(1)}, f32[8,8192]{1,0:T(8,128)S(1)}, u32[]{:S(2)}, u32[]{:S(2)}) collective-permute-start(f32[8,8192]{1,0:T(8,128)S(1)} %get-tuple-element.81.dual), channel_id=1, source_target_pairs={{0,16},{16,32},{32,48},{48,64},{64,80},{80,96},{96,112},{112,128},... | collective-permute-start | bytes 786440 | tf_op jit(solution)/shard_map/ppermute | solution.py:21
  58.5 2.9 %all-to-all-done.2.refs_1_ = f32[16,16,128]{2,1,0:T(8,128)S(1)} async-done(((f32[16,16,128]{2,1,0:T(8,128)}), f32[16,16,128]{2,1,0:T(8,128)S(1)}, u32[]{:S(2)}, u32[]{:S(2)}) %all-to-all-start.2) | async-done | bytes 131104 | tf_op jit(solution)/shard_map/all_to_all | solution.py:31
  61.4 0.7 third.1
  62.1 8.2 %all-to-all-start.3 = ((f32[32,2,2,128]{3,2,1,0:T(2,128)}), f32[32,2,2,128]{3,2,1,0:T(2,128)S(1)}, u32[]{:S(2)}, u32[]{:S(2)}) async-start(f32[32,2,2,128]{3,2,1,0:T(2,128)} %get-tuple-element.86), calls=%async_computation.3 | async-start | bytes 131072 | tf_op jit(solution)/shard_map/all_to_all | solution.py:42
  70.3 0.7 copy.17
  71.1 0.7 copy.18
  71.8 0.7 constant_dynamic-slice_fusion
  72.4 0.0 collective-permute-done.4.dual_prev
  72.4 0.8 unshift.1
  73.2 5.9 %all-to-all-done.3 = f32[32,2,2,128]{3,2,1,0:T(2,128)S(1)} async-done(((f32[32,2,2,128]{3,2,1,0:T(2,128)}), f32[32,2,2,128]{3,2,1,0:T(2,128)S(1)}, u32[]{:S(2)}, u32[]{:S(2)}) %all-to-all-start.3) | async-done | bytes 65568 | tf_op jit(solution)/shard_map/all_to_all | solution.py:42
  79.2 0.1 reduce_sum.9
  79.3 0.6 broadcast_multiply_fusion
  (1 shorter events, 0.0 us)
Async XLA Ops:
  2.1 24.4 %collective-permute-start = (f32[8,10240]{1,0:T(8,128)S(1)}, f32[8,10240]{1,0:T(8,128)S(1)}, u32[]{:S(2)}, u32[]{:S(2)}) collective-permute-start(f32[8,10240]{1,0:T(8,128)S(1)} %get-tuple-element.63), channel_id=1, source_target_pairs={{0,496},{16,0},{32,16},{48,32},{64,48},{80,64},{96,80},{112,96},{1... | collective-permute-start | bytes 983048 | tf_op jit(solution)/shard_map/ppermute | solution.py:21
  10.9 15.6 %all-to-all-start = ((f32[16,16,128]{2,1,0:T(8,128)}), f32[16,16,128]{2,1,0:T(8,128)S(1)}, u32[]{:S(2)}, u32[]{:S(2)}) async-start(f32[16,16,128]{2,1,0:T(8,128)} %get-tuple-element.60), calls=%async_computation | async-start | bytes 262144 | tf_op jit(solution)/shard_map/all_to_all | solution.py:31
  16.7 0.7 copy-start
  19.3 20.8 %collective-permute-start.3 = (f32[8,10240]{1,0:T(8,128)S(1)}, f32[8,10240]{1,0:T(8,128)S(1)}, u32[]{:S(2)}, u32[]{:S(2)}) collective-permute-start(f32[8,10240]{1,0:T(8,128)S(1)} %get-tuple-element.76), channel_id=1, source_target_pairs={{0,496},{16,0},{32,16},{48,32},{64,48},{80,64},{96,80},{112,96},{1... | collective-permute-start | bytes 983048 | tf_op jit(solution)/shard_map/ppermute | solution.py:21
  28.3 11.8 %collective-permute-start.1 = (f32[8,9216]{1,0:T(8,128)}, f32[8,9216]{1,0:T(8,128)S(1)}, u32[]{:S(2)}, u32[]{:S(2)}) collective-permute-start(f32[8,9216]{1,0:T(8,128)} %get-tuple-element.74), channel_id=1, source_target_pairs={{0,16},{16,0},{32,48},{48,32},{64,80},{80,64},{96,112},{112,96},{1... | collective-permute-start | bytes 884744 | tf_op jit(solution)/shard_map/ppermute | solution.py:27
  34.2 11.9 %collective-permute-start.2 = (f32[8,9216]{1,0:T(8,128)}, f32[8,9216]{1,0:T(8,128)S(1)}, u32[]{:S(2)}, u32[]{:S(2)}) collective-permute-start(f32[8,9216]{1,0:T(8,128)} %get-tuple-element.75), channel_id=1, source_target_pairs={{0,496},{16,32},{32,16},{48,64},{64,48},{80,96},{96,80},{112,128},... | collective-permute-start | bytes 884744 | tf_op jit(solution)/shard_map/ppermute | solution.py:27
  36.1 12.0 %all-to-all-start.1 = ((f32[16,8,128]{2,1,0:T(8,128)}), f32[16,8,128]{2,1,0:T(8,128)S(1)}, u32[]{:S(2)}, u32[]{:S(2)}) async-start(f32[16,8,128]{2,1,0:T(8,128)} %get-tuple-element.70), calls=%async_computation.1 | async-start | bytes 131072 | tf_op jit(solution)/shard_map/all_to_all | solution.py:31
  49.6 11.8 %all-to-all-start.2 = ((f32[16,16,128]{2,1,0:T(8,128)}), f32[16,16,128]{2,1,0:T(8,128)S(1)}, u32[]{:S(2)}, u32[]{:S(2)}) async-start(f32[16,16,128]{2,1,0:T(8,128)} %get-tuple-element.82), calls=%async_computation.2 | async-start | bytes 262144 | tf_op jit(solution)/shard_map/all_to_all | solution.py:31
  53.9 18.5 %collective-permute-start.4 = (f32[8,8192]{1,0:T(8,128)S(1)}, f32[8,8192]{1,0:T(8,128)S(1)}, u32[]{:S(2)}, u32[]{:S(2)}) collective-permute-start(f32[8,8192]{1,0:T(8,128)S(1)} %get-tuple-element.81.dual), channel_id=1, source_target_pairs={{0,16},{16,32},{32,48},{48,64},{64,80},{80,96},{96,112},{112,128},... | collective-permute-start | bytes 786440 | tf_op jit(solution)/shard_map/ppermute | solution.py:21
  62.1 17.1 %all-to-all-start.3 = ((f32[32,2,2,128]{3,2,1,0:T(2,128)}), f32[32,2,2,128]{3,2,1,0:T(2,128)S(1)}, u32[]{:S(2)}, u32[]{:S(2)}) async-start(f32[32,2,2,128]{3,2,1,0:T(2,128)} %get-tuple-element.86), calls=%async_computation.3 | async-start | bytes 131072 | tf_op jit(solution)/shard_map/all_to_all | solution.py:42

commit v5 on v4

--- a/solution.py
+++ b/solution.py
@@ -124,51 +124,55 @@
     return slice(index // each, index // each + 1), slice(start, start + BLOCK)
 
 
-def start(plant_dual, y, v, d, copies):
+def start(codes, plant_dual, y, v, d, holding, copies):
     rows, width = y.shape
     each = plant_dual.shape[1]
+    operands = (codes, plant_dual, y, v, d, holding)
     parts = 4
 
-    def kernel(w, y, v, d, payload, sent, mine, firsts, filled, sems):
+    def kernel(at_hbm, w, y, v, d, holding, payload, sent, codes, mine, firsts, filled, sems):
         piece = width // parts
         fetches = [
             pltpu.make_async_copy(w, mine, sems.at[0]),
             pltpu.make_async_copy(v.at[0:1], firsts.at[0], sems.at[1]),
             pltpu.make_async_copy(d.at[0:1], firsts.at[1], sems.at[2]),
+            pltpu.make_async_copy(holding, firsts.at[2], sems.at[3]),
+            pltpu.make_async_copy(at_hbm, codes, sems.at[5 + parts]),
         ]
         for k in range(parts):
             at = pl.ds(k * piece, piece)
-            fetches.append(pltpu.make_async_copy(y.at[:, at], sent.at[:, at], sems.at[3 + k]))
+            fetches.append(pltpu.make_async_copy(y.at[:, at], sent.at[:, at], sems.at[4 + k]))
         for fetch in fetches:
             fetch.start()
         filled[...] = jnp.zeros(filled.shape, F32)
         fetches[0].wait()
         filled[:, 0:rows, 0:each] = jnp.broadcast_to(mine[...][None], (copies, rows, each))
-        out = pltpu.make_async_copy(filled, payload, sems.at[3 + parts])
+        out = pltpu.make_async_copy(filled, payload, sems.at[4 + parts])
         out.start()
-        fetches[1].wait()
-        fetches[2].wait()
+        for fetch in fetches[1:]:
+            fetch.wait()
+        primal = step_size(codes, 0)
         for i, at in blocks(width):
-            sent[extra_slot(i, width, 0)] = firsts[0, :, at]
-            sent[extra_slot(i, width, 1)] = firsts[1, :, at]
-        for fetch in fetches[3:]:
-            fetch.wait()
+            v0, d0, cost = (firsts[k, :, at] for k in range(3))
+            stock = stock_step(v0, cost, sent[0:1, at], sent[1:2, at], primal)
+            sent[extra_slot(i, width, 0)] = v0 - 2.0 * stock - d0
         out.wait()
 
     return pl.pallas_call(
         kernel,
-        out_shape=(shape(copies, 2 * rows, P_SIZE), near(rows, width + 2 * (width // rows))),
-        in_specs=[pl.BlockSpec(memory_space=pltpu.HBM)] * 4,
+        out_shape=(shape(copies, rows, P_SIZE), near(rows, width + width // rows)),
+        in_specs=[pl.BlockSpec(memory_space=pltpu.HBM)] * 6,
         out_specs=(pl.BlockSpec(memory_space=pltpu.HBM), VMEM),
         scratch_shapes=[
+            pltpu.SMEM(codes.shape, jnp.int32),
             pltpu.VMEM((rows, each), F32),
-            pltpu.VMEM((2, 1, width), F32),
-            pltpu.VMEM((copies, 2 * rows, P_SIZE), F32),
-            pltpu.SemaphoreType.DMA((4 + parts,)),
+            pltpu.VMEM((3, 1, width), F32),
+            pltpu.VMEM((copies, rows, P_SIZE), F32),
+            pltpu.SemaphoreType.DMA((6 + parts,)),
         ],
         name="start",
         compiler_params=pltpu.CompilerParams(vmem_limit_bytes=16 * 2**20),
-    )(*(pltpu.with_memory_space_constraint(o, pltpu.HBM) for o in (plant_dual, y, v, d)))
+    )(*(pltpu.with_memory_space_constraint(o, pltpu.HBM) for o in operands))
 
 
 def stage(scalars, v, d, others):
@@ -176,12 +180,17 @@
     count, at_v = len(operands), len(scalars)
 
     def kernel(*refs):
-        outs, sent, sems = refs[count : 2 * count], refs[2 * count], refs[2 * count + 1]
-        copies = [pltpu.make_async_copy(refs[i], outs[i], sems.at[i]) for i in range(count)]
+        outs, (sent, steps, sems) = refs[count : 2 * count], refs[2 * count :]
+        copies = [
+            pltpu.make_async_copy(refs[i], outs[i] if i > 0 else steps, sems.at[i])
+            for i in range(count)
+        ]
         for copy in copies:
             copy.start()
         for copy in copies:
             copy.wait()
+        outs[0][0], outs[0][1] = steps[0], steps[1]
+        outs[0][2] = lax.axis_index("tm") % 2
         v, d = outs[at_v], outs[at_v + 1]
         width = v.shape[1]
         sent[:, 0:width] = v[...]
@@ -192,12 +201,15 @@
     width = v.shape[1]
     return pl.pallas_call(
         kernel,
-        out_shape=tuple(pltpu.SMEM(o.shape, o.dtype) for o in scalars)
+        out_shape=(pltpu.SMEM((3,), jnp.int32),)
+        + tuple(pltpu.SMEM(o.shape, o.dtype) for o in scalars[1:])
         + tuple(near(*o.shape, dtype=o.dtype) for o in operands[at_v:])
         + (near(ROWS, width + 2 * (width // ROWS)),),
         in_specs=[pl.BlockSpec(memory_space=pltpu.HBM)] * count,
         out_specs=(SMEM,) * at_v + (VMEM,) * (count - at_v + 1),
-        scratch_shapes=[pltpu.SemaphoreType.DMA((count,))],
+        scratch_shapes=[
+            pltpu.SMEM(scalars[0].shape, jnp.int32), pltpu.SemaphoreType.DMA((count,)),
+        ],
         name="stage",
         compiler_params=pltpu.CompilerParams(vmem_limit_bytes=16 * 2**20),
     )(*(pltpu.with_memory_space_constraint(o, pltpu.HBM) for o in operands))
@@ -227,11 +239,10 @@
         over = 2.0 * new - old
         x1[:, at] = new
         total += load_terms(over * load[:, at], plants[:, at], plant_ids)
-        v7, v8 = v[7:8, at], y_next[extra_slot(i, width, 0)]
-        d8 = y_next[extra_slot(i, width, 1)]
+        v7 = v[7:8, at]
         bar7 = 2.0 * stock_step(v7, holding[:, at], y[7:8, at], yb[0:1], primal) - v7
-        bar8 = 2.0 * stock_step(v8, holding[:, at], yb[0:1], yb[1:2], primal) - v8
-        first_row = over[0:1] + jnp.where(lag == LAGMAX, -d8 - bar8 + bar7, 0.0)
+        field8 = y_next[extra_slot(i, width, 0)] + bar7
+        first_row = over[0:1] + jnp.where(lag == LAGMAX, field8, 0.0)
         down = jnp.where(rows == 0, first_row, jnp.where(rows == 1, yb[0:1], d[:, at]))
         inner[:, at] = jnp.where(odd, down, over)
         outer[:, at] = jnp.where(odd, over, down)
@@ -278,7 +289,7 @@
         y8 = yb[0:1] + dual_step * (hb[0:1] + pltpu.roll(over, lag & (ROWS - 1), 0)[0:1])
         va2 = stock_step(va1, cost, ya1, row_after(ya1, y8, rows), primal)
         v2[:, at] = va2
-        start_bar = pltpu.roll(2.0 * va2 - va1, ROWS - lag + 1, 0)[0:1]
+        start_bar = pltpu.roll(2.0 * va2 - va1, (ROWS - lag + 1) & (ROWS - 1), 0)[0:1]
         whole = lag == LAGMAX
         y_end = jnp.where(whole, y16, pltpu.roll(yb, ROWS - lag, 0)[0:1])
         h_end = jnp.where(whole, 0.0, pltpu.roll(hb, ROWS - lag, 0)[0:1])
@@ -316,16 +327,21 @@
         dual_x[:, at] = dual[:, at] + dual_step * misfit
         square += misfit * misfit
         total += load_terms(over * load[:, at], plants[:, at], plant_ids)
-    count = loads.shape[0]
+    own = folded(total)
     pair = (field[:, x.shape[1] :], square)
-    lines = jnp.concatenate([jnp.sum(p, axis=0, keepdims=True) for p in pair] * 4, 0)
-    loads[:, 0:8, :] = jnp.broadcast_to(folded(total)[None], (count, ROWS, P_SIZE))
-    loads[:, 8:16, :] = jnp.broadcast_to(lines[None], (count, ROWS, P_SIZE))
+    lines = [own[k : k + 1] for k in range(ROWS)]
+    lines += [jnp.sum(p, axis=0, keepdims=True) for p in pair]
+    for k, line in enumerate(lines):
+        at = slice(k * P_SIZE, (k + 1) * P_SIZE)
+        loads[:, :, at] = jnp.broadcast_to(line[None], (loads.shape[0], 1, P_SIZE))
 
 
 def third_kernel(codes, sums, prices, cap, excess_row, price_out, out, *, total_skus):
     plant_step = step_size(codes, 1) * (P_SIZE / total_skus)
-    totals = jnp.sum(sums[...], axis=0)
+    row = jnp.sum(sums[...], axis=0)
+    totals = jnp.concatenate(
+        [row[:, k * P_SIZE : (k + 1) * P_SIZE] for k in range(ROWS + 2)], axis=0
+    )
     excess = totals[0:8] - cap[...]
     price_out[...] = jnp.maximum(prices[...] + plant_step * excess, 0.0)
     above = jnp.maximum(excess, 0.0)
@@ -366,7 +382,9 @@
     load = load_coef.reshape(1, width)
     plant_row = plants.reshape(1, width)
 
-    payload, y_sent = start(plant_dual, balance_dual, stock_v, demand, skus)
+    payload, y_sent = start(
+        step_codes, plant_dual, balance_dual, stock_v, demand, holding, skus
+    )
     y_next = shifted(y_sent, "tm", -1)
     payload, codes, lags, v, d, *held = lax.optimization_barrier(
         (
@@ -374,8 +392,6 @@
             load, plant_row, capacity,
         )
     )
-    parity = lax.axis_index("tm") % 2
-    codes = jnp.concatenate([codes, parity.astype(jnp.int32)[None]])
     codes, lags, v, d, x, y, cost, holding, load, plant_row, limits, v_sent = stage(
         (codes, lags), v, d, held
     )
@@ -404,7 +420,7 @@
     x2, dual_x2, loads2, prices1, above1 = call(
         second_kernel,
         (
-            near(ROWS, width), near(ROWS, width), shape(skus, 2 * ROWS, P_SIZE),
+            near(ROWS, width), near(ROWS, width), shape(skus, 1, (ROWS + 2) * P_SIZE),
             near(ROWS, P_SIZE), near(1, P_SIZE),
         ),
         (

time: 80.5 us -> 78.8 us (0.979)
    ppermute x2, starting transfers between devices: 7.82 us -> 9.23 us  [swapped(): return lax.ppermute(value, axis, pairs)]
    all_to_all x1, starting transfers between devices: 8.23 us -> 7.1 us  [spread_rows(): lax.all_to_all(value, ('tm', 'sku'), 0, 0, axis_index_groups=groups, tile...]
    unnamed x4 -> x2, local copies, waits for them, and re-layouts: 2.06 us -> 1.41 us
where the time goes in v5:
time: 78.8 us; the launch traced here: 78.2 us
  starting transfers between devices  50.8 us (64%)
  waiting for transfers between devices  15.4 us (20%)
  Pallas kernels  8.46 us (11%)
  local copies, waits for them, and re-layouts  2.07 us (3%)
    ppermute x3, starting transfers between devices, shifted(): lax.ppermute(value, axis, [(i, (i + steps) % count) for i in range(count)])  20.4 us
    all_to_all x3, starting transfers between devices, spread(): return lax.all_to_all(value, axis, 0, 0, tiled=True)  14.1 us
    ppermute x2, starting transfers between devices, swapped(): return lax.ppermute(value, axis, pairs)  9.23 us
    all_to_all x1, starting transfers between devices, spread_rows(): lax.all_to_all(value, ('tm', 'sku'), 0, 0, axis_index_groups=groups, tile...  7.1 us
    all_to_all x1, waiting for transfers between devices, spread_rows(): lax.all_to_all(value, ('tm', 'sku'), 0, 0, axis_index_groups=groups, tile...  6.06 us
    ppermute x2, waiting for transfers between devices, swapped(): return lax.ppermute(value, axis, pairs)  5.68 us
    pallas_call x5, Pallas kernels, call(): pl.pallas_call(kernel, out_shape=out_shape, in_specs=[SMEM] * smem + [VME...  5.68 us
    all_to_all x3, waiting for transfers between devices, spread(): return lax.all_to_all(value, axis, 0, 0, tiled=True)  3.66 us
  transfers between devices with their start and end apart: 9, of which 4 were waited for; matrix products, arithmetic and copies ran while one was open for 3% of the time, Pallas kernels for 7%

profile of v5, /device:TPU:1, one launch (start us, length us, event | category | flops | bytes accessed | tf_op | source)
XLA Modules:
  0.0 78.2 jit_solution(7432470441528812377)
XLA Ops:
  0.6 1.4 %start.1 = (f32[16,8,128]{2,1,0:T(8,128)}, f32[8,9216]{1,0:T(8,128)S(1)}) custom-call(s32[2]{0:T(128)} %refs_0_, f32[8,8]{1,0:T(8,128)} %w.1, f32[8,8192]{1,0:T(8,128)} %refs_5_, f32[8,8192]{1,0:T(8,128)} %refs_2_, f32[8,8192]{1,0:T(8,128)} %refs_3_, f32[1,8192]{1,0:T(1,128)} %bitcast.4), custom_call_target="tpu_custom_call" | custom-call | tf_op jit(solution)/shard_map/start/pallas_call | solution.py:161
  2.0 8.8 %collective-permute-start = (f32[8,9216]{1,0:T(8,128)S(1)}, f32[8,9216]{1,0:T(8,128)S(1)}, u32[]{:S(2)}, u32[]{:S(2)}) collective-permute-start(f32[8,9216]{1,0:T(8,128)S(1)} %get-tuple-element.63), channel_id=1, source_target_pairs={{0,496},{16,0},{32,16},{48,32},{64,48},{80,64},{96,80},{112,96},{1... | collective-permute-start | bytes 884744 | tf_op jit(solution)/shard_map/ppermute | solution.py:21
  10.8 5.8 %all-to-all-start = ((f32[16,8,128]{2,1,0:T(8,128)}), f32[16,8,128]{2,1,0:T(8,128)S(1)}, u32[]{:S(2)}, u32[]{:S(2)}) async-start(f32[16,8,128]{2,1,0:T(8,128)} %get-tuple-element.60), calls=%async_computation | async-start | bytes 131072 | tf_op jit(solution)/shard_map/all_to_all | solution.py:31
  16.6 1.4 %stage.1 = (s32[3]{0:T(128)S(4)}, s32[64]{0:T(128)S(4)}, f32[8,8192]{1,0:T(8,128)S(1)}, f32[8,8192]{1,0:T(8,128)S(1)}, f32[8,8192]{1,0:T(8,128)S(1)}, /*index=5*...) custom-call(s32[2]{0:T(128)} %refs_0_, s32[64]{0:T(128)} %refs_1_, ...), custom_call_target="tpu_custom_call" | custom-call | tf_op jit(solution)/shard_map/stage/pallas_call | solution.py:202
  18.0 7.2 %collective-permute-start.3 = (f32[8,10240]{1,0:T(8,128)S(1)}, f32[8,10240]{1,0:T(8,128)S(1)}, u32[]{:S(2)}, u32[]{:S(2)}) collective-permute-start(f32[8,10240]{1,0:T(8,128)S(1)} %get-tuple-element.76), channel_id=1, source_target_pairs={{0,496},{16,0},{32,16},{48,32},{64,48},{80,64},{96,80},{112,96},{1... | collective-permute-start | bytes 983048 | tf_op jit(solution)/shard_map/ppermute | solution.py:21
  25.2 0.0 all-to-all-done.gathered
  25.2 0.0 collective-permute-done.y_next
  25.2 1.7 %first.1 = (f32[8,8192]{1,0:T(8,128)S(1)}, f32[8,9216]{1,0:T(8,128)}, f32[8,9216]{1,0:T(8,128)}, f32[16,8,128]{2,1,0:T(8,128)}, f32[8,128]{1,0:T(8,128)S(1)}) custom-call(s32[3]{0:T(128)S(4)} %get-tuple-element.58.codes.refs_0_, s32[64]{0:T(128)S(4)} %get-tuple-element.59.lags, f32[16,8,128]{2,1,0:T(8,128)S(1)} %all-to-all-done.gathered, ...), custom_call_target="tpu_custom_call" | custom-call | flops 49239280 | bytes 2461964 | tf_op jit(solution)/shard_map/first/pallas_call | solution.py:56
  27.0 7.3 %collective-permute-start.1 = (f32[8,9216]{1,0:T(8,128)}, f32[8,9216]{1,0:T(8,128)S(1)}, u32[]{:S(2)}, u32[]{:S(2)}) collective-permute-start(f32[8,9216]{1,0:T(8,128)} %get-tuple-element.74), channel_id=1, source_target_pairs={{0,16},{16,0},{32,48},{48,32},{64,80},{80,64},{96,112},{112,96},{1... | collective-permute-start | bytes 884744 | tf_op jit(solution)/shard_map/ppermute | solution.py:27
  34.3 1.9 %collective-permute-start.2 = (f32[8,9216]{1,0:T(8,128)}, f32[8,9216]{1,0:T(8,128)S(1)}, u32[]{:S(2)}, u32[]{:S(2)}) collective-permute-start(f32[8,9216]{1,0:T(8,128)} %get-tuple-element.75), channel_id=1, source_target_pairs={{0,496},{16,32},{32,16},{48,64},{64,48},{80,96},{96,80},{112,128},... | collective-permute-start | bytes 884744 | tf_op jit(solution)/shard_map/ppermute | solution.py:27
  36.2 3.5 %all-to-all-start.1 = ((f32[16,8,128]{2,1,0:T(8,128)}), f32[16,8,128]{2,1,0:T(8,128)S(1)}, u32[]{:S(2)}, u32[]{:S(2)}) async-start(f32[16,8,128]{2,1,0:T(8,128)} %get-tuple-element.70), calls=%async_computation.1 | async-start | bytes 131072 | tf_op jit(solution)/shard_map/all_to_all | solution.py:31
  39.7 0.0 collective-permute-done.3.v_next
  39.7 0.0 collective-permute-done.1.inner
  39.7 5.7 %collective-permute-done.2.outer = f32[8,9216]{1,0:T(8,128)S(1)} collective-permute-done((f32[8,9216]{1,0:T(8,128)}, f32[8,9216]{1,0:T(8,128)S(1)}, u32[]{:S(2)}, u32[]{:S(2)}) %collective-permute-start.2) | collective-permute-done | bytes 294944 | tf_op jit(solution)/shard_map/ppermute | solution.py:27
  45.4 0.9 %middle.1 = (f32[8,8192]{1,0:T(8,128)S(1)}, f32[8,8192]{1,0:T(8,128)S(1)}, f32[8,8320]{1,0:T(8,128)S(1)}) custom-call(s32[3]{0:T(128)S(4)} %get-tuple-element.58.codes.refs_0_, s32[64]{0:T(128)S(4)} %get-tuple-element.59.lags, f32[8,8192]{1,0:T(8,128)S(1)} %get-tuple-element.61.x, f32[8,8192]{1,0:T(8,128)S(1)} %get-tuple-element.73.x1.x, ...), custom_call_target="tpu_custom_call" | custom-call | flops 66934000 | bytes 3346700 | tf_op jit(solution)/shard_map/middle/pallas_call | solution.py:56
  46.3 0.8 all-to-all-done.1.sums
  47.1 1.6 %second.1 = (f32[8,8192]{1,0:T(8,128)S(1)}, f32[8,8192]{1,0:T(8,128)S(1)}, f32[16,1,1280]{2,1,0:T(1,128)}, f32[8,128]{1,0:T(8,128)S(1)}, f32[1,128]{1,0:T(1,128)S(1)}) custom-call(s32[3]{0:T(128)S(4)} %get-tuple-element.58.codes.refs_0_, f32[16,8,128]{2,1,0:T(8,128)S(1)} %all-to-all-done.1.sums, f32[8,128]{1,0:T(8,128)S(1)} %get-tuple-element.71.prices, ...), custom_call_target="tpu_custom_call" | custom-call | flops 31467760 | bytes 1573388 | tf_op jit(solution)/shard_map/second/pallas_call | solution.py:56
  48.6 4.8 %all-to-all-start.2 = ((f32[16,1,1280]{2,1,0:T(1,128)}), f32[16,1,1280]{2,1,0:T(1,128)S(1)}, u32[]{:S(2)}, u32[]{:S(2)}) async-start(f32[16,1,1280]{2,1,0:T(1,128)} %get-tuple-element.82), calls=%async_computation.2 | async-start | bytes 163840 | tf_op jit(solution)/shard_map/all_to_all | solution.py:31
  53.4 4.5 %collective-permute-start.4 = (f32[8,8192]{1,0:T(8,128)S(1)}, f32[8,8192]{1,0:T(8,128)S(1)}, u32[]{:S(2)}, u32[]{:S(2)}) collective-permute-start(f32[8,8192]{1,0:T(8,128)S(1)} %get-tuple-element.81.dual), channel_id=1, source_target_pairs={{0,16},{16,32},{32,48},{48,64},{64,80},{80,96},{96,112},{112,128},... | collective-permute-start | bytes 786440 | tf_op jit(solution)/shard_map/ppermute | solution.py:21
  57.9 2.9 %all-to-all-done.2.refs_1_ = f32[16,1,1280]{2,1,0:T(1,128)S(1)} async-done(((f32[16,1,1280]{2,1,0:T(1,128)}), f32[16,1,1280]{2,1,0:T(1,128)S(1)}, u32[]{:S(2)}, u32[]{:S(2)}) %all-to-all-start.2) | async-done | bytes 81952 | tf_op jit(solution)/shard_map/all_to_all | solution.py:31
  60.8 0.7 third.1
  61.5 7.1 %all-to-all-start.3 = ((f32[32,2,2,128]{3,2,1,0:T(2,128)}), f32[32,2,2,128]{3,2,1,0:T(2,128)S(1)}, u32[]{:S(2)}, u32[]{:S(2)}) async-start(f32[32,2,2,128]{3,2,1,0:T(2,128)} %get-tuple-element.86), calls=%async_computation.3 | async-start | bytes 131072 | tf_op jit(solution)/shard_map/all_to_all | solution.py:42
  68.6 0.7 copy.17
  69.3 0.7 copy.18
  70.0 0.7 constant_dynamic-slice_fusion
  70.7 0.0 collective-permute-done.4.dual_prev
  70.7 0.8 %unshift.1 = f32[8,8192]{1,0:T(8,128)} custom-call(s32[64]{0:T(128)S(4)} %get-tuple-element.59.lags, f32[8,8192]{1,0:T(8,128)S(1)} %get-tuple-element.81.dual, f32[8,8192]{1,0:T(8,128)S(1)} %collective-permute-done.4.dual_prev), custom_call_target="tpu_custom_call" | custom-call | flops 15733760 | bytes 786688 | tf_op jit(solution)/shard_map/unshift/pallas_call | solution.py:56
  71.5 6.1 %all-to-all-done.3 = f32[32,2,2,128]{3,2,1,0:T(2,128)S(1)} async-done(((f32[32,2,2,128]{3,2,1,0:T(2,128)}), f32[32,2,2,128]{3,2,1,0:T(2,128)S(1)}, u32[]{:S(2)}, u32[]{:S(2)}) %all-to-all-start.3) | async-done | bytes 65568 | tf_op jit(solution)/shard_map/all_to_all | solution.py:42
  77.6 0.1 reduce_sum.9
  77.7 0.6 broadcast_multiply_fusion
  (1 shorter events, 0.0 us)
Async XLA Ops:
  2.0 23.2 %collective-permute-start = (f32[8,9216]{1,0:T(8,128)S(1)}, f32[8,9216]{1,0:T(8,128)S(1)}, u32[]{:S(2)}, u32[]{:S(2)}) collective-permute-start(f32[8,9216]{1,0:T(8,128)S(1)} %get-tuple-element.63), channel_id=1, source_target_pairs={{0,496},{16,0},{32,16},{48,32},{64,48},{80,64},{96,80},{112,96},{1... | collective-permute-start | bytes 884744 | tf_op jit(solution)/shard_map/ppermute | solution.py:21
  10.8 14.4 %all-to-all-start = ((f32[16,8,128]{2,1,0:T(8,128)}), f32[16,8,128]{2,1,0:T(8,128)S(1)}, u32[]{:S(2)}, u32[]{:S(2)}) async-start(f32[16,8,128]{2,1,0:T(8,128)} %get-tuple-element.60), calls=%async_computation | async-start | bytes 131072 | tf_op jit(solution)/shard_map/all_to_all | solution.py:31
  18.0 21.7 %collective-permute-start.3 = (f32[8,10240]{1,0:T(8,128)S(1)}, f32[8,10240]{1,0:T(8,128)S(1)}, u32[]{:S(2)}, u32[]{:S(2)}) collective-permute-start(f32[8,10240]{1,0:T(8,128)S(1)} %get-tuple-element.76), channel_id=1, source_target_pairs={{0,496},{16,0},{32,16},{48,32},{64,48},{80,64},{96,80},{112,96},{1... | collective-permute-start | bytes 983048 | tf_op jit(solution)/shard_map/ppermute | solution.py:21
  27.0 12.8 %collective-permute-start.1 = (f32[8,9216]{1,0:T(8,128)}, f32[8,9216]{1,0:T(8,128)S(1)}, u32[]{:S(2)}, u32[]{:S(2)}) collective-permute-start(f32[8,9216]{1,0:T(8,128)} %get-tuple-element.74), channel_id=1, source_target_pairs={{0,16},{16,0},{32,48},{48,32},{64,80},{80,64},{96,112},{112,96},{1... | collective-permute-start | bytes 884744 | tf_op jit(solution)/shard_map/ppermute | solution.py:27
  34.3 11.1 %collective-permute-start.2 = (f32[8,9216]{1,0:T(8,128)}, f32[8,9216]{1,0:T(8,128)S(1)}, u32[]{:S(2)}, u32[]{:S(2)}) collective-permute-start(f32[8,9216]{1,0:T(8,128)} %get-tuple-element.75), channel_id=1, source_target_pairs={{0,496},{16,32},{32,16},{48,64},{64,48},{80,96},{96,80},{112,128},... | collective-permute-start | bytes 884744 | tf_op jit(solution)/shard_map/ppermute | solution.py:27
  36.2 10.9 %all-to-all-start.1 = ((f32[16,8,128]{2,1,0:T(8,128)}), f32[16,8,128]{2,1,0:T(8,128)S(1)}, u32[]{:S(2)}, u32[]{:S(2)}) async-start(f32[16,8,128]{2,1,0:T(8,128)} %get-tuple-element.70), calls=%async_computation.1 | async-start | bytes 131072 | tf_op jit(solution)/shard_map/all_to_all | solution.py:31
  48.6 12.2 %all-to-all-start.2 = ((f32[16,1,1280]{2,1,0:T(1,128)}), f32[16,1,1280]{2,1,0:T(1,128)S(1)}, u32[]{:S(2)}, u32[]{:S(2)}) async-start(f32[16,1,1280]{2,1,0:T(1,128)} %get-tuple-element.82), calls=%async_computation.2 | async-start | bytes 163840 | tf_op jit(solution)/shard_map/all_to_all | solution.py:31
  53.4 17.3 %collective-permute-start.4 = (f32[8,8192]{1,0:T(8,128)S(1)}, f32[8,8192]{1,0:T(8,128)S(1)}, u32[]{:S(2)}, u32[]{:S(2)}) collective-permute-start(f32[8,8192]{1,0:T(8,128)S(1)} %get-tuple-element.81.dual), channel_id=1, source_target_pairs={{0,16},{16,32},{32,48},{48,64},{64,80},{80,96},{96,112},{112,128},... | collective-permute-start | bytes 786440 | tf_op jit(solution)/shard_map/ppermute | solution.py:21
  61.5 16.0 %all-to-all-start.3 = ((f32[32,2,2,128]{3,2,1,0:T(2,128)}), f32[32,2,2,128]{3,2,1,0:T(2,128)S(1)}, u32[]{:S(2)}, u32[]{:S(2)}) async-start(f32[32,2,2,128]{3,2,1,0:T(2,128)} %get-tuple-element.86), calls=%async_computation.3 | async-start | bytes 131072 | tf_op jit(solution)/shard_map/all_to_all | solution.py:42

commit v6 on v5

--- a/solution.py
+++ b/solution.py
@@ -244,10 +244,9 @@
         field8 = y_next[extra_slot(i, width, 0)] + bar7
         first_row = over[0:1] + jnp.where(lag == LAGMAX, field8, 0.0)
         down = jnp.where(rows == 0, first_row, jnp.where(rows == 1, yb[0:1], d[:, at]))
-        inner[:, at] = jnp.where(odd, down, over)
-        outer[:, at] = jnp.where(odd, over, down)
-        inner[extra_slot(i, width, 0)] = bar7
-        outer[extra_slot(i, width, 0)] = bar7
+        up = over + jnp.where(rows == ROWS - lag, bar7, 0.0)
+        inner[:, at] = jnp.where(odd, down, up)
+        outer[:, at] = jnp.where(odd, up, down)
     loads[...] = jnp.broadcast_to(folded(total)[None], loads.shape)
 
 
@@ -272,14 +271,12 @@
         d8, d9 = v_next[extra_slot(i, width, 0)], v_next[extra_slot(i, width, 1)]
         bar8, y16 = mixed[0:1], mixed[1:2]
         db = jnp.where(rows == 0, d8, jnp.where(rows == 1, d9, mixed))
-        slot = extra_slot(i, width, 0)
-        bar_before = jnp.where(odd, inner[slot], outer[slot])
         over = 2.0 * x1[:, at] - x[:, at]
         va1 = stock_step(va, cost, ya, row_after(ya, yb[0:1], rows), primal)
         vb1 = stock_step(vb, cost, yb, row_after(yb, y16, rows), primal)
         va_bar = 2.0 * va1 - va
         vb_bar = 2.0 * vb1 - vb
-        ha = -da - va_bar + row_before(va_bar, bar_before, rows)
+        ha = -da - va_bar + row_before(va_bar, jnp.zeros((1, BLOCK), F32), rows)
         hb = -db - vb_bar + row_before(vb_bar, va_bar[7:8], rows)
         misfit = ahead(ha, hb, lag, rows) + over
         square += misfit * misfit
@@ -400,8 +397,8 @@
     x1, inner, outer, loads1, prices0 = call(
         first_kernel,
         (
-            near(ROWS, width), near(ROWS, width + width // ROWS),
-            near(ROWS, width + width // ROWS), shape(skus, ROWS, P_SIZE), near(ROWS, P_SIZE),
+            near(ROWS, width), near(ROWS, width), near(ROWS, width),
+            shape(skus, ROWS, P_SIZE), near(ROWS, P_SIZE),
         ),
         (codes, lags, gathered, x, y, y_next, v, d, cost, holding, load, plant_row),
         smem=2,

time: 78.8 us -> 78.5 us (level)
  waiting for transfers between devices: 15.4 us -> 14.6 us
    ppermute x3, starting transfers between devices: 20.4 us -> 21.5 us  [shifted(): lax.ppermute(value, axis, [(i, (i + steps) % count) for i in range(count)])]
    ppermute x2, waiting for transfers between devices: 5.68 us -> 4.74 us  [swapped(): return lax.ppermute(value, axis, pairs)]
    ppermute x2, starting transfers between devices: 9.23 us -> 8.29 us  [swapped(): return lax.ppermute(value, axis, pairs)]
    all_to_all x3, starting transfers between devices: 14.1 us -> 13.2 us  [spread(): return lax.all_to_all(value, axis, 0, 0, tiled=True)]
  transfers between devices with their start and end apart: 9 -> 9, of which waited for: 4 -> 4; matrix products, arithmetic and copies ran while one was open for 3% -> 3% of each run, Pallas kernels for 7% -> 8%
where the time goes in v6:
time: 78.5 us; the launch traced here: 77.9 us
  starting transfers between devices  50.6 us (64%)
  waiting for transfers between devices  14.6 us (19%)
  Pallas kernels  9.21 us (12%)
  local copies, waits for them, and re-layouts  2.07 us (3%)
    ppermute x3, starting transfers between devices, shifted(): lax.ppermute(value, axis, [(i, (i + steps) % count) for i in range(count)])  21.5 us
    all_to_all x3, starting transfers between devices, spread(): return lax.all_to_all(value, axis, 0, 0, tiled=True)  13.2 us
    ppermute x2, starting transfers between devices, swapped(): return lax.ppermute(value, axis, pairs)  8.29 us
    all_to_all x1, starting transfers between devices, spread_rows(): lax.all_to_all(value, ('tm', 'sku'), 0, 0, axis_index_groups=groups, tile...  7.69 us
    all_to_all x1, waiting for transfers between devices, spread_rows(): lax.all_to_all(value, ('tm', 'sku'), 0, 0, axis_index_groups=groups, tile...  6.06 us
    pallas_call x5, Pallas kernels, call(): pl.pallas_call(kernel, out_shape=out_shape, in_specs=[SMEM] * smem + [VME...  5.7 us
    ppermute x2, waiting for transfers between devices, swapped(): return lax.ppermute(value, axis, pairs)  4.74 us
    all_to_all x3, waiting for transfers between devices, spread(): return lax.all_to_all(value, axis, 0, 0, tiled=True)  3.79 us
  transfers between devices with their start and end apart: 9, of which 4 were waited for; matrix products, arithmetic and copies ran while one was open for 3% of the time, Pallas kernels for 8%

profile of v6, /device:TPU:1, one launch (start us, length us, event | category | flops | bytes accessed | tf_op | source)
XLA Modules:
  0.0 77.9 jit_solution(9502043512616317897)
XLA Ops:
  0.6 1.4 %start.1 = (f32[16,8,128]{2,1,0:T(8,128)}, f32[8,9216]{1,0:T(8,128)S(1)}) custom-call(s32[2]{0:T(128)} %refs_0_, f32[8,8]{1,0:T(8,128)} %w.1, f32[8,8192]{1,0:T(8,128)} %refs_5_, f32[8,8192]{1,0:T(8,128)} %refs_2_, f32[8,8192]{1,0:T(8,128)} %refs_3_, f32[1,8192]{1,0:T(1,128)} %bitcast.4), custom_call_target="tpu_custom_call" | custom-call | tf_op jit(solution)/shard_map/start/pallas_call | solution.py:161
  2.0 8.8 %collective-permute-start = (f32[8,9216]{1,0:T(8,128)S(1)}, f32[8,9216]{1,0:T(8,128)S(1)}, u32[]{:S(2)}, u32[]{:S(2)}) collective-permute-start(f32[8,9216]{1,0:T(8,128)S(1)} %get-tuple-element.63), channel_id=1, source_target_pairs={{0,496},{16,0},{32,16},{48,32},{64,48},{80,64},{96,80},{112,96},{1... | collective-permute-start | bytes 884744 | tf_op jit(solution)/shard_map/ppermute | solution.py:21
  10.8 5.8 %all-to-all-start = ((f32[16,8,128]{2,1,0:T(8,128)}), f32[16,8,128]{2,1,0:T(8,128)S(1)}, u32[]{:S(2)}, u32[]{:S(2)}) async-start(f32[16,8,128]{2,1,0:T(8,128)} %get-tuple-element.60), calls=%async_computation | async-start | bytes 131072 | tf_op jit(solution)/shard_map/all_to_all | solution.py:31
  16.6 2.1 %stage.1 = (s32[3]{0:T(128)S(4)}, s32[64]{0:T(128)S(4)}, f32[8,8192]{1,0:T(8,128)S(1)}, f32[8,8192]{1,0:T(8,128)S(1)}, f32[8,8192]{1,0:T(8,128)S(1)}, /*index=5*...) custom-call(s32[2]{0:T(128)} %refs_0_, s32[64]{0:T(128)} %refs_1_, ...), custom_call_target="tpu_custom_call" | custom-call | tf_op jit(solution)/shard_map/stage/pallas_call | solution.py:202
  18.7 7.2 %collective-permute-start.3 = (f32[8,10240]{1,0:T(8,128)}, f32[8,10240]{1,0:T(8,128)S(1)}, u32[]{:S(2)}, u32[]{:S(2)}) collective-permute-start(f32[8,10240]{1,0:T(8,128)} %get-tuple-element.76), channel_id=1, source_target_pairs={{0,496},{16,0},{32,16},{48,32},{64,48},{80,64},{96,80},{112,96},{1... | collective-permute-start | bytes 983048 | tf_op jit(solution)/shard_map/ppermute | solution.py:21
  25.9 0.0 all-to-all-done.gathered
  25.9 0.0 collective-permute-done.y_next
  26.0 1.8 %first.1 = (f32[8,8192]{1,0:T(8,128)S(1)}, f32[8,8192]{1,0:T(8,128)S(1)}, f32[8,8192]{1,0:T(8,128)S(1)}, f32[16,8,128]{2,1,0:T(8,128)}, f32[8,128]{1,0:T(8,128)S(1)}) custom-call(s32[3]{0:T(128)S(4)} %get-tuple-element.58.codes.refs_0_, s32[64]{0:T(128)S(4)} %get-tuple-element.59.lags, f32[16,8,128]{2,1,0:T(8,128)S(1)} %all-to-all-done.gathered, ...), custom_call_target="tpu_custom_call" | custom-call | flops 47928560 | bytes 2396428 | tf_op jit(solution)/shard_map/first/pallas_call | solution.py:56
  27.7 6.4 %collective-permute-start.1 = (f32[8,8192]{1,0:T(8,128)S(1)}, f32[8,8192]{1,0:T(8,128)S(1)}, u32[]{:S(2)}, u32[]{:S(2)}) collective-permute-start(f32[8,8192]{1,0:T(8,128)S(1)} %get-tuple-element.74), channel_id=1, source_target_pairs={{0,16},{16,0},{32,48},{48,32},{64,80},{80,64},{96,112},{112,96},{1... | collective-permute-start | bytes 786440 | tf_op jit(solution)/shard_map/ppermute | solution.py:27
  34.1 1.9 %collective-permute-start.2 = (f32[8,8192]{1,0:T(8,128)S(1)}, f32[8,8192]{1,0:T(8,128)S(1)}, u32[]{:S(2)}, u32[]{:S(2)}) collective-permute-start(f32[8,8192]{1,0:T(8,128)S(1)} %get-tuple-element.75), channel_id=1, source_target_pairs={{0,496},{16,32},{32,16},{48,64},{64,48},{80,96},{96,80},{112,128},... | collective-permute-start | bytes 786440 | tf_op jit(solution)/shard_map/ppermute | solution.py:27
  36.0 3.5 %all-to-all-start.1 = ((f32[16,8,128]{2,1,0:T(8,128)}), f32[16,8,128]{2,1,0:T(8,128)S(1)}, u32[]{:S(2)}, u32[]{:S(2)}) async-start(f32[16,8,128]{2,1,0:T(8,128)} %get-tuple-element.70), calls=%async_computation.1 | async-start | bytes 131072 | tf_op jit(solution)/shard_map/all_to_all | solution.py:31
  39.5 0.0 collective-permute-done.3.v_next
  39.5 0.0 collective-permute-done.1.inner
  39.6 4.7 %collective-permute-done.2.outer = f32[8,8192]{1,0:T(8,128)S(1)} collective-permute-done((f32[8,8192]{1,0:T(8,128)S(1)}, f32[8,8192]{1,0:T(8,128)S(1)}, u32[]{:S(2)}, u32[]{:S(2)}) %collective-permute-start.2) | collective-permute-done | bytes 262176 | tf_op jit(solution)/shard_map/ppermute | solution.py:27
  44.3 0.9 %middle.1 = (f32[8,8192]{1,0:T(8,128)S(1)}, f32[8,8192]{1,0:T(8,128)S(1)}, f32[8,8320]{1,0:T(8,128)S(1)}) custom-call(s32[3]{0:T(128)S(4)} %get-tuple-element.58.codes.refs_0_, s32[64]{0:T(128)S(4)} %get-tuple-element.59.lags, f32[8,8192]{1,0:T(8,128)S(1)} %get-tuple-element.61.x, f32[8,8192]{1,0:T(8,128)S(1)} %get-tuple-element.73.x1.x, ...), custom_call_target="tpu_custom_call" | custom-call | flops 65623280 | bytes 3281164 | tf_op jit(solution)/shard_map/middle/pallas_call | solution.py:56
  45.2 1.8 %all-to-all-done.1.sums = f32[16,8,128]{2,1,0:T(8,128)S(1)} async-done(((f32[16,8,128]{2,1,0:T(8,128)}), f32[16,8,128]{2,1,0:T(8,128)S(1)}, u32[]{:S(2)}, u32[]{:S(2)}) %all-to-all-start.1) | async-done | bytes 65568 | tf_op jit(solution)/shard_map/all_to_all | solution.py:31
  47.0 1.6 %second.1 = (f32[8,8192]{1,0:T(8,128)S(1)}, f32[8,8192]{1,0:T(8,128)S(1)}, f32[16,1,1280]{2,1,0:T(1,128)}, f32[8,128]{1,0:T(8,128)S(1)}, f32[1,128]{1,0:T(1,128)S(1)}) custom-call(s32[3]{0:T(128)S(4)} %get-tuple-element.58.codes.refs_0_, f32[16,8,128]{2,1,0:T(8,128)S(1)} %all-to-all-done.1.sums, f32[8,128]{1,0:T(8,128)S(1)} %get-tuple-element.71.prices, ...), custom_call_target="tpu_custom_call" | custom-call | flops 31467760 | bytes 1573388 | tf_op jit(solution)/shard_map/second/pallas_call | solution.py:56
  48.5 3.9 %all-to-all-start.2 = ((f32[16,1,1280]{2,1,0:T(1,128)}), f32[16,1,1280]{2,1,0:T(1,128)S(1)}, u32[]{:S(2)}, u32[]{:S(2)}) async-start(f32[16,1,1280]{2,1,0:T(1,128)} %get-tuple-element.82), calls=%async_computation.2 | async-start | bytes 163840 | tf_op jit(solution)/shard_map/all_to_all | solution.py:31
  52.4 5.5 %collective-permute-start.4 = (f32[8,8192]{1,0:T(8,128)S(1)}, f32[8,8192]{1,0:T(8,128)S(1)}, u32[]{:S(2)}, u32[]{:S(2)}) collective-permute-start(f32[8,8192]{1,0:T(8,128)S(1)} %get-tuple-element.81.dual), channel_id=1, source_target_pairs={{0,16},{16,32},{32,48},{48,64},{64,80},{80,96},{96,112},{112,128},... | collective-permute-start | bytes 786440 | tf_op jit(solution)/shard_map/ppermute | solution.py:21
  57.9 2.0 %all-to-all-done.2.refs_1_ = f32[16,1,1280]{2,1,0:T(1,128)S(1)} async-done(((f32[16,1,1280]{2,1,0:T(1,128)}), f32[16,1,1280]{2,1,0:T(1,128)S(1)}, u32[]{:S(2)}, u32[]{:S(2)}) %all-to-all-start.2) | async-done | bytes 81952 | tf_op jit(solution)/shard_map/all_to_all | solution.py:31
  59.9 0.7 third.1
  60.6 7.7 %all-to-all-start.3 = ((f32[32,2,2,128]{3,2,1,0:T(2,128)}), f32[32,2,2,128]{3,2,1,0:T(2,128)S(1)}, u32[]{:S(2)}, u32[]{:S(2)}) async-start(f32[32,2,2,128]{3,2,1,0:T(2,128)} %get-tuple-element.86), calls=%async_computation.3 | async-start | bytes 131072 | tf_op jit(solution)/shard_map/all_to_all | solution.py:42
  68.3 0.7 copy.17
  69.0 0.7 copy.18
  69.7 0.7 constant_dynamic-slice_fusion
  70.4 0.0 collective-permute-done.4.dual_prev
  70.4 0.8 %unshift.1 = f32[8,8192]{1,0:T(8,128)} custom-call(s32[64]{0:T(128)S(4)} %get-tuple-element.59.lags, f32[8,8192]{1,0:T(8,128)S(1)} %get-tuple-element.81.dual, f32[8,8192]{1,0:T(8,128)S(1)} %collective-permute-done.4.dual_prev), custom_call_target="tpu_custom_call" | custom-call | flops 15733760 | bytes 786688 | tf_op jit(solution)/shard_map/unshift/pallas_call | solution.py:56
  71.2 6.1 %all-to-all-done.3 = f32[32,2,2,128]{3,2,1,0:T(2,128)S(1)} async-done(((f32[32,2,2,128]{3,2,1,0:T(2,128)}), f32[32,2,2,128]{3,2,1,0:T(2,128)S(1)}, u32[]{:S(2)}, u32[]{:S(2)}) %all-to-all-start.3) | async-done | bytes 65568 | tf_op jit(solution)/shard_map/all_to_all | solution.py:42
  77.2 0.1 reduce_sum.9
  77.4 0.6 broadcast_multiply_fusion
  (1 shorter events, 0.0 us)
Async XLA Ops:
  2.0 23.9 %collective-permute-start = (f32[8,9216]{1,0:T(8,128)S(1)}, f32[8,9216]{1,0:T(8,128)S(1)}, u32[]{:S(2)}, u32[]{:S(2)}) collective-permute-start(f32[8,9216]{1,0:T(8,128)S(1)} %get-tuple-element.63), channel_id=1, source_target_pairs={{0,496},{16,0},{32,16},{48,32},{64,48},{80,64},{96,80},{112,96},{1... | collective-permute-start | bytes 884744 | tf_op jit(solution)/shard_map/ppermute | solution.py:21
  10.8 15.1 %all-to-all-start = ((f32[16,8,128]{2,1,0:T(8,128)}), f32[16,8,128]{2,1,0:T(8,128)S(1)}, u32[]{:S(2)}, u32[]{:S(2)}) async-start(f32[16,8,128]{2,1,0:T(8,128)} %get-tuple-element.60), calls=%async_computation | async-start | bytes 131072 | tf_op jit(solution)/shard_map/all_to_all | solution.py:31
  18.7 20.8 %collective-permute-start.3 = (f32[8,10240]{1,0:T(8,128)}, f32[8,10240]{1,0:T(8,128)S(1)}, u32[]{:S(2)}, u32[]{:S(2)}) collective-permute-start(f32[8,10240]{1,0:T(8,128)} %get-tuple-element.76), channel_id=1, source_target_pairs={{0,496},{16,0},{32,16},{48,32},{64,48},{80,64},{96,80},{112,96},{1... | collective-permute-start | bytes 983048 | tf_op jit(solution)/shard_map/ppermute | solution.py:21
  27.7 11.8 %collective-permute-start.1 = (f32[8,8192]{1,0:T(8,128)S(1)}, f32[8,8192]{1,0:T(8,128)S(1)}, u32[]{:S(2)}, u32[]{:S(2)}) collective-permute-start(f32[8,8192]{1,0:T(8,128)S(1)} %get-tuple-element.74), channel_id=1, source_target_pairs={{0,16},{16,0},{32,48},{48,32},{64,80},{80,64},{96,112},{112,96},{1... | collective-permute-start | bytes 786440 | tf_op jit(solution)/shard_map/ppermute | solution.py:27
  34.1 10.2 %collective-permute-start.2 = (f32[8,8192]{1,0:T(8,128)S(1)}, f32[8,8192]{1,0:T(8,128)S(1)}, u32[]{:S(2)}, u32[]{:S(2)}) collective-permute-start(f32[8,8192]{1,0:T(8,128)S(1)} %get-tuple-element.75), channel_id=1, source_target_pairs={{0,496},{16,32},{32,16},{48,64},{64,48},{80,96},{96,80},{112,128},... | collective-permute-start | bytes 786440 | tf_op jit(solution)/shard_map/ppermute | solution.py:27
  36.0 11.0 %all-to-all-start.1 = ((f32[16,8,128]{2,1,0:T(8,128)}), f32[16,8,128]{2,1,0:T(8,128)S(1)}, u32[]{:S(2)}, u32[]{:S(2)}) async-start(f32[16,8,128]{2,1,0:T(8,128)} %get-tuple-element.70), calls=%async_computation.1 | async-start | bytes 131072 | tf_op jit(solution)/shard_map/all_to_all | solution.py:31
  48.5 11.3 %all-to-all-start.2 = ((f32[16,1,1280]{2,1,0:T(1,128)}), f32[16,1,1280]{2,1,0:T(1,128)S(1)}, u32[]{:S(2)}, u32[]{:S(2)}) async-start(f32[16,1,1280]{2,1,0:T(1,128)} %get-tuple-element.82), calls=%async_computation.2 | async-start | bytes 163840 | tf_op jit(solution)/shard_map/all_to_all | solution.py:31
  52.4 18.0 %collective-permute-start.4 = (f32[8,8192]{1,0:T(8,128)S(1)}, f32[8,8192]{1,0:T(8,128)S(1)}, u32[]{:S(2)}, u32[]{:S(2)}) collective-permute-start(f32[8,8192]{1,0:T(8,128)S(1)} %get-tuple-element.81.dual), channel_id=1, source_target_pairs={{0,16},{16,32},{32,48},{48,64},{64,80},{80,96},{96,112},{112,128},... | collective-permute-start | bytes 786440 | tf_op jit(solution)/shard_map/ppermute | solution.py:21
  60.6 16.6 %all-to-all-start.3 = ((f32[32,2,2,128]{3,2,1,0:T(2,128)}), f32[32,2,2,128]{3,2,1,0:T(2,128)S(1)}, u32[]{:S(2)}, u32[]{:S(2)}) async-start(f32[32,2,2,128]{3,2,1,0:T(2,128)} %get-tuple-element.86), calls=%async_computation.3 | async-start | bytes 131072 | tf_op jit(solution)/shard_map/all_to_all | solution.py:42

commit v7 on v6

--- a/solution.py
+++ b/solution.py
@@ -333,7 +333,7 @@
         loads[:, :, at] = jnp.broadcast_to(line[None], (loads.shape[0], 1, P_SIZE))
 
 
-def third_kernel(codes, sums, prices, cap, excess_row, price_out, out, *, total_skus):
+def third_kernel(codes, sums, prices, cap, excess_row, price_out, out, *, total_skus, total_rows):
     plant_step = step_size(codes, 1) * (P_SIZE / total_skus)
     row = jnp.sum(sums[...], axis=0)
     totals = jnp.concatenate(
@@ -344,7 +344,10 @@
     above = jnp.maximum(excess, 0.0)
     above_row = jnp.sum(above * above, axis=0, keepdims=True)
     for k, rows in enumerate(((totals[8:9], excess_row[...]), (totals[9:10], above_row))):
-        pair = jnp.concatenate(rows, 0)
+        cells, scale = total_rows * total_skus, P_SIZE / total_skus
+        pair = jnp.concatenate(
+            [rows[0] * (1.0 / cells), rows[1] * (scale * scale / (total_rows * P_SIZE))], 0
+        )
         out[:, k] = jnp.broadcast_to(pair[None], (out.shape[0],) + pair.shape)
 
 
@@ -431,7 +434,7 @@
     dual_prev = shifted(dual_x2, "tm", 1)
 
     def third(*refs):
-        third_kernel(*refs, total_skus=total_skus)
+        third_kernel(*refs, total_skus=total_skus, total_rows=ROWS * times)
 
     prices2, packed = call(
         third,
@@ -441,11 +444,7 @@
         name="third",
     )
     portion = lax.dynamic_slice_in_dim(prices2, owner, each, 1)
-    totals = jnp.sum(spread_rows(packed), axis=(0, 3))
-    scale = P_SIZE / total_skus
-    cells, cap_rows = ROWS * times * total_skus, ROWS * times * P_SIZE
-    column = lax.broadcasted_iota(jnp.int32, totals.shape, 1)
-    residuals = totals * jnp.where(column == 0, 1.0 / cells, scale * scale / cap_rows)
+    residuals = jnp.sum(spread_rows(packed), axis=(0, 3))
     next_y = call(
         unshift_kernel, shape(ROWS, width), (lags, dual_x2, dual_prev), smem=1, name="unshift"
     )

time: 78.5 us -> 78.5 us (level)
  no operation moved by 1% of the time
where the time goes in v7:
time: 78.5 us; the launch traced here: 77.9 us
  starting transfers between devices  50.6 us (64%)
  waiting for transfers between devices  14.6 us (19%)
  Pallas kernels  9.21 us (12%)
  local copies, waits for them, and re-layouts  2.07 us (3%)
    ppermute x3, starting transfers between devices, shifted(): lax.ppermute(value, axis, [(i, (i + steps) % count) for i in range(count)])  21.5 us
    all_to_all x3, starting transfers between devices, spread(): return lax.all_to_all(value, axis, 0, 0, tiled=True)  13.2 us
    ppermute x2, starting transfers between devices, swapped(): return lax.ppermute(value, axis, pairs)  8.29 us
    all_to_all x1, starting transfers between devices, spread_rows(): lax.all_to_all(value, ('tm', 'sku'), 0, 0, axis_index_groups=groups, tile...  7.69 us
    all_to_all x1, waiting for transfers between devices, spread_rows(): lax.all_to_all(value, ('tm', 'sku'), 0, 0, axis_index_groups=groups, tile...  6.07 us
    pallas_call x5, Pallas kernels, call(): pl.pallas_call(kernel, out_shape=out_shape, in_specs=[SMEM] * smem + [VME...  5.7 us
    ppermute x2, waiting for transfers between devices, swapped(): return lax.ppermute(value, axis, pairs)  4.74 us
    all_to_all x3, waiting for transfers between devices, spread(): return lax.all_to_all(value, axis, 0, 0, tiled=True)  3.79 us
  transfers between devices with their start and end apart: 9, of which 4 were waited for; matrix products, arithmetic and copies ran while one was open for 3% of the time, Pallas kernels for 8%

profile of v7, /device:TPU:1, one launch (start us, length us, event | category | flops | bytes accessed | tf_op | source)
XLA Modules:
  0.0 77.9 jit_solution(2483107728890491858)
XLA Ops:
  0.6 1.4 %start.1 = (f32[16,8,128]{2,1,0:T(8,128)}, f32[8,9216]{1,0:T(8,128)S(1)}) custom-call(s32[2]{0:T(128)} %refs_0_, f32[8,8]{1,0:T(8,128)} %w.1, f32[8,8192]{1,0:T(8,128)} %refs_5_, f32[8,8192]{1,0:T(8,128)} %refs_2_, f32[8,8192]{1,0:T(8,128)} %refs_3_, f32[1,8192]{1,0:T(1,128)} %bitcast.4), custom_call_target="tpu_custom_call" | custom-call | tf_op jit(solution)/shard_map/start/pallas_call | solution.py:161
  2.0 8.8 %collective-permute-start = (f32[8,9216]{1,0:T(8,128)S(1)}, f32[8,9216]{1,0:T(8,128)S(1)}, u32[]{:S(2)}, u32[]{:S(2)}) collective-permute-start(f32[8,9216]{1,0:T(8,128)S(1)} %get-tuple-element.63), channel_id=1, source_target_pairs={{0,496},{16,0},{32,16},{48,32},{64,48},{80,64},{96,80},{112,96},{1... | collective-permute-start | bytes 884744 | tf_op jit(solution)/shard_map/ppermute | solution.py:21
  10.8 5.8 %all-to-all-start = ((f32[16,8,128]{2,1,0:T(8,128)}), f32[16,8,128]{2,1,0:T(8,128)S(1)}, u32[]{:S(2)}, u32[]{:S(2)}) async-start(f32[16,8,128]{2,1,0:T(8,128)} %get-tuple-element.60), calls=%async_computation | async-start | bytes 131072 | tf_op jit(solution)/shard_map/all_to_all | solution.py:31
  16.6 2.1 %stage.1 = (s32[3]{0:T(128)S(4)}, s32[64]{0:T(128)S(4)}, f32[8,8192]{1,0:T(8,128)S(1)}, f32[8,8192]{1,0:T(8,128)S(1)}, f32[8,8192]{1,0:T(8,128)S(1)}, /*index=5*...) custom-call(s32[2]{0:T(128)} %refs_0_, s32[64]{0:T(128)} %refs_1_, ...), custom_call_target="tpu_custom_call" | custom-call | tf_op jit(solution)/shard_map/stage/pallas_call | solution.py:202
  18.7 7.2 %collective-permute-start.3 = (f32[8,10240]{1,0:T(8,128)}, f32[8,10240]{1,0:T(8,128)S(1)}, u32[]{:S(2)}, u32[]{:S(2)}) collective-permute-start(f32[8,10240]{1,0:T(8,128)} %get-tuple-element.76), channel_id=1, source_target_pairs={{0,496},{16,0},{32,16},{48,32},{64,48},{80,64},{96,80},{112,96},{1... | collective-permute-start | bytes 983048 | tf_op jit(solution)/shard_map/ppermute | solution.py:21
  25.9 0.0 all-to-all-done.gathered
  25.9 0.0 collective-permute-done.y_next
  26.0 1.8 %first.1 = (f32[8,8192]{1,0:T(8,128)S(1)}, f32[8,8192]{1,0:T(8,128)S(1)}, f32[8,8192]{1,0:T(8,128)S(1)}, f32[16,8,128]{2,1,0:T(8,128)}, f32[8,128]{1,0:T(8,128)S(1)}) custom-call(s32[3]{0:T(128)S(4)} %get-tuple-element.58.codes.refs_0_, s32[64]{0:T(128)S(4)} %get-tuple-element.59.lags, f32[16,8,128]{2,1,0:T(8,128)S(1)} %all-to-all-done.gathered, ...), custom_call_target="tpu_custom_call" | custom-call | flops 47928560 | bytes 2396428 | tf_op jit(solution)/shard_map/first/pallas_call | solution.py:56
  27.7 6.4 %collective-permute-start.1 = (f32[8,8192]{1,0:T(8,128)S(1)}, f32[8,8192]{1,0:T(8,128)S(1)}, u32[]{:S(2)}, u32[]{:S(2)}) collective-permute-start(f32[8,8192]{1,0:T(8,128)S(1)} %get-tuple-element.74), channel_id=1, source_target_pairs={{0,16},{16,0},{32,48},{48,32},{64,80},{80,64},{96,112},{112,96},{1... | collective-permute-start | bytes 786440 | tf_op jit(solution)/shard_map/ppermute | solution.py:27
  34.1 1.9 %collective-permute-start.2 = (f32[8,8192]{1,0:T(8,128)S(1)}, f32[8,8192]{1,0:T(8,128)S(1)}, u32[]{:S(2)}, u32[]{:S(2)}) collective-permute-start(f32[8,8192]{1,0:T(8,128)S(1)} %get-tuple-element.75), channel_id=1, source_target_pairs={{0,496},{16,32},{32,16},{48,64},{64,48},{80,96},{96,80},{112,128},... | collective-permute-start | bytes 786440 | tf_op jit(solution)/shard_map/ppermute | solution.py:27
  36.0 3.5 %all-to-all-start.1 = ((f32[16,8,128]{2,1,0:T(8,128)}), f32[16,8,128]{2,1,0:T(8,128)S(1)}, u32[]{:S(2)}, u32[]{:S(2)}) async-start(f32[16,8,128]{2,1,0:T(8,128)} %get-tuple-element.70), calls=%async_computation.1 | async-start | bytes 131072 | tf_op jit(solution)/shard_map/all_to_all | solution.py:31
  39.5 0.0 collective-permute-done.3.v_next
  39.5 0.0 collective-permute-done.1.inner
  39.6 4.7 %collective-permute-done.2.outer = f32[8,8192]{1,0:T(8,128)S(1)} collective-permute-done((f32[8,8192]{1,0:T(8,128)S(1)}, f32[8,8192]{1,0:T(8,128)S(1)}, u32[]{:S(2)}, u32[]{:S(2)}) %collective-permute-start.2) | collective-permute-done | bytes 262176 | tf_op jit(solution)/shard_map/ppermute | solution.py:27
  44.3 0.9 %middle.1 = (f32[8,8192]{1,0:T(8,128)S(1)}, f32[8,8192]{1,0:T(8,128)S(1)}, f32[8,8320]{1,0:T(8,128)S(1)}) custom-call(s32[3]{0:T(128)S(4)} %get-tuple-element.58.codes.refs_0_, s32[64]{0:T(128)S(4)} %get-tuple-element.59.lags, f32[8,8192]{1,0:T(8,128)S(1)} %get-tuple-element.61.x, f32[8,8192]{1,0:T(8,128)S(1)} %get-tuple-element.73.x1.x, ...), custom_call_target="tpu_custom_call" | custom-call | flops 65623280 | bytes 3281164 | tf_op jit(solution)/shard_map/middle/pallas_call | solution.py:56
  45.2 1.8 %all-to-all-done.1.sums = f32[16,8,128]{2,1,0:T(8,128)S(1)} async-done(((f32[16,8,128]{2,1,0:T(8,128)}), f32[16,8,128]{2,1,0:T(8,128)S(1)}, u32[]{:S(2)}, u32[]{:S(2)}) %all-to-all-start.1) | async-done | bytes 65568 | tf_op jit(solution)/shard_map/all_to_all | solution.py:31
  47.0 1.6 %second.1 = (f32[8,8192]{1,0:T(8,128)S(1)}, f32[8,8192]{1,0:T(8,128)S(1)}, f32[16,1,1280]{2,1,0:T(1,128)}, f32[8,128]{1,0:T(8,128)S(1)}, f32[1,128]{1,0:T(1,128)S(1)}) custom-call(s32[3]{0:T(128)S(4)} %get-tuple-element.58.codes.refs_0_, f32[16,8,128]{2,1,0:T(8,128)S(1)} %all-to-all-done.1.sums, f32[8,128]{1,0:T(8,128)S(1)} %get-tuple-element.71.prices, ...), custom_call_target="tpu_custom_call" | custom-call | flops 31467760 | bytes 1573388 | tf_op jit(solution)/shard_map/second/pallas_call | solution.py:56
  48.5 3.9 %all-to-all-start.2 = ((f32[16,1,1280]{2,1,0:T(1,128)}), f32[16,1,1280]{2,1,0:T(1,128)S(1)}, u32[]{:S(2)}, u32[]{:S(2)}) async-start(f32[16,1,1280]{2,1,0:T(1,128)} %get-tuple-element.82), calls=%async_computation.2 | async-start | bytes 163840 | tf_op jit(solution)/shard_map/all_to_all | solution.py:31
  52.4 5.5 %collective-permute-start.4 = (f32[8,8192]{1,0:T(8,128)S(1)}, f32[8,8192]{1,0:T(8,128)S(1)}, u32[]{:S(2)}, u32[]{:S(2)}) collective-permute-start(f32[8,8192]{1,0:T(8,128)S(1)} %get-tuple-element.81.dual), channel_id=1, source_target_pairs={{0,16},{16,32},{32,48},{48,64},{64,80},{80,96},{96,112},{112,128},... | collective-permute-start | bytes 786440 | tf_op jit(solution)/shard_map/ppermute | solution.py:21
  57.9 2.0 %all-to-all-done.2.refs_1_ = f32[16,1,1280]{2,1,0:T(1,128)S(1)} async-done(((f32[16,1,1280]{2,1,0:T(1,128)}), f32[16,1,1280]{2,1,0:T(1,128)S(1)}, u32[]{:S(2)}, u32[]{:S(2)}) %all-to-all-start.2) | async-done | bytes 81952 | tf_op jit(solution)/shard_map/all_to_all | solution.py:31
  59.9 0.7 third.1
  60.6 7.7 %all-to-all-start.3 = ((f32[32,2,2,128]{3,2,1,0:T(2,128)}), f32[32,2,2,128]{3,2,1,0:T(2,128)S(1)}, u32[]{:S(2)}, u32[]{:S(2)}) async-start(f32[32,2,2,128]{3,2,1,0:T(2,128)} %get-tuple-element.86), calls=%async_computation.3 | async-start | bytes 131072 | tf_op jit(solution)/shard_map/all_to_all | solution.py:42
  68.3 0.7 copy.17
  69.0 0.7 copy.18
  69.7 0.7 constant_dynamic-slice_fusion
  70.4 0.0 collective-permute-done.4.dual_prev
  70.4 0.8 %unshift.1 = f32[8,8192]{1,0:T(8,128)} custom-call(s32[64]{0:T(128)S(4)} %get-tuple-element.59.lags, f32[8,8192]{1,0:T(8,128)S(1)} %get-tuple-element.81.dual, f32[8,8192]{1,0:T(8,128)S(1)} %collective-permute-done.4.dual_prev), custom_call_target="tpu_custom_call" | custom-call | flops 15733760 | bytes 786688 | tf_op jit(solution)/shard_map/unshift/pallas_call | solution.py:56
  71.2 6.1 %all-to-all-done.3 = f32[32,2,2,128]{3,2,1,0:T(2,128)S(1)} async-done(((f32[32,2,2,128]{3,2,1,0:T(2,128)}), f32[32,2,2,128]{3,2,1,0:T(2,128)S(1)}, u32[]{:S(2)}, u32[]{:S(2)}) %all-to-all-start.3) | async-done | bytes 65568 | tf_op jit(solution)/shard_map/all_to_all | solution.py:42
  77.2 0.7 reduce_sum.9
Async XLA Ops:
  2.0 23.9 %collective-permute-start = (f32[8,9216]{1,0:T(8,128)S(1)}, f32[8,9216]{1,0:T(8,128)S(1)}, u32[]{:S(2)}, u32[]{:S(2)}) collective-permute-start(f32[8,9216]{1,0:T(8,128)S(1)} %get-tuple-element.63), channel_id=1, source_target_pairs={{0,496},{16,0},{32,16},{48,32},{64,48},{80,64},{96,80},{112,96},{1... | collective-permute-start | bytes 884744 | tf_op jit(solution)/shard_map/ppermute | solution.py:21
  10.8 15.1 %all-to-all-start = ((f32[16,8,128]{2,1,0:T(8,128)}), f32[16,8,128]{2,1,0:T(8,128)S(1)}, u32[]{:S(2)}, u32[]{:S(2)}) async-start(f32[16,8,128]{2,1,0:T(8,128)} %get-tuple-element.60), calls=%async_computation | async-start | bytes 131072 | tf_op jit(solution)/shard_map/all_to_all | solution.py:31
  18.7 20.8 %collective-permute-start.3 = (f32[8,10240]{1,0:T(8,128)}, f32[8,10240]{1,0:T(8,128)S(1)}, u32[]{:S(2)}, u32[]{:S(2)}) collective-permute-start(f32[8,10240]{1,0:T(8,128)} %get-tuple-element.76), channel_id=1, source_target_pairs={{0,496},{16,0},{32,16},{48,32},{64,48},{80,64},{96,80},{112,96},{1... | collective-permute-start | bytes 983048 | tf_op jit(solution)/shard_map/ppermute | solution.py:21
  27.7 11.8 %collective-permute-start.1 = (f32[8,8192]{1,0:T(8,128)S(1)}, f32[8,8192]{1,0:T(8,128)S(1)}, u32[]{:S(2)}, u32[]{:S(2)}) collective-permute-start(f32[8,8192]{1,0:T(8,128)S(1)} %get-tuple-element.74), channel_id=1, source_target_pairs={{0,16},{16,0},{32,48},{48,32},{64,80},{80,64},{96,112},{112,96},{1... | collective-permute-start | bytes 786440 | tf_op jit(solution)/shard_map/ppermute | solution.py:27
  34.1 10.2 %collective-permute-start.2 = (f32[8,8192]{1,0:T(8,128)S(1)}, f32[8,8192]{1,0:T(8,128)S(1)}, u32[]{:S(2)}, u32[]{:S(2)}) collective-permute-start(f32[8,8192]{1,0:T(8,128)S(1)} %get-tuple-element.75), channel_id=1, source_target_pairs={{0,496},{16,32},{32,16},{48,64},{64,48},{80,96},{96,80},{112,128},... | collective-permute-start | bytes 786440 | tf_op jit(solution)/shard_map/ppermute | solution.py:27
  36.0 11.0 %all-to-all-start.1 = ((f32[16,8,128]{2,1,0:T(8,128)}), f32[16,8,128]{2,1,0:T(8,128)S(1)}, u32[]{:S(2)}, u32[]{:S(2)}) async-start(f32[16,8,128]{2,1,0:T(8,128)} %get-tuple-element.70), calls=%async_computation.1 | async-start | bytes 131072 | tf_op jit(solution)/shard_map/all_to_all | solution.py:31
  48.5 11.3 %all-to-all-start.2 = ((f32[16,1,1280]{2,1,0:T(1,128)}), f32[16,1,1280]{2,1,0:T(1,128)S(1)}, u32[]{:S(2)}, u32[]{:S(2)}) async-start(f32[16,1,1280]{2,1,0:T(1,128)} %get-tuple-element.82), calls=%async_computation.2 | async-start | bytes 163840 | tf_op jit(solution)/shard_map/all_to_all | solution.py:31
  52.4 18.0 %collective-permute-start.4 = (f32[8,8192]{1,0:T(8,128)S(1)}, f32[8,8192]{1,0:T(8,128)S(1)}, u32[]{:S(2)}, u32[]{:S(2)}) collective-permute-start(f32[8,8192]{1,0:T(8,128)S(1)} %get-tuple-element.81.dual), channel_id=1, source_target_pairs={{0,16},{16,32},{32,48},{48,64},{64,80},{80,96},{96,112},{112,128},... | collective-permute-start | bytes 786440 | tf_op jit(solution)/shard_map/ppermute | solution.py:21
  60.6 16.6 %all-to-all-start.3 = ((f32[32,2,2,128]{3,2,1,0:T(2,128)}), f32[32,2,2,128]{3,2,1,0:T(2,128)S(1)}, u32[]{:S(2)}, u32[]{:S(2)}) async-start(f32[32,2,2,128]{3,2,1,0:T(2,128)} %get-tuple-element.86), calls=%async_computation.3 | async-start | bytes 131072 | tf_op jit(solution)/shard_map/all_to_all | solution.py:42
